TPU v7x, 256 devices: a whole 4x4x8 slice. The times are simulated.
256 devices in a mesh: row: 16 (over x, z_hi), col: 16 (over y, z_lo, core).
Axes of the slice: x: 4, y: 4, z: 8 (z_hi: 4, z_lo: 2; z = z_hi * 2 + z_lo), core: 2. Of those that a mesh axis runs over, the one named last changes fastest.
Arguments:
- positions: float32 [3, 65536], P(None, ('row', 'col')), may hold values from -6 to 6
- features: bfloat16 [128, 65536], P(None, ('row', 'col')), may hold values from -6 to 6
- fill: int32 [512], P(('row', 'col')), may hold values from 64 to 128, as said below
- tiles: int32 [2048, 2], P(('row', 'col')), may hold values from 0 to 31, as said below
- tile_count: int32 [256], P(('row', 'col')), may hold values from 2 to 8, as said below
- w_radial: float32 [64, 32], replicated, may hold values from -1 to 1
- w_left: bfloat16 [128, 64], replicated, may hold values from -0.5 to 0.5
- w_right: bfloat16 [128, 64], replicated, may hold values from -0.5 to 0.5
- w_hidden: bfloat16 [64, 64], replicated, may hold values from -0.75 to 0.75
- w_out: bfloat16 [64], replicated, may hold values from -0.25 to 0.25
Outputs:
- forces: float32 [3, 65536], P(None, ('row', 'col'))
- bead_energy: float32 [65536], P(('row', 'col'))
Inputs may be any that keep to these rules, and one draw needn't show every extreme that they name: `fill`: at least 64; some cluster holds 128. `tiles`: A device's 8 slots name distinct cluster pairs; the first entry is below 32, the second below 32; some device has the pair of the last clusters of both groups. `tile_count`: at least 2; some device has all 8 slots live.
All inputs are finite; a program needn't handle non-finite values.
Results may differ from a plain program's by a relative error of at most 0.0045.
Values may be sent and summed in bfloat16 or wider, within the bound.
No kernel may reach another device: no remote copies, remote signals or barrier semaphores. Data moves between devices by JAX's collectives and lax.ppermute only.
A program may use at most 64 MiB of HBM per device.

v0:
```python
import jax
import jax.numpy as jnp
from jax import lax
from jax.sharding import PartitionSpec as P

CL = 128
CPD = 2


SOFT = 0.01
RANGE = 6.0


def dsilu(value):
    sig = jax.nn.sigmoid(value)
    return sig * (1.0 + value * (1.0 - sig))


def tile_terms(left, right, proj_a, proj_b, same, live_tile, w_radial, w_hidden, w_out):
    slots = left.shape[1]
    hidden = w_radial.shape[0]
    nbasis = w_radial.shape[1]
    delta = left[:3, :, None] - right[:3, None, :]
    dist = jnp.sqrt(jnp.sum(delta * delta, 0) + SOFT)
    ident = (jnp.arange(slots)[:, None] == jnp.arange(slots)[None, :]).astype(jnp.float32)
    mask = left[3][:, None] * right[3][None, :] * (1.0 - same * ident) * live_tile
    flat = dist.reshape(-1)
    centers = RANGE * jnp.arange(nbasis, dtype=jnp.float32) / (nbasis - 1)
    sharp = ((nbasis - 1) / RANGE) ** 2
    offset = flat[None, :] - centers[:, None]
    basis = jnp.exp(-sharp * offset * offset)
    pair_in = (
        proj_a.astype(jnp.float32)[:, :, None] + proj_b.astype(jnp.float32)[:, None, :]
    ).reshape(hidden, -1)
    pre1 = jnp.dot(w_radial, basis, precision=lax.Precision.HIGHEST) + pair_in
    act1 = jax.nn.silu(pre1).astype(jnp.bfloat16)
    pre2 = jnp.dot(w_hidden, act1, preferred_element_type=jnp.float32)
    act2 = jax.nn.silu(pre2).astype(jnp.bfloat16)
    energy = jnp.dot(w_out[None, :], act2, preferred_element_type=jnp.float32)[0]
    back2 = (w_out.astype(jnp.float32)[:, None] * dsilu(pre2)).astype(jnp.bfloat16)
    back1 = lax.dot_general(
        w_hidden, back2, (((0,), (0,)), ((), ())), preferred_element_type=jnp.float32
    ) * dsilu(pre1)
    radial = lax.dot_general(
        w_radial, back1, (((0,), (0,)), ((), ())), precision=lax.Precision.HIGHEST
    )
    slope = jnp.sum(radial * basis * (-2.0 * sharp * offset), 0)
    weight = mask * slope.reshape(slots, slots) / dist
    energy_left = jnp.sum(mask * energy.reshape(slots, slots), 1)
    pos_left = left[:3]
    pos_right = right[:3]
    force_left = (
        jnp.dot(pos_right, weight.T, precision=lax.Precision.HIGHEST)
        - pos_left * jnp.sum(weight, 1)[None, :]
    )
    force_right = (
        jnp.dot(pos_left, weight, precision=lax.Precision.HIGHEST)
        - pos_right * jnp.sum(weight, 0)[None, :]
    )
    return (force_left, energy_left, force_right)


def project(weight, descriptors):
    return lax.dot_general(
        weight, descriptors, (((0,), (0,)), ((), ())), preferred_element_type=jnp.float32
    ).astype(jnp.bfloat16)


def body(positions, features, fill, tiles, tile_count, w_radial, w_left, w_right, w_hidden, w_out):
    beads = positions.shape[1]
    live = (
        (jnp.arange(CL, dtype=jnp.int32)[None, :] < fill[:, None])
        .astype(jnp.float32)
        .reshape(beads)
    )
    coords = jnp.concatenate([positions, live[None, :]], 0)
    row_coords = lax.all_gather(coords, "col", axis=1, tiled=True)
    col_coords = lax.all_gather(coords, "row", axis=1, tiled=True)
    row_desc = lax.all_gather(features, "col", axis=1, tiled=True)
    col_desc = lax.all_gather(features, "row", axis=1, tiled=True)
    row_proj = project(w_left, row_desc)
    col_proj = project(w_right, col_desc)
    row_index = lax.axis_index("row")
    col_index = lax.axis_index("col")
    col_count = lax.axis_size("col")
    row_base = row_index * col_count * CPD
    live_count = tile_count[0]

    def step(slot, carry):
        firsts, seconds = carry
        first = tiles[slot, 0]
        other = tiles[slot, 1]
        global_a = row_base + first
        global_b = (other // CPD * col_count + col_index) * CPD + other % CPD
        same = (global_a == global_b).astype(jnp.float32)
        live_tile = (slot < live_count).astype(jnp.float32)
        start_a = first * CL
        start_b = other * CL
        left = lax.dynamic_slice_in_dim(row_coords, start_a, CL, 1)
        right = lax.dynamic_slice_in_dim(col_coords, start_b, CL, 1)
        part_a = lax.dynamic_slice_in_dim(row_proj, start_a, CL, 1)
        part_b = lax.dynamic_slice_in_dim(col_proj, start_b, CL, 1)
        force_a, energy_a, force_b = tile_terms(
            left, right, part_a, part_b, same, live_tile, w_radial, w_hidden, w_out
        )
        added = jnp.concatenate([force_a, energy_a[None, :]], 0)
        firsts = lax.dynamic_update_slice_in_dim(
            firsts, lax.dynamic_slice_in_dim(firsts, start_a, CL, 1) + added, start_a, 1
        )
        seconds = lax.dynamic_update_slice_in_dim(
            seconds, lax.dynamic_slice_in_dim(seconds, start_b, CL, 1) + force_b, start_b, 1
        )
        return (firsts, seconds)

    start = (
        jnp.zeros((4, row_coords.shape[1]), jnp.float32),
        jnp.zeros((3, col_coords.shape[1]), jnp.float32),
    )
    firsts, seconds = lax.fori_loop(0, tiles.shape[0], step, start)
    row_part = lax.psum_scatter(firsts, "col", scatter_dimension=1, tiled=True)
    col_part = lax.psum_scatter(seconds, "row", scatter_dimension=1, tiled=True)
    return (row_part[:3] + col_part, row_part[3])


def solution(mesh):
    return jax.shard_map(
        body,
        mesh=mesh,
        in_specs=(
            P(None, ("row", "col")),
            P(None, ("row", "col")),
            P(("row", "col")),
            P(("row", "col"), None),
            P(("row", "col")),
            P(),
            P(),
            P(),
            P(),
            P(),
        ),
        out_specs=(P(None, ("row", "col")), P(("row", "col"))),
        check_vma=False,
    )
```

profile of v0, /device:TPU:1, one launch (start us, length us, event | category | flops | bytes accessed | tf_op | source)
XLA Modules:
  0.0 457.2 jit_solution(3099563848737792870)
XLA Ops:
  10.1 40.6 %all_gather.12 = f32[4,4096]{1,0:T(4,128)S(1)} all-gather(f32[4,256]{1,0:T(4,128)S(1)} %pad_maximum_fusion), channel_id=1, replica_groups=mesh['row'=16,'col'=16] {'row'}, dimensions={1}, use_global_device_ids=true | all-gather | bytes 69632 | tf_op jit(solution)/shard_map/all_gather | solution.py:78
  50.8 27.9 %all_gather.13 = f32[4,4096]{1,0:T(4,128)S(1)} all-gather(f32[4,256]{1,0:T(4,128)S(1)} %pad_maximum_fusion), channel_id=1, replica_groups=mesh['row'=16,'col'=16] {'col'}, dimensions={1}, use_global_device_ids=true | all-gather | bytes 69632 | tf_op jit(solution)/shard_map/all_gather | solution.py:77
  80.2 25.2 %all-gather.3.cloned.1.call-done = bf16[128,4096]{1,0:T(8,128)(2,1)} async-done(((bf16[128,256]{1,0:T(8,128)(2,1)}), bf16[128,4096]{1,0:T(8,128)(2,1)}) %all-gather.3.cloned.1.call-update) | async-done | bytes 1048592 | tf_op jit(solution)/shard_map/all_gather | solution.py:79
  107.0 186.5 %while.17 = (s32[]{:T(128)}, f32[4,4096]{1,0:T(4,128)S(1)}, f32[3,4096]{1,0:T(4,128)S(1)}, s32[8,2]{0,1:T(2,128)}, f32[4,4096]{1,0:T(4,128)S(1)}, /*index=5*/f32...) while((s32[]{:T(128)}, f32[4,4096]{1,0:T(4,128)S(1)}, ...), condition=%wide.region_6.7_spmd, body=%wide.region_0.6_spmd.sunk | while | flops 1113033216 | bytes 43096360 | solution.py:119
  111.0 5.9 %fusion.85 = f32[64,16384]{1,0:T(8,128)S(1)} fusion(f32[64,32]{0,1:T(8,128)S(1)} %copy-done.1, f32[8,8,128,128]{3,2,1,0:T(8,128)S(1)} %bitcast.136, f32[32]{0:T(128)S(1)} %iota_multiply_fusion.2, f32[16384]{0:T(1024)S(1)} %sqrt_bitcast_fusion.2), kind=kOutput, calls=%fused_computation.3.clone.1 | convolution fusion | flops 405274624 | bytes 8462464 | tf_op jit(solution)/shard_map/while/body/eval_jaxpr/dot_general | solution.py:35
  118.6 3.4 fusion.87
  122.0 2.9 fusion.88
  134.3 5.9 %fusion.85 = f32[64,16384]{1,0:T(8,128)S(1)} fusion(f32[64,32]{0,1:T(8,128)S(1)} %copy-done.1, f32[8,8,128,128]{3,2,1,0:T(8,128)S(1)} %bitcast.136, f32[32]{0:T(128)S(1)} %iota_multiply_fusion.2, f32[16384]{0:T(1024)S(1)} %sqrt_bitcast_fusion.2), kind=kOutput, calls=%fused_computation.3.clone.1 | convolution fusion | flops 405274624 | bytes 8462464 | tf_op jit(solution)/shard_map/while/body/eval_jaxpr/dot_general | solution.py:35
  141.9 3.4 fusion.87
  145.3 2.9 fusion.88
  157.7 5.9 %fusion.85 = f32[64,16384]{1,0:T(8,128)S(1)} fusion(f32[64,32]{0,1:T(8,128)S(1)} %copy-done.1, f32[8,8,128,128]{3,2,1,0:T(8,128)S(1)} %bitcast.136, f32[32]{0:T(128)S(1)} %iota_multiply_fusion.2, f32[16384]{0:T(1024)S(1)} %sqrt_bitcast_fusion.2), kind=kOutput, calls=%fused_computation.3.clone.1 | convolution fusion | flops 405274624 | bytes 8462464 | tf_op jit(solution)/shard_map/while/body/eval_jaxpr/dot_general | solution.py:35
  165.2 3.4 fusion.87
  168.7 2.9 fusion.88
  181.0 5.9 %fusion.85 = f32[64,16384]{1,0:T(8,128)S(1)} fusion(f32[64,32]{0,1:T(8,128)S(1)} %copy-done.1, f32[8,8,128,128]{3,2,1,0:T(8,128)S(1)} %bitcast.136, f32[32]{0:T(128)S(1)} %iota_multiply_fusion.2, f32[16384]{0:T(1024)S(1)} %sqrt_bitcast_fusion.2), kind=kOutput, calls=%fused_computation.3.clone.1 | convolution fusion | flops 405274624 | bytes 8462464 | tf_op jit(solution)/shard_map/while/body/eval_jaxpr/dot_general | solution.py:35
  188.5 3.4 fusion.87
  192.0 2.9 fusion.88
  204.3 5.9 %fusion.85 = f32[64,16384]{1,0:T(8,128)S(1)} fusion(f32[64,32]{0,1:T(8,128)S(1)} %copy-done.1, f32[8,8,128,128]{3,2,1,0:T(8,128)S(1)} %bitcast.136, f32[32]{0:T(128)S(1)} %iota_multiply_fusion.2, f32[16384]{0:T(1024)S(1)} %sqrt_bitcast_fusion.2), kind=kOutput, calls=%fused_computation.3.clone.1 | convolution fusion | flops 405274624 | bytes 8462464 | tf_op jit(solution)/shard_map/while/body/eval_jaxpr/dot_general | solution.py:35
  211.8 3.4 fusion.87
  215.3 2.9 fusion.88
  227.6 5.9 %fusion.85 = f32[64,16384]{1,0:T(8,128)S(1)} fusion(f32[64,32]{0,1:T(8,128)S(1)} %copy-done.1, f32[8,8,128,128]{3,2,1,0:T(8,128)S(1)} %bitcast.136, f32[32]{0:T(128)S(1)} %iota_multiply_fusion.2, f32[16384]{0:T(1024)S(1)} %sqrt_bitcast_fusion.2), kind=kOutput, calls=%fused_computation.3.clone.1 | convolution fusion | flops 405274624 | bytes 8462464 | tf_op jit(solution)/shard_map/while/body/eval_jaxpr/dot_general | solution.py:35
  235.2 3.4 fusion.87
  238.6 2.9 fusion.88
  250.9 5.9 %fusion.85 = f32[64,16384]{1,0:T(8,128)S(1)} fusion(f32[64,32]{0,1:T(8,128)S(1)} %copy-done.1, f32[8,8,128,128]{3,2,1,0:T(8,128)S(1)} %bitcast.136, f32[32]{0:T(128)S(1)} %iota_multiply_fusion.2, f32[16384]{0:T(1024)S(1)} %sqrt_bitcast_fusion.2), kind=kOutput, calls=%fused_computation.3.clone.1 | convolution fusion | flops 405274624 | bytes 8462464 | tf_op jit(solution)/shard_map/while/body/eval_jaxpr/dot_general | solution.py:35
  258.5 3.4 fusion.87
  261.9 2.9 fusion.88
  274.2 5.9 %fusion.85 = f32[64,16384]{1,0:T(8,128)S(1)} fusion(f32[64,32]{0,1:T(8,128)S(1)} %copy-done.1, f32[8,8,128,128]{3,2,1,0:T(8,128)S(1)} %bitcast.136, f32[32]{0:T(128)S(1)} %iota_multiply_fusion.2, f32[16384]{0:T(1024)S(1)} %sqrt_bitcast_fusion.2), kind=kOutput, calls=%fused_computation.3.clone.1 | convolution fusion | flops 405274624 | bytes 8462464 | tf_op jit(solution)/shard_map/while/body/eval_jaxpr/dot_general | solution.py:35
  281.8 3.4 fusion.87
  285.2 2.9 fusion.88
  293.6 2.0 copy.16
  295.6 2.0 copy.14
  297.6 84.1 %reduce-scatter.9.cloned.1.call-done = f32[256,3]{1,0:T(8,128)} async-done(((f32[4096,3]{1,0:T(8,128)}), f32[256,3]{1,0:T(8,128)}) %reduce-scatter.9.cloned.1.call-update) | async-done | bytes 3088
  382.7 64.8 %reduce-scatter.7.cloned.1.call-done = f32[256,4]{1,0:T(8,128)} async-done(((f32[4096,4]{1,0:T(8,128)}), f32[256,4]{1,0:T(8,128)}) %reduce-scatter.7.cloned.1.call-update) | async-done | bytes 4112
  (198 shorter events, 59.3 us)
Async XLA Ops:
  7.2 71.5 %copy-start = (bf16[128,64]{0,1:T(8,128)(2,1)S(1)}, bf16[128,64]{0,1:T(8,128)(2,1)}, u32[]{:S(2)}) copy-start(bf16[128,64]{0,1:T(8,128)(2,1)} %param.19) | copy-start | bytes 49156
  7.2 71.5 %all-gather.5.cloned.1.call-start = ((), (), s32[]{:S(2)}) async-start(), calls=%async_computation.3 | async-start | bytes 1114112 | tf_op jit(solution)/shard_map/all_gather | solution.py:80
  7.9 97.5 %all-gather.3.cloned.1.call-start = ((), (), s32[]{:S(2)}) async-start(), calls=%async_computation.2 | async-start | bytes 1114112 | tf_op jit(solution)/shard_map/all_gather | solution.py:79
  8.7 373.0 %reduce-scatter.9.cloned.1.call-start = ((), (), s32[]{:S(2)}) async-start(), calls=%async_computation.5 | async-start | bytes 2228224
  107.0 4.0 copy-start.1
  111.0 5.9 %copy-start.2 = (bf16[64,64]{1,0:T(8,128)(2,1)S(1)}, bf16[64,64]{1,0:T(8,128)(2,1)}, u32[]{:S(2)}) copy-start(bf16[64,64]{1,0:T(8,128)(2,1)} %get-tuple-element.537) | copy-start | bytes 24580 | tf_op jit(solution)/shard_map/while
  117.0 1.6 copy-start.3
  130.3 4.0 copy-start.1
  134.3 5.9 %copy-start.2 = (bf16[64,64]{1,0:T(8,128)(2,1)S(1)}, bf16[64,64]{1,0:T(8,128)(2,1)}, u32[]{:S(2)}) copy-start(bf16[64,64]{1,0:T(8,128)(2,1)} %get-tuple-element.537) | copy-start | bytes 24580 | tf_op jit(solution)/shard_map/while
  140.3 1.6 copy-start.3
  153.7 4.0 copy-start.1
  157.6 5.9 %copy-start.2 = (bf16[64,64]{1,0:T(8,128)(2,1)S(1)}, bf16[64,64]{1,0:T(8,128)(2,1)}, u32[]{:S(2)}) copy-start(bf16[64,64]{1,0:T(8,128)(2,1)} %get-tuple-element.537) | copy-start | bytes 24580 | tf_op jit(solution)/shard_map/while
  163.6 1.6 copy-start.3
  177.0 4.0 copy-start.1
  181.0 5.9 %copy-start.2 = (bf16[64,64]{1,0:T(8,128)(2,1)S(1)}, bf16[64,64]{1,0:T(8,128)(2,1)}, u32[]{:S(2)}) copy-start(bf16[64,64]{1,0:T(8,128)(2,1)} %get-tuple-element.537) | copy-start | bytes 24580 | tf_op jit(solution)/shard_map/while
  186.9 1.6 copy-start.3
  200.3 4.0 copy-start.1
  204.3 5.9 %copy-start.2 = (bf16[64,64]{1,0:T(8,128)(2,1)S(1)}, bf16[64,64]{1,0:T(8,128)(2,1)}, u32[]{:S(2)}) copy-start(bf16[64,64]{1,0:T(8,128)(2,1)} %get-tuple-element.537) | copy-start | bytes 24580 | tf_op jit(solution)/shard_map/while
  210.2 1.6 copy-start.3
  223.6 4.0 copy-start.1
  227.6 5.9 %copy-start.2 = (bf16[64,64]{1,0:T(8,128)(2,1)S(1)}, bf16[64,64]{1,0:T(8,128)(2,1)}, u32[]{:S(2)}) copy-start(bf16[64,64]{1,0:T(8,128)(2,1)} %get-tuple-element.537) | copy-start | bytes 24580 | tf_op jit(solution)/shard_map/while
  233.5 1.6 copy-start.3
  246.9 4.0 copy-start.1
  250.9 5.9 %copy-start.2 = (bf16[64,64]{1,0:T(8,128)(2,1)S(1)}, bf16[64,64]{1,0:T(8,128)(2,1)}, u32[]{:S(2)}) copy-start(bf16[64,64]{1,0:T(8,128)(2,1)} %get-tuple-element.537) | copy-start | bytes 24580 | tf_op jit(solution)/shard_map/while
  256.9 1.6 copy-start.3
  270.3 4.0 copy-start.1
  274.2 5.9 %copy-start.2 = (bf16[64,64]{1,0:T(8,128)(2,1)S(1)}, bf16[64,64]{1,0:T(8,128)(2,1)}, u32[]{:S(2)}) copy-start(bf16[64,64]{1,0:T(8,128)(2,1)} %get-tuple-element.537) | copy-start | bytes 24580 | tf_op jit(solution)/shard_map/while
  280.2 1.6 copy-start.3
  295.6 151.9 %reduce-scatter.7.cloned.1.call-start = ((), (), s32[]{:S(2)}) async-start(), calls=%async_computation.4 | async-start | bytes 2228224
Sparse Core Ops, SparseCore 0:
  10.4 57.3 all-gather.4
  69.6 35.7 all-gather.2
  295.7 85.9 reduce-scatter.8
  384.2 63.1 reduce-scatter.6
where the time goes:
time: 461 us; the launch traced here: 457 us
  waiting for transfers between devices  176 us (38%)
  matrix products  126 us (27%)
  blocking collectives  68.5 us (15%)
  loops' own time  39.4 us (9%)
  local copies, waits for them, and re-layouts  18.9 us (4%)
  other arithmetic  14.6 us (3%)
  between operations  13.8 us (3%)
    unnamed x6, waiting for transfers between devices  150 us
    dot_general x8, matrix products, tile_terms(): pre1 = jnp.dot(w_radial, basis, precision=lax.Precision.HIGHEST) + pair_in  47.3 us
    all_gather x1, blocking collectives, body(): col_coords = lax.all_gather(coords, 'row', axis=1, tiled=True)  40.6 us
    another operation x1, loops' own time, body(): firsts, seconds = lax.fori_loop(0, tiles.shape[0], step, start)  39.4 us
    all_gather x1, blocking collectives, body(): row_coords = lax.all_gather(coords, 'col', axis=1, tiled=True)  27.9 us
    dot_general x8, matrix products, tile_terms(): lax.dot_general(w_hidden, back2, (((0,), (0,)), ((), ())), preferred_elem...  27.5 us
    all_gather x1, waiting for transfers between devices, body(): row_desc = lax.all_gather(features, 'col', axis=1, tiled=True)  25.2 us
    dot_general x8, matrix products, tile_terms(): lax.dot_general(w_radial, back1, (((0,), (0,)), ((), ())), precision=lax....  23.3 us
  transfers between devices with their start and end apart: 4, of which 3 were waited for; matrix products, arithmetic and copies ran while one was open for 1% of the time, Pallas kernels for 0%

commit v1 on v0

v1 whole, which is shorter than its diff:
```python
import functools

import jax
import jax.numpy as jnp
from jax import lax
from jax.experimental import pallas as pl
from jax.experimental.pallas import tpu as pltpu
from jax.sharding import PartitionSpec as P

CL = 128
CPD = 2
HID = 64
NRBF = 32
PAY = 80
ROWS = 16
SOFT = 0.01
RANGE = 6.0
SHARP = ((NRBF - 1) / RANGE) ** 2
LOG2E = 1.4426950408889634
SCALE = (SHARP * LOG2E) ** 0.5

F32 = jnp.float32
BF16 = jnp.bfloat16


def pack_kernel(fill_ref, pos_ref, feat_ref, wl_ref, wr_ref, left_ref, right_ref):
    peers = left_ref.shape[0]
    feat = feat_ref[...]
    pos = pos_ref[...]
    high = pos.astype(BF16).astype(F32)
    rest = pos - high
    mid = rest.astype(BF16).astype(F32)
    low = (rest - mid).astype(BF16).astype(F32)
    lane = lax.broadcasted_iota(jnp.int32, (1, CL), 1)
    for weight_ref, out_ref in ((wl_ref, left_ref), (wr_ref, right_ref)):
        proj = jnp.dot(weight_ref[...], feat, preferred_element_type=F32)
        for k in range(CPD):
            cut = slice(k * CL, (k + 1) * CL)
            live = (lane < fill_ref[k]).astype(F32)
            extra = jnp.concatenate(
                [high[:, cut], mid[:, cut], low[:, cut], live, jnp.zeros((6, CL), F32)], 0
            )
            both = jnp.concatenate([proj[:, cut], extra], 0).astype(BF16)
            for peer in range(peers):
                out_ref[peer, k] = both


def split(value):
    high = value.astype(BF16)
    return high, (value - high.astype(F32)).astype(BF16)


def unpack(block):
    block = block.astype(F32)
    extra = block[HID:]
    pos = extra[0:3] + extra[3:6] + extra[6:9]
    return block[:HID], pos, extra[9:10]


def tile_kernel(
    tiles_ref, count_ref, base_ref, left_ref, right_ref, wr_ref, wh_ref, wht_ref, wo_ref,
    first_ref, second_ref, mix_ref, head_ref, turned_ref, sides_ref,
):
    first_ref[...] = jnp.zeros_like(first_ref)
    second_ref[...] = jnp.zeros_like(second_ref)
    w_radial = wr_ref[...].T
    w_high, w_low = split(0.5 * w_radial)
    t_high, t_low = split(w_radial * (-SHARP / SCALE))
    mix = jnp.concatenate([w_high, w_high, w_low], 1)
    mix_ref[...] = jnp.concatenate([t_high, t_high, t_low], 1)
    wh = wh_ref[...]
    wht = wht_ref[...]
    wo = wo_ref[...]
    wo_half = jnp.broadcast_to(0.5 * wo, (HID, 2 * CL))
    wo_full = jnp.broadcast_to(wo, (HID, 2 * CL))
    centers = (
        lax.broadcasted_iota(jnp.int32, (NRBF, 2 * CL), 0).astype(F32) * (RANGE / (NRBF - 1) * SCALE)
    )
    sub = lax.broadcasted_iota(jnp.int32, (ROWS, CL), 0)
    lane = lax.broadcasted_iota(jnp.int32, (ROWS, CL), 1)

    def tile(slot, carry):
        first = tiles_ref[0, slot]
        other = tiles_ref[1, slot]
        same = base_ref[0] + first == (other // CPD * base_ref[2] + base_ref[1]) * CPD + other % CPD
        same = same.astype(F32)
        proj_a, pos_a, live_a = unpack(left_ref[first])
        proj_b, pos_b, live_b = unpack(right_ref[other])
        fill_a = jnp.sum(live_a).astype(jnp.int32)
        half_a = (0.5 * proj_a).astype(BF16)
        for g in range(CL // ROWS):
            head_ref[g] = jnp.concatenate([mix, half_a[:, g * ROWS : (g + 1) * ROWS]], 1)
        turned_ref[...] = jnp.concatenate([pos_a, live_a, jnp.zeros((CL - 4, CL), F32)], 0).T
        sides_ref[...] = jnp.zeros_like(sides_ref)
        add_b = jnp.concatenate([0.5 * proj_b] * 2, 1)

        def block(g, sums):
            start = pl.multiple_of(g * ROWS, ROWS)
            mine = turned_ref[pl.ds(start, ROWS), :]
            delta = [mine[:, c : c + 1] - pos_b[c : c + 1] for c in range(3)]
            dist = jnp.sqrt(delta[0] * delta[0] + delta[1] * delta[1] + delta[2] * delta[2] + SOFT)
            scaled = dist * SCALE
            head = head_ref[g]
            tail = mix_ref[...]
            slopes = []
            energies = []
            for c in range(ROWS // 2):
                row = jnp.concatenate([scaled[2 * c : 2 * c + 1], scaled[2 * c + 1 : 2 * c + 2]], 1)
                offset = row - centers
                basis = jnp.exp2(-(offset * offset))
                b_high, b_low = split(basis)
                d_high, d_low = split(basis * offset)
                sel = lax.broadcasted_iota(jnp.int32, (ROWS, 2 * CL), 0)
                which = lax.broadcasted_iota(jnp.int32, (ROWS, 2 * CL), 1) // CL + 2 * c
                pick = (sel == which).astype(F32).astype(BF16)
                stacked = jnp.concatenate([b_high, b_low, b_high, pick], 0)
                half1 = jnp.dot(head, stacked, preferred_element_type=F32) + add_b
                tangent = jnp.dot(
                    tail, jnp.concatenate([d_high, d_low, d_high], 0), preferred_element_type=F32
                )
                up1 = 1.0 + jnp.tanh(half1)
                silu1 = half1 * up1
                grad1 = up1 + silu1 * (2.0 - up1)
                half2 = jnp.dot(wh, silu1.astype(BF16), preferred_element_type=F32)
                up2 = 1.0 + jnp.tanh(half2)
                silu2 = half2 * up2
                grad2 = up2 + silu2 * (2.0 - up2)
                back2 = (wo_half * grad2).astype(BF16)
                back1 = jnp.dot(wht, back2, preferred_element_type=F32)
                slope = jnp.sum(back1 * (grad1 * tangent), 0, keepdims=True)
                energy = jnp.sum(silu2.astype(BF16).astype(F32) * wo_full, 0, keepdims=True)
                slopes += [slope[:, :CL], slope[:, CL:]]
                energies += [energy[:, :CL], energy[:, CL:]]
            slope = jnp.concatenate(slopes, 0)
            energy = jnp.concatenate(energies, 0)
            mask = mine[:, 3:4] * live_b * (1.0 - same * (sub + start == lane).astype(F32))
            weight = mask * slope / dist
            pulls = [weight * d for d in delta]
            parts = [jnp.sum(p, 1, keepdims=True) for p in pulls]
            parts.append(jnp.sum(mask * energy, 1, keepdims=True))
            side = jnp.zeros((ROWS, CL), F32)
            for c in range(4):
                sign = -1.0 if c < 3 else 1.0
                side = jnp.where(lane == c, sign * parts[c], side)
            sides_ref[pl.ds(start, ROWS), :] = side
            return tuple(s + p for s, p in zip(sums, pulls))

        blank = jnp.zeros((ROWS, CL), F32)
        sums = lax.fori_loop(0, (fill_a + ROWS - 1) // ROWS, block, (blank, blank, blank))
        firsts = sides_ref[...].T[:4]
        seconds = jnp.concatenate(
            [jnp.sum(s, 0, keepdims=True) for s in sums] + [jnp.zeros((1, CL), F32)], 0
        )
        row8 = lax.broadcasted_iota(jnp.int32, (8, CL), 0) // 4
        first_ref[first // CPD] += jnp.where(row8 == first % CPD, jnp.concatenate([firsts] * 2, 0), 0.0)
        second_ref[other // CPD] += jnp.where(
            row8 == other % CPD, jnp.concatenate([seconds] * 2, 0), 0.0
        )
        return carry

    lax.fori_loop(0, count_ref[0], tile, 0)


def add_kernel(first_ref, second_ref, force_ref, energy_ref):
    total = first_ref[0]
    other = second_ref[0]
    for peer in range(1, first_ref.shape[0]):
        total = total + first_ref[peer]
    for peer in range(1, second_ref.shape[0]):
        other = other + second_ref[peer]
    force = total + other
    for k in range(CPD):
        cut = slice(k * CL, (k + 1) * CL)
        force_ref[:, cut] = force[4 * k : 4 * k + 3]
        energy_ref[:, cut] = total[4 * k + 3 : 4 * k + 4]


def body(positions, features, fill, tiles, tile_count, w_radial, w_left, w_right, w_hidden, w_out):
    rows = lax.axis_size("row")
    cols = lax.axis_size("col")
    smem = pl.BlockSpec(memory_space=pltpu.SMEM)
    vmem = pl.BlockSpec(memory_space=pltpu.VMEM)
    with jax.named_scope("pack"):
        left, right = pl.pallas_call(
            pack_kernel,
            out_shape=(
                jax.ShapeDtypeStruct((cols, CPD, PAY, CL), BF16),
                jax.ShapeDtypeStruct((rows, CPD, PAY, CL), BF16),
            ),
            in_specs=[smem] + [vmem] * 4,
            out_specs=(vmem, vmem),
        )(fill, positions, features, w_left.T, w_right.T)
    with jax.named_scope("spread"):
        left = lax.all_to_all(left, "col", 0, 0).reshape(cols * CPD, PAY, CL)
        right = lax.all_to_all(right, "row", 0, 0).reshape(rows * CPD, PAY, CL)
    base = jnp.stack([lax.axis_index("row") * cols * CPD, lax.axis_index("col"), jnp.int32(cols)])
    with jax.named_scope("tiles"):
        firsts, seconds = pl.pallas_call(
            tile_kernel,
            out_shape=(
                jax.ShapeDtypeStruct((cols, 8, CL), F32),
                jax.ShapeDtypeStruct((rows, 8, CL), F32),
            ),
            in_specs=[smem] * 3 + [vmem] * 6,
            out_specs=(vmem, vmem),
            scratch_shapes=[
                pltpu.VMEM((HID, 3 * NRBF), BF16),
                pltpu.VMEM((CL // ROWS, HID, 3 * NRBF + ROWS), BF16),
                pltpu.VMEM((CL, CL), F32),
                pltpu.VMEM((CL, CL), F32),
            ],
            compiler_params=pltpu.CompilerParams(vmem_limit_bytes=48 * 1024 * 1024),
        )(
            tiles.T, tile_count, base, left, right, w_radial.T,
            w_hidden * 0.5, w_hidden.T, w_out.astype(F32)[:, None],
        )
    with jax.named_scope("collect"):
        firsts = lax.all_to_all(firsts, "col", 0, 0)
        seconds = lax.all_to_all(seconds, "row", 0, 0)
    with jax.named_scope("add"):
        force, energy = pl.pallas_call(
            add_kernel,
            out_shape=(
                jax.ShapeDtypeStruct((3, CPD * CL), F32),
                jax.ShapeDtypeStruct((1, CPD * CL), F32),
            ),
        )(firsts, seconds)
    return force, energy.reshape(CPD * CL)


def solution(mesh):
    return jax.shard_map(
        body,
        mesh=mesh,
        in_specs=(
            P(None, ("row", "col")),
            P(None, ("row", "col")),
            P(("row", "col")),
            P(("row", "col"), None),
            P(("row", "col")),
            P(),
            P(),
            P(),
            P(),
            P(),
        ),
        out_specs=(P(None, ("row", "col")), P(("row", "col"))),
        check_vma=False,
    )
```

time: 461 us -> 185 us (0.40); the launches traced: 457 us -> 188 us
  waiting for transfers between devices: 176 us -> 17.1 us
  matrix products: 126 us -> 0 us
  Pallas kernels: 0 us -> 62.9 us
  loops' own time: 39.4 us -> 0 us
  blocking collectives: 68.5 us -> 94.2 us
  local copies, waits for them, and re-layouts: 18.9 us -> 2.14 us
  other arithmetic: 14.6 us -> 0.08 us
  between operations: 13.8 us -> 1.33 us
  starting transfers between devices: 0.16 us -> 9.85 us
    unnamed x6 -> x0, waiting for transfers between devices: 150 us -> none
    dot_general x58 -> x0, matrix products: 126 us -> none  [the longest x8 47.3 us: tile_terms(): pre1 = jnp.dot(w_radial, basis, precision=lax.Precision.HIGHEST) + pair_in]
    all_to_all x0 -> x3, blocking collectives: none -> 94.2 us  [the longest x1 50.5 us: body(): firsts = lax.all_to_all(firsts, 'col', 0, 0)]
    all_gather x2 -> x0, blocking collectives: 68.5 us -> none  [the longest x1 40.6 us: body(): col_coords = lax.all_gather(coords, 'row', axis=1, tiled=True)]
    pallas_call x0 -> x3, Pallas kernels: none -> 62.9 us  [the longest x1 59.3 us: body(): pl.pallas_call(tile_kernel, out_shape=(jax.ShapeDtypeStruct((cols, 8, CL)...]
    another operation x1 -> x0, loops' own time: 39.4 us -> none  [body(): firsts, seconds = lax.fori_loop(0, tiles.shape[0], step, start)]
    all_gather x2 -> x0, waiting for transfers between devices: 25.2 us -> none  [the longest x1 25.2 us: body(): row_desc = lax.all_gather(features, 'col', axis=1, tiled=True)]
    all_to_all x0 -> x1, waiting for transfers between devices: none -> 17.1 us  [body(): right = lax.all_to_all(right, 'row', 0, 0).reshape(rows * CPD, PAY, CL)]
  transfers between devices with their start and end apart: 4 -> 1, of which waited for: 3 -> 1; matrix products, arithmetic and copies ran while one was open for 1% -> 0% of each run, Pallas kernels for 0% -> 0%
where the time goes in v1:
time: 185 us; the launch traced here: 188 us
  blocking collectives  94.2 us (51%)
  Pallas kernels  62.9 us (34%)
  waiting for transfers between devices  17.1 us (9%)
  starting transfers between devices  9.85 us (5%)
  local copies, waits for them, and re-layouts  2.14 us (1%)
    pallas_call x1, Pallas kernels, body(): pl.pallas_call(tile_kernel, out_shape=(jax.ShapeDtypeStruct((cols, 8, CL)...  59.3 us
    all_to_all x1, blocking collectives, body(): firsts = lax.all_to_all(firsts, 'col', 0, 0)  50.5 us
    all_to_all x1, blocking collectives, body(): seconds = lax.all_to_all(seconds, 'row', 0, 0)  24.6 us
    all_to_all x1, blocking collectives, body(): left = lax.all_to_all(left, 'col', 0, 0).reshape(cols * CPD, PAY, CL)  19.1 us
    all_to_all x1, waiting for transfers between devices, body(): right = lax.all_to_all(right, 'row', 0, 0).reshape(rows * CPD, PAY, CL)  17.1 us
    all_to_all x1, starting transfers between devices, body(): right = lax.all_to_all(right, 'row', 0, 0).reshape(rows * CPD, PAY, CL)  9.85 us
  transfers between devices with their start and end apart: 1, of which 1 were waited for; matrix products, arithmetic and copies ran while one was open for 0% of the time, Pallas kernels for 0%

profile of v1, /device:TPU:1, one launch (start us, length us, event | category | flops | bytes accessed | tf_op | source)
XLA Modules:
  0.0 187.6 jit_solution(14475198751112683167)
XLA Ops:
  0.6 2.1 %pack.1 = (bf16[16,2,80,128]{3,2,1,0:T(8,128)(2,1)}, bf16[16,2,80,128]{3,2,1,0:T(8,128)(2,1)}) custom-call(s32[2]{0:T(128)} %fill_ref.1, f32[3,256]{1,0:T(4,128)} %pos_ref.1, bf16[128,256]{1,0:T(8,128)(2,1)} %feat_ref.1, bf16[64,128]{1,0:T(8,128)(2,1)} %bitcast.18, bf16[64,128]{1,0:T(8,128)(2,1)} %bitcast.19), custom_call_target="tpu_custom_call" | custom-call | tf_op jit(solution)/shard_map/pack/pallas_call | solution.py:184
  2.8 19.1 %all_to_all.20 = bf16[16,2,80,128]{3,2,1,0:T(8,128)(2,1)S(1)} all-to-all(bf16[16,2,80,128]{3,2,1,0:T(8,128)(2,1)} %get-tuple-element.8), channel_id=1, replica_groups=mesh['row'=16,'col'=16] {'col'}, dimensions={0} | all-to-all | bytes 1310720 | tf_op jit(solution)/shard_map/spread/all_to_all | solution.py:194
  21.9 9.9 %all-to-all-start.1 = ((bf16[16,2,80,128]{3,2,1,0:T(8,128)(2,1)}), bf16[16,2,80,128]{3,2,1,0:T(8,128)(2,1)S(1)}, u32[]{:S(2)}, u32[]{:S(2)}) async-start(bf16[16,2,80,128]{3,2,1,0:T(8,128)(2,1)} %get-tuple-element.9), calls=%async_computation.1 | async-start | bytes 1310720 | tf_op jit(solution)/shard_map/spread/all_to_all | solution.py:195
  31.7 0.0 copy-start.3
  31.7 0.6 copy-done.3
  32.4 0.0 copy-start.2
  32.4 0.1 copy.13.wo_ref
  32.5 0.6 copy-done.2
  33.1 0.1 copy.12
  33.9 0.1 pad_add_fusion.base_ref
  33.9 0.0 copy-start
  33.9 17.1 %all-to-all-done.1 = bf16[16,2,80,128]{3,2,1,0:T(8,128)(2,1)S(1)} async-done(((bf16[16,2,80,128]{3,2,1,0:T(8,128)(2,1)}), bf16[16,2,80,128]{3,2,1,0:T(8,128)(2,1)S(1)}, u32[]{:S(2)}, u32[]{:S(2)}) %all-to-all-start.1) | async-done | bytes 655392 | tf_op jit(solution)/shard_map/spread/all_to_all | solution.py:195
  51.0 0.0 copy-start.1
  51.0 0.0 copy-done
  51.0 0.7 copy-done.1
  51.7 59.3 %tiles.1 = (f32[16,8,128]{2,1,0:T(8,128)S(1)}, f32[16,8,128]{2,1,0:T(8,128)S(1)}) custom-call(s32[2,8]{1,0:T(2,128)S(1)} %bitcast.17, s32[1]{0:T(128)S(6)} %copy.14.count_ref, s32[3]{0:T(128)S(1)} %pad_add_fusion.base_ref, bf16[32,80,128]{2,1,0:T(8,128)(2,1)S(1)} %bitcast.13, bf16[32,80,128]{2,1,0:T(8,128)(2,1)S(1)} %bitcast.14, f32[32,64]{1,0:T(8,128)S(1)} %bitcast.16, ...), custom_call_target="tpu_custom_call" | custom-call | tf_op jit(solution)/shard_map/tiles/pallas_call | solution.py:198
  111.0 50.5 %all_to_all.21.first_ref = f32[16,8,128]{2,1,0:T(8,128)} all-to-all(f32[16,8,128]{2,1,0:T(8,128)S(1)} %get-tuple-element.10), channel_id=1, replica_groups=mesh['row'=16,'col'=16] {'col'}, dimensions={0} | all-to-all | bytes 131072 | tf_op jit(solution)/shard_map/collect/all_to_all | solution.py:218
  161.6 24.6 %all_to_all.22.second_ref = f32[16,8,128]{2,1,0:T(8,128)} all-to-all(f32[16,8,128]{2,1,0:T(8,128)S(1)} %get-tuple-element.11), channel_id=1, replica_groups=mesh['row'=16,'col'=16] {'row'}, dimensions={0} | all-to-all | bytes 131072 | tf_op jit(solution)/shard_map/collect/all_to_all | solution.py:219
  186.1 1.5 add.5
  (2 shorter events, 0.0 us)
Async XLA Ops:
  21.9 29.2 %all-to-all-start.1 = ((bf16[16,2,80,128]{3,2,1,0:T(8,128)(2,1)}), bf16[16,2,80,128]{3,2,1,0:T(8,128)(2,1)S(1)}, u32[]{:S(2)}, u32[]{:S(2)}) async-start(bf16[16,2,80,128]{3,2,1,0:T(8,128)(2,1)} %get-tuple-element.9), calls=%async_computation.1 | async-start | bytes 1310720 | tf_op jit(solution)/shard_map/spread/all_to_all | solution.py:195
  31.7 0.7 copy-start.3
  32.4 0.7 copy-start.2
  33.9 17.1 %copy-start = (f32[64,32]{0,1:T(8,128)S(1)}, f32[64,32]{0,1:T(8,128)}, u32[]{:S(2)}) copy-start(f32[64,32]{0,1:T(8,128)} %param.15) | copy-start | bytes 24580
  51.0 0.7 copy-start.1

commit v2 on v1

v2 whole, which is shorter than its diff:
```python
import functools

import jax
import jax.numpy as jnp
from jax import lax
from jax.experimental import pallas as pl
from jax.experimental.pallas import tpu as pltpu
from jax.sharding import PartitionSpec as P

CL = 128
CPD = 2
HID = 64
NRBF = 32
PAY = 80
ROWS = 16
SOFT = 0.01
RANGE = 6.0
SHARP = ((NRBF - 1) / RANGE) ** 2
LOG2E = 1.4426950408889634
SCALE = (SHARP * LOG2E) ** 0.5

F32 = jnp.float32
BF16 = jnp.bfloat16


def pack_kernel(fill_ref, pos_ref, feat_ref, wl_ref, wr_ref, left_ref, right_ref):
    peers = left_ref.shape[0]
    feat = feat_ref[...]
    pos = pos_ref[...]
    high = pos.astype(BF16).astype(F32)
    rest = pos - high
    mid = rest.astype(BF16).astype(F32)
    low = (rest - mid).astype(BF16).astype(F32)
    lane = lax.broadcasted_iota(jnp.int32, (1, CL), 1)
    for weight_ref, out_ref in ((wl_ref, left_ref), (wr_ref, right_ref)):
        proj = jnp.dot(weight_ref[...], feat, preferred_element_type=F32)
        for k in range(CPD):
            cut = slice(k * CL, (k + 1) * CL)
            live = (lane < fill_ref[k]).astype(F32)
            extra = jnp.concatenate(
                [high[:, cut], mid[:, cut], low[:, cut], live, jnp.zeros((6, CL), F32)], 0
            )
            both = jnp.concatenate([proj[:, cut], extra], 0).astype(BF16)
            for peer in range(peers):
                out_ref[peer, k] = both


def unpack(block):
    block = block.astype(F32)
    extra = block[HID:]
    pos = extra[0:3] + extra[3:6] + extra[6:9]
    return block[:HID], pos, extra[9:10]


def spread4(value):
    rows, cols = value.shape
    tall = jnp.concatenate([value] * 4, 0)
    wide = jnp.concatenate([tall] * 4, 1)
    down = lax.broadcasted_iota(jnp.int32, wide.shape, 0) // rows
    across = lax.broadcasted_iota(jnp.int32, wide.shape, 1) // cols
    return jnp.where(down == across, wide, 0.0)


def tile_kernel(
    tiles_ref, count_ref, base_ref, left_ref, right_ref, wr_ref, wh_ref, wo_ref,
    first_ref, second_ref,
    radial_ref, tangent_ref, hidden_ref, back_ref, out_ref, pick_ref, head_ref, adds_ref,
    turned_ref, across_ref, slopes_ref, energies_ref, half1_ref, rate_ref, half2_ref, chain_ref, blocks_ref,
):
    count = count_ref[0]
    wide = 2 * CL
    first_ref[...] = jnp.zeros_like(first_ref)
    second_ref[...] = jnp.zeros_like(second_ref)
    w_radial = wr_ref[...].T
    for into_ref, scale in ((radial_ref, 0.5), (tangent_ref, -SHARP / SCALE)):
        full = spread4(scale * w_radial)
        high = full.astype(BF16).astype(F32)
        into_ref[...] = jnp.concatenate([high, full - high], 1).astype(BF16)
    w_hidden = wh_ref[...].astype(F32)
    w_out = wo_ref[...]
    hidden_ref[...] = spread4(0.5 * w_hidden).astype(BF16)
    back_ref[...] = spread4(w_hidden.T).astype(BF16)
    half_out = jnp.broadcast_to(jnp.concatenate([0.5 * w_out] * 4, 0), (4 * HID, wide))
    flat_out = jnp.concatenate([w_out.T] * 4, 1)
    lane8 = lax.broadcasted_iota(jnp.int32, (8, 4 * HID), 1) // HID
    sub8 = lax.broadcasted_iota(jnp.int32, (8, 4 * HID), 0)
    out_ref[...] = jnp.where(lane8 == sub8, flat_out, 0.0).astype(BF16)
    quad = lax.broadcasted_iota(jnp.int32, (CL, wide), 0) // 4
    side = lax.broadcasted_iota(jnp.int32, (CL, wide), 1) // CL
    for g in range(CL // 8):
        pick_ref[g] = (quad == 2 * g + side).astype(F32).astype(BF16)
    centers = (
        lax.broadcasted_iota(jnp.int32, (NRBF, wide), 0).astype(F32) * (RANGE / (NRBF - 1) * SCALE)
    )
    ident = (
        lax.broadcasted_iota(jnp.int32, (HID, HID), 0)
        == lax.broadcasted_iota(jnp.int32, (HID, HID), 1)
    ).astype(F32)
    lane4 = lax.broadcasted_iota(jnp.int32, (HID, CL), 1) % 4

    def prepare(slot, carry):
        proj_a, pos_a, live_a = unpack(left_ref[tiles_ref[0, slot]])
        proj_b, pos_b, live_b = unpack(right_ref[tiles_ref[1, slot]])
        half_a = 0.5 * proj_a
        cols = jnp.concatenate([jnp.where(lane4 == q, half_a, 0.0) for q in range(4)], 0)
        head_ref[slot] = jnp.concatenate([cols, jnp.concatenate([ident] * 4, 0)], 1).astype(BF16)
        adds_ref[slot] = jnp.concatenate([0.5 * proj_b] * 2, 1).astype(BF16)
        turned_ref[slot] = jnp.concatenate([pos_a, live_a, jnp.zeros((CL - 4, CL), F32)], 0).T
        across_ref[slot] = jnp.concatenate([pos_b, live_b, jnp.zeros((4, CL), F32)], 0)
        fill_a = jnp.sum(live_a).astype(jnp.int32)
        blocks_ref[slot] = (fill_a + ROWS - 1) // ROWS
        return carry

    lax.fori_loop(0, count, prepare, 0)

    def distances(mine, across):
        delta = [mine[:, c : c + 1] - across[c : c + 1] for c in range(3)]
        dist = jnp.sqrt(delta[0] * delta[0] + delta[1] * delta[1] + delta[2] * delta[2] + SOFT)
        return delta, dist

    def enter(slot, g):
        start = pl.multiple_of(g * ROWS, ROWS)
        mine = turned_ref[slot, pl.ds(start, ROWS), :]
        scaled = distances(mine, across_ref[slot])[1] * SCALE
        head = jnp.concatenate([radial_ref[...], head_ref[slot]], 1)
        for e in range(ROWS // 8):
            bases = []
            rates = []
            for q in range(4):
                r = 8 * e + q
                row = jnp.concatenate([scaled[r : r + 1], scaled[r + 4 : r + 5]], 1)
                offset = row - centers
                basis = jnp.exp2(-(offset * offset))
                bases.append(basis.astype(BF16))
                rates.append((basis * offset).astype(BF16))
            tail = jnp.concatenate(
                bases + bases + [pick_ref[g * (ROWS // 8) + e], adds_ref[slot]], 0
            )
            half1_ref[e] = jnp.dot(head, tail, preferred_element_type=F32)
            rate_ref[e] = jnp.dot(
                tangent_ref[...], jnp.concatenate(rates + rates, 0), preferred_element_type=F32
            )

    def middle():
        for e in range(ROWS // 8):
            half1 = half1_ref[e]
            up1 = 1.0 + jnp.tanh(half1)
            silu1 = half1 * up1
            grad1 = up1 + silu1 * (2.0 - up1)
            chain_ref[e] = grad1 * rate_ref[e]
            half2_ref[e] = jnp.dot(hidden_ref[...], silu1.astype(BF16), preferred_element_type=F32)

    def leave(slot, g):
        for e in range(ROWS // 8):
            half2 = half2_ref[e]
            up2 = 1.0 + jnp.tanh(half2)
            silu2 = half2 * up2
            grad2 = up2 + silu2 * (2.0 - up2)
            back1 = jnp.dot(back_ref[...], (half_out * grad2).astype(BF16), preferred_element_type=F32)
            energy = jnp.dot(out_ref[...], silu2.astype(BF16), preferred_element_type=F32)
            terms = back1 * chain_ref[e]
            lines = jnp.concatenate(
                [jnp.sum(terms[q * HID : (q + 1) * HID], 0, keepdims=True) for q in range(4)], 0
            )
            at = pl.ds(pl.multiple_of(g * ROWS + 8 * e, 8), 8)
            slopes_ref[slot, at, :] = jnp.concatenate([lines[:, :CL], lines[:, CL:]], 0)
            energies_ref[slot, at, :] = jnp.concatenate([energy[:4, :CL], energy[:4, CL:]], 0)

    spare = slopes_ref.shape[0] - 1

    def step(carry):
        slot, g, slot1, g1, slot2, g2, left = carry
        leave(slot2, g2)
        middle()
        enter(slot, g)
        last = g + 1 >= blocks_ref[slot]
        ended = jnp.logical_and(last, slot + 1 >= count)
        slot2, g2 = slot1, g1
        slot1 = jnp.where(left > 2, slot, spare)
        g1 = g
        g = jnp.where(ended, g, jnp.where(last, 0, g + 1))
        slot = jnp.where(jnp.logical_and(last, jnp.logical_not(ended)), slot + 1, slot)
        return slot, g, slot1, g1, slot2, g2, left - 1

    total = lax.fori_loop(0, count, lambda slot, n: n + blocks_ref[slot], 0)
    zero = jnp.int32(0)
    far = jnp.int32(spare)
    lax.while_loop(
        lambda carry: carry[6] > 0, step, (zero, zero, far, zero, far, zero, total + 2)
    )

    sub = lax.broadcasted_iota(jnp.int32, (CL, CL), 0)
    lane = lax.broadcasted_iota(jnp.int32, (CL, CL), 1)
    row8 = lax.broadcasted_iota(jnp.int32, (8, CL), 0) // 4

    def finish(slot, carry):
        first = tiles_ref[0, slot]
        other = tiles_ref[1, slot]
        same = base_ref[0] + first == (other // CPD * base_ref[2] + base_ref[1]) * CPD + other % CPD
        mine = turned_ref[slot]
        across = across_ref[slot]
        delta, dist = distances(mine, across)
        mask = mine[:, 3:4] * across[3:4]
        keep = jnp.logical_and(mask > 0.0, jnp.logical_or(jnp.logical_not(same), sub != lane))
        weight = jnp.where(keep, slopes_ref[slot] / dist, 0.0)
        pulls = [weight * d for d in delta]
        parts = [-jnp.sum(p, 1, keepdims=True) for p in pulls]
        parts.append(jnp.sum(jnp.where(keep, energies_ref[slot], 0.0), 1, keepdims=True))
        side = jnp.zeros((CL, CL), F32)
        for c in range(4):
            side = jnp.where(lane == c, parts[c], side)
        firsts = side.T[:4]
        seconds = jnp.concatenate(
            [jnp.sum(p, 0, keepdims=True) for p in pulls] + [jnp.zeros((1, CL), F32)], 0
        )
        first_ref[first // CPD] += jnp.where(row8 == first % CPD, jnp.concatenate([firsts] * 2, 0), 0.0)
        second_ref[other // CPD] += jnp.where(
            row8 == other % CPD, jnp.concatenate([seconds] * 2, 0), 0.0
        )
        return carry

    lax.fori_loop(0, count, finish, 0)


def tile_call(tiles, tile_count, base, left, right, w_radial, w_hidden, w_out):
    smem = pl.BlockSpec(memory_space=pltpu.SMEM)
    vmem = pl.BlockSpec(memory_space=pltpu.VMEM)
    slots = tiles.shape[0]
    groups = ROWS // 8
    hid4 = 4 * HID
    wide = 2 * CL
    return pl.pallas_call(
        tile_kernel,
        name="tiles",
        out_shape=(
            jax.ShapeDtypeStruct((left.shape[0] // CPD, 8, CL), F32),
            jax.ShapeDtypeStruct((right.shape[0] // CPD, 8, CL), F32),
        ),
        in_specs=[smem] * 3 + [vmem] * 5,
        out_specs=(vmem, vmem),
        scratch_shapes=[
            pltpu.VMEM((hid4, 8 * NRBF), BF16),
            pltpu.VMEM((hid4, 8 * NRBF), BF16),
            pltpu.VMEM((hid4, hid4), BF16),
            pltpu.VMEM((hid4, hid4), BF16),
            pltpu.VMEM((8, hid4), BF16),
            pltpu.VMEM((CL // 8, CL, wide), BF16),
            pltpu.VMEM((slots, hid4, CL + HID), BF16),
            pltpu.VMEM((slots, HID, wide), BF16),
            pltpu.VMEM((slots, CL, CL), F32),
            pltpu.VMEM((slots, 8, CL), F32),
            pltpu.VMEM((slots + 1, CL, CL), F32),
            pltpu.VMEM((slots + 1, CL, CL), F32),
            pltpu.VMEM((groups, hid4, wide), F32),
            pltpu.VMEM((groups, hid4, wide), F32),
            pltpu.VMEM((groups, hid4, wide), F32),
            pltpu.VMEM((groups, hid4, wide), F32),
            pltpu.SMEM((slots,), jnp.int32),
        ],
        compiler_params=pltpu.CompilerParams(vmem_limit_bytes=48 * 1024 * 1024),
    )(
        tiles.T, tile_count, base, left, right, w_radial.T, w_hidden, w_out.astype(F32)[:, None],
    )


def add_kernel(first_ref, second_ref, force_ref, energy_ref):
    total = first_ref[0]
    other = second_ref[0]
    for peer in range(1, first_ref.shape[0]):
        total = total + first_ref[peer]
    for peer in range(1, second_ref.shape[0]):
        other = other + second_ref[peer]
    force = total + other
    for k in range(CPD):
        cut = slice(k * CL, (k + 1) * CL)
        force_ref[:, cut] = force[4 * k : 4 * k + 3]
        energy_ref[:, cut] = total[4 * k + 3 : 4 * k + 4]


def body(positions, features, fill, tiles, tile_count, w_radial, w_left, w_right, w_hidden, w_out):
    rows = lax.axis_size("row")
    cols = lax.axis_size("col")
    smem = pl.BlockSpec(memory_space=pltpu.SMEM)
    vmem = pl.BlockSpec(memory_space=pltpu.VMEM)
    with jax.named_scope("pack"):
        left, right = pl.pallas_call(
            pack_kernel,
            out_shape=(
                jax.ShapeDtypeStruct((cols, CPD, PAY, CL), BF16),
                jax.ShapeDtypeStruct((rows, CPD, PAY, CL), BF16),
            ),
            in_specs=[smem] + [vmem] * 4,
            out_specs=(vmem, vmem),
        )(fill, positions, features, w_left.T, w_right.T)
    with jax.named_scope("spread"):
        left = lax.all_to_all(left, "col", 0, 0).reshape(cols * CPD, PAY, CL)
        right = lax.all_to_all(right, "row", 0, 0).reshape(rows * CPD, PAY, CL)
    base = jnp.stack([lax.axis_index("row") * cols * CPD, lax.axis_index("col"), jnp.int32(cols)])
    with jax.named_scope("tiles"):
        firsts, seconds = tile_call(
            tiles, tile_count, base, left, right, w_radial, w_hidden, w_out
        )
    with jax.named_scope("collect"):
        firsts = lax.all_to_all(firsts, "col", 0, 0)
        seconds = lax.all_to_all(seconds, "row", 0, 0)
    with jax.named_scope("add"):
        force, energy = pl.pallas_call(
            add_kernel,
            out_shape=(
                jax.ShapeDtypeStruct((3, CPD * CL), F32),
                jax.ShapeDtypeStruct((1, CPD * CL), F32),
            ),
        )(firsts, seconds)
    return force, energy.reshape(CPD * CL)


def solution(mesh):
    return jax.shard_map(
        body,
        mesh=mesh,
        in_specs=(
            P(None, ("row", "col")),
            P(None, ("row", "col")),
            P(("row", "col")),
            P(("row", "col"), None),
            P(("row", "col")),
            P(),
            P(),
            P(),
            P(),
            P(),
        ),
        out_specs=(P(None, ("row", "col")), P(("row", "col"))),
        check_vma=False,
    )
```

time: 185 us -> 121 us (0.65); the launches traced: 188 us -> 120 us
  blocking collectives: 94.2 us -> 53.9 us
  Pallas kernels: 62.9 us -> 35.9 us
    all_to_all x1, blocking collectives: 50.5 us -> 21.8 us  [body(): firsts = lax.all_to_all(firsts, 'col', 0, 0)]
    pallas_call x1, Pallas kernels: 59.3 us -> 32.3 us  [tile_call(): pl.pallas_call(tile_kernel, name='tiles', out_shape=(jax.ShapeDtypeStruct...]
    all_to_all x1, blocking collectives: 24.6 us -> 13 us  [body(): seconds = lax.all_to_all(seconds, 'row', 0, 0)]
where the time goes in v2:
time: 121 us; the launch traced here: 120 us
  blocking collectives  53.9 us (45%)
  Pallas kernels  35.9 us (30%)
  waiting for transfers between devices  17.8 us (15%)
  starting transfers between devices  9.85 us (8%)
  local copies, waits for them, and re-layouts  1.43 us (1%)
  between operations  1.32 us (1%)
    pallas_call x1, Pallas kernels, tile_call(): pl.pallas_call(tile_kernel, name='tiles', out_shape=(jax.ShapeDtypeStruct...  32.3 us
    all_to_all x1, blocking collectives, body(): firsts = lax.all_to_all(firsts, 'col', 0, 0)  21.8 us
    all_to_all x1, blocking collectives, body(): left = lax.all_to_all(left, 'col', 0, 0).reshape(cols * CPD, PAY, CL)  19.1 us
    all_to_all x1, waiting for transfers between devices, body(): right = lax.all_to_all(right, 'row', 0, 0).reshape(rows * CPD, PAY, CL)  17.8 us
    all_to_all x1, blocking collectives, body(): seconds = lax.all_to_all(seconds, 'row', 0, 0)  13 us
    all_to_all x1, starting transfers between devices, body(): right = lax.all_to_all(right, 'row', 0, 0).reshape(rows * CPD, PAY, CL)  9.85 us
  transfers between devices with their start and end apart: 1, of which 1 were waited for; matrix products, arithmetic and copies ran while one was open for 0% of the time, Pallas kernels for 0%

profile of v2, /device:TPU:1, one launch (start us, length us, event | category | flops | bytes accessed | tf_op | source)
XLA Modules:
  0.0 120.2 jit_solution(15542614441550101889)
XLA Ops:
  0.6 2.1 %pack.1 = (bf16[16,2,80,128]{3,2,1,0:T(8,128)(2,1)}, bf16[16,2,80,128]{3,2,1,0:T(8,128)(2,1)}) custom-call(s32[2]{0:T(128)} %fill_ref.1, f32[3,256]{1,0:T(4,128)} %pos_ref.1, bf16[128,256]{1,0:T(8,128)(2,1)} %feat_ref.1, bf16[64,128]{1,0:T(8,128)(2,1)} %bitcast.16, bf16[64,128]{1,0:T(8,128)(2,1)} %bitcast.17), custom_call_target="tpu_custom_call" | custom-call | tf_op jit(solution)/shard_map/pack/pallas_call | solution.py:286
  2.8 19.1 %all_to_all.20 = bf16[16,2,80,128]{3,2,1,0:T(8,128)(2,1)S(1)} all-to-all(bf16[16,2,80,128]{3,2,1,0:T(8,128)(2,1)} %get-tuple-element.8), channel_id=1, replica_groups=mesh['row'=16,'col'=16] {'col'}, dimensions={0} | all-to-all | bytes 1310720 | tf_op jit(solution)/shard_map/spread/all_to_all | solution.py:296
  21.9 9.9 %all-to-all-start.1 = ((bf16[16,2,80,128]{3,2,1,0:T(8,128)(2,1)}), bf16[16,2,80,128]{3,2,1,0:T(8,128)(2,1)S(1)}, u32[]{:S(2)}, u32[]{:S(2)}) async-start(bf16[16,2,80,128]{3,2,1,0:T(8,128)(2,1)} %get-tuple-element.9), calls=%async_computation.1 | async-start | bytes 1310720 | tf_op jit(solution)/shard_map/spread/all_to_all | solution.py:297
  31.7 0.0 copy-start.3
  31.7 0.6 copy-done.3
  32.4 0.0 copy-start.1
  32.4 0.1 copy.12.wo_ref
  32.5 0.0 copy-start
  33.2 0.1 pad_add_fusion.base_ref
  33.2 17.8 %all-to-all-done.1 = bf16[16,2,80,128]{3,2,1,0:T(8,128)(2,1)S(1)} async-done(((bf16[16,2,80,128]{3,2,1,0:T(8,128)(2,1)}), bf16[16,2,80,128]{3,2,1,0:T(8,128)(2,1)S(1)}, u32[]{:S(2)}, u32[]{:S(2)}) %all-to-all-start.1) | async-done | bytes 655392 | tf_op jit(solution)/shard_map/spread/all_to_all | solution.py:297
  51.0 0.0 copy-start.2
  51.0 0.0 copy-done.1
  51.0 0.0 copy-done
  51.0 0.7 copy-done.2
  51.7 32.3 %tiles.1 = (f32[16,8,128]{2,1,0:T(8,128)S(1)}, f32[16,8,128]{2,1,0:T(8,128)S(1)}) custom-call(s32[2,8]{1,0:T(2,128)S(1)} %bitcast.15, s32[1]{0:T(128)S(6)} %copy.13.count_ref, s32[3]{0:T(128)S(1)} %pad_add_fusion.base_ref, bf16[32,80,128]{2,1,0:T(8,128)(2,1)S(1)} %bitcast.12, bf16[32,80,128]{2,1,0:T(8,128)(2,1)S(1)} %bitcast.13, f32[32,64]{1,0:T(8,128)S(1)} %bitcast.14, ...), custom_call_target="tpu_custom_call" | custom-call | tf_op jit(solution)/shard_map/tiles/tiles/pallas_call | solution.py:232
  84.0 21.8 %all_to_all.21.first_ref = f32[16,8,128]{2,1,0:T(8,128)} all-to-all(f32[16,8,128]{2,1,0:T(8,128)S(1)} %get-tuple-element.10), channel_id=1, replica_groups=mesh['row'=16,'col'=16] {'col'}, dimensions={0} | all-to-all | bytes 131072 | tf_op jit(solution)/shard_map/collect/all_to_all | solution.py:304
  105.8 13.0 %all_to_all.22.second_ref = f32[16,8,128]{2,1,0:T(8,128)} all-to-all(f32[16,8,128]{2,1,0:T(8,128)S(1)} %get-tuple-element.11), channel_id=1, replica_groups=mesh['row'=16,'col'=16] {'row'}, dimensions={0} | all-to-all | bytes 131072 | tf_op jit(solution)/shard_map/collect/all_to_all | solution.py:305
  118.7 1.5 %add.5 = (f32[3,256]{1,0:T(4,128)}, f32[1,256]{1,0:T(1,128)}) custom-call(f32[16,8,128]{2,1,0:T(8,128)} %all_to_all.21.first_ref, f32[16,8,128]{2,1,0:T(8,128)} %all_to_all.22.second_ref), custom_call_target="tpu_custom_call" | custom-call | tf_op jit(solution)/shard_map/add/pallas_call | solution.py:307
  (1 shorter events, 0.0 us)
Async XLA Ops:
  21.9 29.2 %all-to-all-start.1 = ((bf16[16,2,80,128]{3,2,1,0:T(8,128)(2,1)}), bf16[16,2,80,128]{3,2,1,0:T(8,128)(2,1)S(1)}, u32[]{:S(2)}, u32[]{:S(2)}) async-start(bf16[16,2,80,128]{3,2,1,0:T(8,128)(2,1)} %get-tuple-element.9), calls=%async_computation.1 | async-start | bytes 1310720 | tf_op jit(solution)/shard_map/spread/all_to_all | solution.py:297
  31.7 0.7 copy-start.3
  32.4 18.7 %copy-start.1 = (bf16[64,64]{1,0:T(8,128)(2,1)S(1)}, bf16[64,64]{1,0:T(8,128)(2,1)}, u32[]{:S(2)}) copy-start(bf16[64,64]{1,0:T(8,128)(2,1)} %wh_ref.1) | copy-start | bytes 24580
  32.5 18.6 %copy-start = (f32[64,32]{0,1:T(8,128)S(1)}, f32[64,32]{0,1:T(8,128)}, u32[]{:S(2)}) copy-start(f32[64,32]{0,1:T(8,128)} %param.15) | copy-start | bytes 24580
  51.0 0.7 copy-start.2

commit v3 on v2

--- a/solution.py
+++ b/solution.py
@@ -12,6 +12,7 @@
 HID = 64
 NRBF = 32
 PAY = 80
+LIVE = HID + 9
 ROWS = 16
 SOFT = 0.01
 RANGE = 6.0
@@ -24,7 +25,6 @@
 
 
 def pack_kernel(fill_ref, pos_ref, feat_ref, wl_ref, wr_ref, left_ref, right_ref):
-    peers = left_ref.shape[0]
     feat = feat_ref[...]
     pos = pos_ref[...]
     high = pos.astype(BF16).astype(F32)
@@ -41,12 +41,11 @@
                 [high[:, cut], mid[:, cut], low[:, cut], live, jnp.zeros((6, CL), F32)], 0
             )
             both = jnp.concatenate([proj[:, cut], extra], 0).astype(BF16)
-            for peer in range(peers):
+            for peer in range(out_ref.shape[0]):
                 out_ref[peer, k] = both
 
 
 def unpack(block):
-    block = block.astype(F32)
     extra = block[HID:]
     pos = extra[0:3] + extra[3:6] + extra[6:9]
     return block[:HID], pos, extra[9:10]
@@ -64,18 +63,16 @@
 def tile_kernel(
     tiles_ref, count_ref, base_ref, left_ref, right_ref, wr_ref, wh_ref, wo_ref,
     first_ref, second_ref,
-    radial_ref, tangent_ref, hidden_ref, back_ref, out_ref, pick_ref, head_ref, adds_ref,
-    turned_ref, across_ref, slopes_ref, energies_ref, half1_ref, rate_ref, half2_ref, chain_ref, blocks_ref,
+    tangent_ref, hidden_ref, back_ref, out_ref, pick_ref, head_ref, adds_ref,
+    turned_ref, across_ref, slopes_ref, energies_ref, half1_ref, rate_ref, half2_ref, chain_ref, blocks_ref, swaps_ref,
 ):
     count = count_ref[0]
     wide = 2 * CL
     first_ref[...] = jnp.zeros_like(first_ref)
     second_ref[...] = jnp.zeros_like(second_ref)
     w_radial = wr_ref[...].T
-    for into_ref, scale in ((radial_ref, 0.5), (tangent_ref, -SHARP / SCALE)):
-        full = spread4(scale * w_radial)
-        high = full.astype(BF16).astype(F32)
-        into_ref[...] = jnp.concatenate([high, full - high], 1).astype(BF16)
+    radial = spread4(0.5 * w_radial)
+    tangent_ref[...] = spread4(w_radial * (-SHARP / SCALE)).astype(BF16)
     w_hidden = wh_ref[...].astype(F32)
     w_out = wo_ref[...]
     hidden_ref[...] = spread4(0.5 * w_hidden).astype(BF16)
@@ -85,9 +82,9 @@
     lane8 = lax.broadcasted_iota(jnp.int32, (8, 4 * HID), 1) // HID
     sub8 = lax.broadcasted_iota(jnp.int32, (8, 4 * HID), 0)
     out_ref[...] = jnp.where(lane8 == sub8, flat_out, 0.0).astype(BF16)
-    quad = lax.broadcasted_iota(jnp.int32, (CL, wide), 0) // 4
-    side = lax.broadcasted_iota(jnp.int32, (CL, wide), 1) // CL
-    for g in range(CL // 8):
+    quad = lax.broadcasted_iota(jnp.int32, (HID, wide), 0) // 4
+    side = lax.broadcasted_iota(jnp.int32, (HID, wide), 1) // CL
+    for g in range(HID // 8):
         pick_ref[g] = (quad == 2 * g + side).astype(F32).astype(BF16)
     centers = (
         lax.broadcasted_iota(jnp.int32, (NRBF, wide), 0).astype(F32) * (RANGE / (NRBF - 1) * SCALE)
@@ -99,16 +96,28 @@
     lane4 = lax.broadcasted_iota(jnp.int32, (HID, CL), 1) % 4
 
     def prepare(slot, carry):
-        proj_a, pos_a, live_a = unpack(left_ref[tiles_ref[0, slot]])
-        proj_b, pos_b, live_b = unpack(right_ref[tiles_ref[1, slot]])
+        first = tiles_ref[0, slot]
+        away = jnp.bitwise_xor(first // CPD, base_ref[1])
+        left = left_ref[away * CPD + first % CPD].astype(F32)
+        other = tiles_ref[1, slot]
+        beyond = jnp.bitwise_xor(other // CPD, base_ref[3])
+        right = right_ref[beyond * CPD + other % CPD].astype(F32)
+        fill_left = jnp.sum(left[LIVE : LIVE + 1]).astype(jnp.int32)
+        fill_right = jnp.sum(right[LIVE : LIVE + 1]).astype(jnp.int32)
+        swap = fill_right < fill_left
+        swaps_ref[slot] = swap.astype(jnp.int32)
+        proj_a, pos_a, live_a = unpack(jnp.where(swap, right, left))
+        proj_b, pos_b, live_b = unpack(jnp.where(swap, left, right))
         half_a = 0.5 * proj_a
         cols = jnp.concatenate([jnp.where(lane4 == q, half_a, 0.0) for q in range(4)], 0)
-        head_ref[slot] = jnp.concatenate([cols, jnp.concatenate([ident] * 4, 0)], 1).astype(BF16)
+        for half in range(2):
+            head_ref[slot, half] = jnp.concatenate(
+                [radial, cols[:, half * HID : (half + 1) * HID], jnp.concatenate([ident] * 4, 0)], 1
+            ).astype(BF16)
         adds_ref[slot] = jnp.concatenate([0.5 * proj_b] * 2, 1).astype(BF16)
         turned_ref[slot] = jnp.concatenate([pos_a, live_a, jnp.zeros((CL - 4, CL), F32)], 0).T
         across_ref[slot] = jnp.concatenate([pos_b, live_b, jnp.zeros((4, CL), F32)], 0)
-        fill_a = jnp.sum(live_a).astype(jnp.int32)
-        blocks_ref[slot] = (fill_a + ROWS - 1) // ROWS
+        blocks_ref[slot] = (jnp.minimum(fill_left, fill_right) + ROWS - 1) // ROWS
         return carry
 
     lax.fori_loop(0, count, prepare, 0)
@@ -122,7 +131,6 @@
         start = pl.multiple_of(g * ROWS, ROWS)
         mine = turned_ref[slot, pl.ds(start, ROWS), :]
         scaled = distances(mine, across_ref[slot])[1] * SCALE
-        head = jnp.concatenate([radial_ref[...], head_ref[slot]], 1)
         for e in range(ROWS // 8):
             bases = []
             rates = []
@@ -133,12 +141,11 @@
                 basis = jnp.exp2(-(offset * offset))
                 bases.append(basis.astype(BF16))
                 rates.append((basis * offset).astype(BF16))
-            tail = jnp.concatenate(
-                bases + bases + [pick_ref[g * (ROWS // 8) + e], adds_ref[slot]], 0
-            )
-            half1_ref[e] = jnp.dot(head, tail, preferred_element_type=F32)
+            block = g * (ROWS // 8) + e
+            tail = jnp.concatenate(bases + [pick_ref[block % 8], adds_ref[slot]], 0)
+            half1_ref[e] = jnp.dot(head_ref[slot, block // 8], tail, preferred_element_type=F32)
             rate_ref[e] = jnp.dot(
-                tangent_ref[...], jnp.concatenate(rates + rates, 0), preferred_element_type=F32
+                tangent_ref[...], jnp.concatenate(rates, 0), preferred_element_type=F32
             )
 
     def middle():
@@ -205,15 +212,18 @@
         weight = jnp.where(keep, slopes_ref[slot] / dist, 0.0)
         pulls = [weight * d for d in delta]
         parts = [-jnp.sum(p, 1, keepdims=True) for p in pulls]
-        parts.append(jnp.sum(jnp.where(keep, energies_ref[slot], 0.0), 1, keepdims=True))
+        kept = jnp.where(keep, energies_ref[slot], 0.0)
+        parts.append(jnp.sum(kept, 1, keepdims=True))
         side = jnp.zeros((CL, CL), F32)
         for c in range(4):
             side = jnp.where(lane == c, parts[c], side)
-        firsts = side.T[:4]
-        seconds = jnp.concatenate(
-            [jnp.sum(p, 0, keepdims=True) for p in pulls] + [jnp.zeros((1, CL), F32)], 0
-        )
-        first_ref[first // CPD] += jnp.where(row8 == first % CPD, jnp.concatenate([firsts] * 2, 0), 0.0)
+        down = side.T[:4]
+        along = jnp.concatenate([jnp.sum(p, 0, keepdims=True) for p in pulls + [kept]], 0)
+        swap = swaps_ref[slot] == 1
+        firsts = jnp.where(swap, along, down)
+        seconds = jnp.where(swap, down, along)
+        away = jnp.bitwise_xor(first // CPD, base_ref[1])
+        first_ref[away % 4 * 4 + away // 4] += jnp.where(row8 == first % CPD, jnp.concatenate([firsts] * 2, 0), 0.0)
         second_ref[other // CPD] += jnp.where(
             row8 == other % CPD, jnp.concatenate([seconds] * 2, 0), 0.0
         )
@@ -239,13 +249,12 @@
         in_specs=[smem] * 3 + [vmem] * 5,
         out_specs=(vmem, vmem),
         scratch_shapes=[
-            pltpu.VMEM((hid4, 8 * NRBF), BF16),
-            pltpu.VMEM((hid4, 8 * NRBF), BF16),
+            pltpu.VMEM((hid4, 4 * NRBF), BF16),
             pltpu.VMEM((hid4, hid4), BF16),
             pltpu.VMEM((hid4, hid4), BF16),
             pltpu.VMEM((8, hid4), BF16),
-            pltpu.VMEM((CL // 8, CL, wide), BF16),
-            pltpu.VMEM((slots, hid4, CL + HID), BF16),
+            pltpu.VMEM((HID // 8, HID, wide), BF16),
+            pltpu.VMEM((slots, 2, hid4, hid4), BF16),
             pltpu.VMEM((slots, HID, wide), BF16),
             pltpu.VMEM((slots, CL, CL), F32),
             pltpu.VMEM((slots, 8, CL), F32),
@@ -256,6 +265,7 @@
             pltpu.VMEM((groups, hid4, wide), F32),
             pltpu.VMEM((groups, hid4, wide), F32),
             pltpu.SMEM((slots,), jnp.int32),
+            pltpu.SMEM((slots,), jnp.int32),
         ],
         compiler_params=pltpu.CompilerParams(vmem_limit_bytes=48 * 1024 * 1024),
     )(
@@ -263,11 +273,13 @@
     )
 
 
-def add_kernel(first_ref, second_ref, force_ref, energy_ref):
-    total = first_ref[0]
+def across(count, step):
+    return [(i, i ^ step) for i in range(count)]
+
+
+def add_kernel(own_ref, one_ref, two_ref, three_ref, second_ref, force_ref, energy_ref):
+    total = own_ref[...] + one_ref[...] + two_ref[...] + three_ref[...]
     other = second_ref[0]
-    for peer in range(1, first_ref.shape[0]):
-        total = total + first_ref[peer]
     for peer in range(1, second_ref.shape[0]):
         other = other + second_ref[peer]
     force = total + other
@@ -286,23 +298,36 @@
         left, right = pl.pallas_call(
             pack_kernel,
             out_shape=(
-                jax.ShapeDtypeStruct((cols, CPD, PAY, CL), BF16),
-                jax.ShapeDtypeStruct((rows, CPD, PAY, CL), BF16),
+                jax.ShapeDtypeStruct((1, CPD, PAY, CL), BF16),
+                jax.ShapeDtypeStruct((1, CPD, PAY, CL), BF16),
             ),
             in_specs=[smem] + [vmem] * 4,
             out_specs=(vmem, vmem),
         )(fill, positions, features, w_left.T, w_right.T)
     with jax.named_scope("spread"):
-        left = lax.all_to_all(left, "col", 0, 0).reshape(cols * CPD, PAY, CL)
-        right = lax.all_to_all(right, "row", 0, 0).reshape(rows * CPD, PAY, CL)
-    base = jnp.stack([lax.axis_index("row") * cols * CPD, lax.axis_index("col"), jnp.int32(cols)])
+        left, right = [
+            jnp.concatenate([own] + [lax.ppermute(own, axis, across(16, k)) for k in range(1, 4)], 0)
+            for own, axis in ((left, "col"), (right, "row"))
+        ]
+        left, right = [
+            jnp.concatenate([own] + [lax.ppermute(own, axis, across(16, 4 * k)) for k in range(1, 4)], 0)
+            .reshape(16 * CPD, PAY, CL)
+            for own, axis in ((left, "col"), (right, "row"))
+        ]
+    base = jnp.stack(
+        [lax.axis_index("row") * cols * CPD, lax.axis_index("col"), jnp.int32(cols), lax.axis_index("row")]
+    )
     with jax.named_scope("tiles"):
         firsts, seconds = tile_call(
             tiles, tile_count, base, left, right, w_radial, w_hidden, w_out
         )
     with jax.named_scope("collect"):
-        firsts = lax.all_to_all(firsts, "col", 0, 0)
         seconds = lax.all_to_all(seconds, "row", 0, 0)
+        firsts = firsts.reshape(4, 4, 8, CL)
+        near = firsts[0]
+        for k in range(1, 4):
+            near = near + lax.ppermute(firsts[k], "col", across(cols, k))
+        firsts = [near[0]] + [lax.ppermute(near[k], "col", across(cols, 4 * k)) for k in range(1, 4)]
     with jax.named_scope("add"):
         force, energy = pl.pallas_call(
             add_kernel,
@@ -310,7 +335,7 @@
                 jax.ShapeDtypeStruct((3, CPD * CL), F32),
                 jax.ShapeDtypeStruct((1, CPD * CL), F32),
             ),
-        )(firsts, seconds)
+        )(*firsts, seconds)
     return force, energy.reshape(CPD * CL)
 
 

time: 121 us -> 92.9 us (0.77); the launches traced: 120 us -> 93.7 us
  blocking collectives: 53.9 us -> 0 us
  starting transfers between devices: 9.85 us -> 60.8 us
  Pallas kernels: 35.9 us -> 17 us
  waiting for transfers between devices: 17.8 us -> 11.2 us
  local copies, waits for them, and re-layouts: 1.43 us -> 3.11 us
    all_to_all x3 -> x0, blocking collectives: 53.9 us -> none  [the longest x1 21.8 us: body(): firsts = lax.all_to_all(firsts, 'col', 0, 0)]
    ppermute x0 -> x18, starting transfers between devices: none -> 52.1 us  [the longest x3 28.4 us: body(): near = near + lax.ppermute(firsts[k], 'col', across(cols, k))]
    pallas_call x1, Pallas kernels: 32.3 us -> 13.9 us  [tile_call(): pl.pallas_call(tile_kernel, name='tiles', out_shape=(jax.ShapeDtypeStruct...]
    all_to_all x1, waiting for transfers between devices: 17.8 us -> 3.4 us  [body(): seconds = lax.all_to_all(seconds, 'row', 0, 0)]
    ppermute x0 -> x18, waiting for transfers between devices: none -> 7.8 us  [the longest x6 6.06 us: body(): lax.ppermute(own, axis, across(16, 4 * k))]
  transfers between devices with their start and end apart: 1 -> 19, of which waited for: 1 -> 8; matrix products, arithmetic and copies ran while one was open for 0% -> 2% of each run, Pallas kernels for 0% -> 0%
where the time goes in v3:
time: 92.9 us; the launch traced here: 93.7 us
  starting transfers between devices  60.8 us (65%)
  Pallas kernels  17 us (18%)
  waiting for transfers between devices  11.2 us (12%)
  local copies, waits for them, and re-layouts  3.11 us (3%)
  between operations  1.5 us (2%)
    ppermute x3, starting transfers between devices, body(): near = near + lax.ppermute(firsts[k], 'col', across(cols, k))  28.4 us
    pallas_call x1, Pallas kernels, tile_call(): pl.pallas_call(tile_kernel, name='tiles', out_shape=(jax.ShapeDtypeStruct...  13.9 us
    ppermute x6, starting transfers between devices, body(): lax.ppermute(own, axis, across(16, k))  11.9 us
    all_to_all x1, starting transfers between devices, body(): seconds = lax.all_to_all(seconds, 'row', 0, 0)  8.69 us
    ppermute x6, starting transfers between devices, body(): lax.ppermute(own, axis, across(16, 4 * k))  7.95 us
    ppermute x6, waiting for transfers between devices, body(): lax.ppermute(own, axis, across(16, 4 * k))  6.06 us
    ppermute x3, starting transfers between devices, body(): lax.ppermute(near[k], 'col', across(cols, 4 * k))  3.86 us
    all_to_all x1, waiting for transfers between devices, body(): seconds = lax.all_to_all(seconds, 'row', 0, 0)  3.4 us
  transfers between devices with their start and end apart: 19, of which 8 were waited for; matrix products, arithmetic and copies ran while one was open for 2% of the time, Pallas kernels for 0%

profile of v3, /device:TPU:1, one launch (start us, length us, event | category | flops | bytes accessed | tf_op | source)
XLA Modules:
  0.0 93.7 jit_solution(3419339310620009547)
XLA Ops:
  0.6 1.6 %pack.1 = (bf16[1,2,80,128]{3,2,1,0:T(8,128)(2,1)}, bf16[1,2,80,128]{3,2,1,0:T(8,128)(2,1)}) custom-call(s32[2]{0:T(128)} %fill_ref.1, f32[3,256]{1,0:T(4,128)} %pos_ref.1, bf16[128,256]{1,0:T(8,128)(2,1)} %feat_ref.1, bf16[64,128]{1,0:T(8,128)(2,1)} %bitcast.25, bf16[64,128]{1,0:T(8,128)(2,1)} %bitcast.26), custom_call_target="tpu_custom_call" | custom-call | tf_op jit(solution)/shard_map/pack/pallas_call | solution.py:298
  2.3 3.8 %collective-permute-start.6 = (bf16[1,2,80,128]{3,2,1,0:T(8,128)(2,1)}, bf16[1,2,80,128]{3,2,1,0:T(8,128)(2,1)S(1)}, u32[]{:S(2)}, u32[]{:S(2)}) collective-permute-start(bf16[1,2,80,128]{3,2,1,0:T(8,128)(2,1)} %get-tuple-element.9), channel_id=1, source_target_pairs={{0,16},{16,0},{32,48},{48,32},{64,80},{80,64},{96,112},{112,96},{1... | collective-permute-start | bytes 122888 | tf_op jit(solution)/shard_map/spread/ppermute | solution.py:309
  6.1 5.1 %collective-permute-start.7 = (bf16[1,2,80,128]{3,2,1,0:T(8,128)(2,1)}, bf16[1,2,80,128]{3,2,1,0:T(8,128)(2,1)S(1)}, u32[]{:S(2)}, u32[]{:S(2)}) collective-permute-start(bf16[1,2,80,128]{3,2,1,0:T(8,128)(2,1)} %get-tuple-element.9), channel_id=1, source_target_pairs={{0,32},{16,48},{32,0},{48,16},{64,96},{80,112},{96,64},{112,80},{1... | collective-permute-start | bytes 122888 | tf_op jit(solution)/shard_map/spread/ppermute | solution.py:309
  11.2 1.2 %collective-permute-start = (bf16[1,2,80,128]{3,2,1,0:T(8,128)(2,1)}, bf16[1,2,80,128]{3,2,1,0:T(8,128)(2,1)S(1)}, u32[]{:S(2)}, u32[]{:S(2)}) collective-permute-start(bf16[1,2,80,128]{3,2,1,0:T(8,128)(2,1)} %get-tuple-element.8), channel_id=1, source_target_pairs={{0,1},{1,0},{2,3},{3,2},{4,5},{5,4},{6,7},{7,6},{8,9},{9,8},{10,11... | collective-permute-start | bytes 122888 | tf_op jit(solution)/shard_map/spread/ppermute | solution.py:309
  12.4 0.7 collective-permute-start.1
  13.2 0.8 constant_dynamic-update-slice_fusion.3
  14.1 0.1 pad_add_fusion.base_ref
  14.1 0.1 copy.12.wo_ref
  14.9 1.0 %collective-permute-start.2 = (bf16[1,2,80,128]{3,2,1,0:T(8,128)(2,1)S(1)}, bf16[1,2,80,128]{3,2,1,0:T(8,128)(2,1)S(1)}, u32[]{:S(2)}, u32[]{:S(2)}) collective-permute-start(bf16[1,2,80,128]{3,2,1,0:T(8,128)(2,1)S(1)} %copy-done.4), channel_id=1, source_target_pairs={{0,3},{1,2},{2,1},{3,0},{4,7},{5,6},{6,5},{7,4},{8,11},{9,10},{10,... | collective-permute-start | bytes 122888 | tf_op jit(solution)/shard_map/spread/ppermute | solution.py:309
  15.9 0.4 collective-permute-done.8
  16.4 1.3 %collective-permute-start.9 = (bf16[4,2,80,128]{3,2,1,0:T(8,128)(2,1)S(1)}, bf16[4,2,80,128]{3,2,1,0:T(8,128)(2,1)S(1)}, u32[]{:S(2)}, u32[]{:S(2)}) collective-permute-start(bf16[4,2,80,128]{3,2,1,0:T(8,128)(2,1)S(1)} %get-tuple-element.17), channel_id=1, source_target_pairs={{0,64},{16,80},{32,96},{48,112},{64,0},{80,16},{96,32},{112,48},{1... | collective-permute-start | bytes 491528 | tf_op jit(solution)/shard_map/spread/ppermute | solution.py:313
  17.7 2.5 %collective-permute-start.10 = (bf16[4,2,80,128]{3,2,1,0:T(8,128)(2,1)S(1)}, bf16[4,2,80,128]{3,2,1,0:T(8,128)(2,1)S(1)}, u32[]{:S(2)}, u32[]{:S(2)}) collective-permute-start(bf16[4,2,80,128]{3,2,1,0:T(8,128)(2,1)S(1)} %get-tuple-element.17), channel_id=1, source_target_pairs={{0,128},{16,144},{32,160},{48,176},{64,192},{80,208},{96,224},{112... | collective-permute-start | bytes 491528 | tf_op jit(solution)/shard_map/spread/ppermute | solution.py:313
  20.1 0.2 collective-permute-start.11
  20.4 1.4 %collective-permute-start.3 = (bf16[4,2,80,128]{3,2,1,0:T(8,128)(2,1)S(1)}, bf16[4,2,80,128]{3,2,1,0:T(8,128)(2,1)S(1)}, u32[]{:S(2)}, u32[]{:S(2)}) collective-permute-start(bf16[4,2,80,128]{3,2,1,0:T(8,128)(2,1)S(1)} %get-tuple-element.25), channel_id=1, source_target_pairs={{0,4},{1,5},{2,6},{3,7},{4,0},{5,1},{6,2},{7,3},{8,12},{9,13},{10,... | collective-permute-start | bytes 491528 | tf_op jit(solution)/shard_map/spread/ppermute | solution.py:313
  21.8 2.6 %collective-permute-start.4 = (bf16[4,2,80,128]{3,2,1,0:T(8,128)(2,1)S(1)}, bf16[4,2,80,128]{3,2,1,0:T(8,128)(2,1)S(1)}, u32[]{:S(2)}, u32[]{:S(2)}) collective-permute-start(bf16[4,2,80,128]{3,2,1,0:T(8,128)(2,1)S(1)} %get-tuple-element.25), channel_id=1, source_target_pairs={{0,8},{1,9},{2,10},{3,11},{4,12},{5,13},{6,14},{7,15},{8,0},{9,1},... | collective-permute-start | bytes 491528 | tf_op jit(solution)/shard_map/spread/ppermute | solution.py:313
  24.5 0.7 collective-permute-done.10
  25.2 1.1 %collective-permute-done.11 = bf16[4,2,80,128]{3,2,1,0:T(8,128)(2,1)S(1)} collective-permute-done((bf16[4,2,80,128]{3,2,1,0:T(8,128)(2,1)S(1)}, bf16[4,2,80,128]{3,2,1,0:T(8,128)(2,1)S(1)}, u32[]{:S(2)}, u32[]{:S(2)}) %collective-permute-start.11) | collective-permute-done | bytes 163872 | tf_op jit(solution)/shard_map/spread/ppermute | solution.py:313
  26.4 2.6 %collective-permute-done.4 = bf16[4,2,80,128]{3,2,1,0:T(8,128)(2,1)S(1)} collective-permute-done((bf16[4,2,80,128]{3,2,1,0:T(8,128)(2,1)S(1)}, bf16[4,2,80,128]{3,2,1,0:T(8,128)(2,1)S(1)}, u32[]{:S(2)}, u32[]{:S(2)}) %collective-permute-start.4) | collective-permute-done | bytes 163872 | tf_op jit(solution)/shard_map/spread/ppermute | solution.py:313
  29.0 1.6 %collective-permute-done.5 = bf16[4,2,80,128]{3,2,1,0:T(8,128)(2,1)S(1)} collective-permute-done((bf16[4,2,80,128]{3,2,1,0:T(8,128)(2,1)S(1)}, bf16[4,2,80,128]{3,2,1,0:T(8,128)(2,1)S(1)}, u32[]{:S(2)}, u32[]{:S(2)}) %collective-permute-start.5) | collective-permute-done | bytes 163872 | tf_op jit(solution)/shard_map/spread/ppermute | solution.py:313
  30.7 0.7 copy-done
  31.4 13.9 %tiles.1 = (f32[16,8,128]{2,1,0:T(8,128)S(1)}, f32[16,8,128]{2,1,0:T(8,128)}) custom-call(s32[2,8]{1,0:T(2,128)S(1)} %bitcast.24, s32[1]{0:T(128)S(6)} %copy.31.count_ref, s32[4]{0:T(128)S(1)} %pad_add_fusion.base_ref, bf16[32,80,128]{2,1,0:T(8,128)(2,1)S(1)} %bitcast.21, bf16[32,80,128]{2,1,0:T(8,128)(2,1)S(1)} %bitcast.22, f32[32,64]{1,0:T(8,128)S(1)} %bitcast.23, ...), custom_call_target="tpu_custom_call" | custom-call | tf_op jit(solution)/shard_map/tiles/tiles/pallas_call | solution.py:242
  45.3 9.1 %collective-permute-start.12 = (f32[4,8,128]{2,1,0:T(8,128)S(1)}, f32[4,8,128]{2,1,0:T(8,128)S(1)}, u32[]{:S(2)}, u32[]{:S(2)}) collective-permute-start(f32[4,8,128]{2,1,0:T(8,128)S(1)} %get-tuple-element.14), channel_id=1, source_target_pairs={{0,1},{1,0},{2,3},{3,2},{4,5},{5,4},{6,7},{7,6},{8,9},{9,8},{10,11... | collective-permute-start | bytes 49160 | tf_op jit(solution)/shard_map/collect/ppermute | solution.py:329
  54.4 19.3 %collective-permute-start.13 = (f32[4,8,128]{2,1,0:T(8,128)S(1)}, f32[4,8,128]{2,1,0:T(8,128)S(1)}, u32[]{:S(2)}, u32[]{:S(2)}) collective-permute-start(f32[4,8,128]{2,1,0:T(8,128)S(1)} %get-tuple-element.16), channel_id=1, source_target_pairs={{0,2},{1,3},{2,0},{3,1},{4,6},{5,7},{6,4},{7,5},{8,10},{9,11},{10,... | collective-permute-start | bytes 49160 | tf_op jit(solution)/shard_map/collect/ppermute | solution.py:329
  73.7 8.7 %all-to-all-start = ((f32[16,8,128]{2,1,0:T(8,128)}), f32[16,8,128]{2,1,0:T(8,128)S(1)}, u32[]{:S(2)}, u32[]{:S(2)}) async-start(f32[16,8,128]{2,1,0:T(8,128)} %get-tuple-element.11), calls=%async_computation | async-start | bytes 131072 | tf_op jit(solution)/shard_map/collect/all_to_all | solution.py:325
  82.5 0.6 slice_bitcast_fusion
  83.1 0.4 collective-permute-start.16
  83.4 3.5 %collective-permute-start.17 = (f32[8,128]{1,0:T(8,128)S(1)}, f32[8,128]{1,0:T(8,128)S(1)}, u32[]{:S(2)}, u32[]{:S(2)}) collective-permute-start(f32[8,128]{1,0:T(8,128)S(1)} %get-tuple-element.33), channel_id=1, source_target_pairs={{0,12},{1,13},{2,14},{3,15},{4,8},{5,9},{6,10},{7,11},{8,4},{9,5},... | collective-permute-start | bytes 12296 | tf_op jit(solution)/shard_map/collect/ppermute | solution.py:330
  86.9 0.1 collective-permute-done.16.two_ref
  87.0 1.2 %collective-permute-done.17.three_ref = f32[8,128]{1,0:T(8,128)S(1)} collective-permute-done((f32[8,128]{1,0:T(8,128)S(1)}, f32[8,128]{1,0:T(8,128)S(1)}, u32[]{:S(2)}, u32[]{:S(2)}) %collective-permute-start.17) | collective-permute-done | bytes 4128 | tf_op jit(solution)/shard_map/collect/ppermute | solution.py:330
  88.2 3.4 %all-to-all-done.second_ref = f32[16,8,128]{2,1,0:T(8,128)S(1)} async-done(((f32[16,8,128]{2,1,0:T(8,128)}), f32[16,8,128]{2,1,0:T(8,128)S(1)}, u32[]{:S(2)}, u32[]{:S(2)}) %all-to-all-start) | async-done | bytes 65568 | tf_op jit(solution)/shard_map/collect/all_to_all | solution.py:325
  91.6 0.6 copy-done.3
  92.2 1.5 %add.22 = (f32[3,256]{1,0:T(4,128)}, f32[1,256]{1,0:T(1,128)}) custom-call(f32[8,128]{1,0:T(8,128)} %get-tuple-element.36.own_ref, f32[8,128]{1,0:T(8,128)} %copy-done.5, f32[8,128]{1,0:T(8,128)} %copy-done.6, f32[8,128]{1,0:T(8,128)} %copy-done.7, f32[16,8,128]{2,1,0:T(8,128)} %copy-done.3), custom_call_target="tpu_custom_call" | custom-call | tf_op jit(solution)/shard_map/add/pallas_call | solution.py:332
  (46 shorter events, 0.4 us)
Async XLA Ops:
  2.3 12.6 %collective-permute-start.6 = (bf16[1,2,80,128]{3,2,1,0:T(8,128)(2,1)}, bf16[1,2,80,128]{3,2,1,0:T(8,128)(2,1)S(1)}, u32[]{:S(2)}, u32[]{:S(2)}) collective-permute-start(bf16[1,2,80,128]{3,2,1,0:T(8,128)(2,1)} %get-tuple-element.9), channel_id=1, source_target_pairs={{0,16},{16,0},{32,48},{48,32},{64,80},{80,64},{96,112},{112,96},{1... | collective-permute-start | bytes 122888 | tf_op jit(solution)/shard_map/spread/ppermute | solution.py:309
  6.1 9.8 %collective-permute-start.7 = (bf16[1,2,80,128]{3,2,1,0:T(8,128)(2,1)}, bf16[1,2,80,128]{3,2,1,0:T(8,128)(2,1)S(1)}, u32[]{:S(2)}, u32[]{:S(2)}) collective-permute-start(bf16[1,2,80,128]{3,2,1,0:T(8,128)(2,1)} %get-tuple-element.9), channel_id=1, source_target_pairs={{0,32},{16,48},{32,0},{48,16},{64,96},{80,112},{96,64},{112,80},{1... | collective-permute-start | bytes 122888 | tf_op jit(solution)/shard_map/spread/ppermute | solution.py:309
  11.2 5.2 %collective-permute-start.8 = (bf16[1,2,80,128]{3,2,1,0:T(8,128)(2,1)}, bf16[1,2,80,128]{3,2,1,0:T(8,128)(2,1)S(1)}, u32[]{:S(2)}, u32[]{:S(2)}) collective-permute-start(bf16[1,2,80,128]{3,2,1,0:T(8,128)(2,1)} %get-tuple-element.9), channel_id=1, source_target_pairs={{0,48},{16,32},{32,16},{48,0},{64,112},{80,96},{96,80},{112,64},{1... | collective-permute-start | bytes 122888 | tf_op jit(solution)/shard_map/spread/ppermute | solution.py:309
  11.2 8.9 %collective-permute-start = (bf16[1,2,80,128]{3,2,1,0:T(8,128)(2,1)}, bf16[1,2,80,128]{3,2,1,0:T(8,128)(2,1)S(1)}, u32[]{:S(2)}, u32[]{:S(2)}) collective-permute-start(bf16[1,2,80,128]{3,2,1,0:T(8,128)(2,1)} %get-tuple-element.8), channel_id=1, source_target_pairs={{0,1},{1,0},{2,3},{3,2},{4,5},{5,4},{6,7},{7,6},{8,9},{9,8},{10,11... | collective-permute-start | bytes 122888 | tf_op jit(solution)/shard_map/spread/ppermute | solution.py:309
  12.4 7.9 %collective-permute-start.1 = (bf16[1,2,80,128]{3,2,1,0:T(8,128)(2,1)}, bf16[1,2,80,128]{3,2,1,0:T(8,128)(2,1)S(1)}, u32[]{:S(2)}, u32[]{:S(2)}) collective-permute-start(bf16[1,2,80,128]{3,2,1,0:T(8,128)(2,1)} %get-tuple-element.8), channel_id=1, source_target_pairs={{0,2},{1,3},{2,0},{3,1},{4,6},{5,7},{6,4},{7,5},{8,10},{9,11},{10,... | collective-permute-start | bytes 122888 | tf_op jit(solution)/shard_map/spread/ppermute | solution.py:309
  13.2 0.9 copy-start.8
  14.0 0.9 copy-start.4
  14.9 5.5 %collective-permute-start.2 = (bf16[1,2,80,128]{3,2,1,0:T(8,128)(2,1)S(1)}, bf16[1,2,80,128]{3,2,1,0:T(8,128)(2,1)S(1)}, u32[]{:S(2)}, u32[]{:S(2)}) collective-permute-start(bf16[1,2,80,128]{3,2,1,0:T(8,128)(2,1)S(1)} %copy-done.4), channel_id=1, source_target_pairs={{0,3},{1,2},{2,1},{3,0},{4,7},{5,6},{6,5},{7,4},{8,11},{9,10},{10,... | collective-permute-start | bytes 122888 | tf_op jit(solution)/shard_map/spread/ppermute | solution.py:309
  16.4 8.1 %collective-permute-start.9 = (bf16[4,2,80,128]{3,2,1,0:T(8,128)(2,1)S(1)}, bf16[4,2,80,128]{3,2,1,0:T(8,128)(2,1)S(1)}, u32[]{:S(2)}, u32[]{:S(2)}) collective-permute-start(bf16[4,2,80,128]{3,2,1,0:T(8,128)(2,1)S(1)} %get-tuple-element.17), channel_id=1, source_target_pairs={{0,64},{16,80},{32,96},{48,112},{64,0},{80,16},{96,32},{112,48},{1... | collective-permute-start | bytes 491528 | tf_op jit(solution)/shard_map/spread/ppermute | solution.py:313
  17.7 7.5 %collective-permute-start.10 = (bf16[4,2,80,128]{3,2,1,0:T(8,128)(2,1)S(1)}, bf16[4,2,80,128]{3,2,1,0:T(8,128)(2,1)S(1)}, u32[]{:S(2)}, u32[]{:S(2)}) collective-permute-start(bf16[4,2,80,128]{3,2,1,0:T(8,128)(2,1)S(1)} %get-tuple-element.17), channel_id=1, source_target_pairs={{0,128},{16,144},{32,160},{48,176},{64,192},{80,208},{96,224},{112... | collective-permute-start | bytes 491528 | tf_op jit(solution)/shard_map/spread/ppermute | solution.py:313
  20.1 6.2 %collective-permute-start.11 = (bf16[4,2,80,128]{3,2,1,0:T(8,128)(2,1)S(1)}, bf16[4,2,80,128]{3,2,1,0:T(8,128)(2,1)S(1)}, u32[]{:S(2)}, u32[]{:S(2)}) collective-permute-start(bf16[4,2,80,128]{3,2,1,0:T(8,128)(2,1)S(1)} %get-tuple-element.17), channel_id=1, source_target_pairs={{0,192},{16,208},{32,224},{48,240},{64,128},{80,144},{96,160},{112... | collective-permute-start | bytes 491528 | tf_op jit(solution)/shard_map/spread/ppermute | solution.py:313
  20.4 5.9 %collective-permute-start.3 = (bf16[4,2,80,128]{3,2,1,0:T(8,128)(2,1)S(1)}, bf16[4,2,80,128]{3,2,1,0:T(8,128)(2,1)S(1)}, u32[]{:S(2)}, u32[]{:S(2)}) collective-permute-start(bf16[4,2,80,128]{3,2,1,0:T(8,128)(2,1)S(1)} %get-tuple-element.25), channel_id=1, source_target_pairs={{0,4},{1,5},{2,6},{3,7},{4,0},{5,1},{6,2},{7,3},{8,12},{9,13},{10,... | collective-permute-start | bytes 491528 | tf_op jit(solution)/shard_map/spread/ppermute | solution.py:313
  21.8 7.2 %collective-permute-start.4 = (bf16[4,2,80,128]{3,2,1,0:T(8,128)(2,1)S(1)}, bf16[4,2,80,128]{3,2,1,0:T(8,128)(2,1)S(1)}, u32[]{:S(2)}, u32[]{:S(2)}) collective-permute-start(bf16[4,2,80,128]{3,2,1,0:T(8,128)(2,1)S(1)} %get-tuple-element.25), channel_id=1, source_target_pairs={{0,8},{1,9},{2,10},{3,11},{4,12},{5,13},{6,14},{7,15},{8,0},{9,1},... | collective-permute-start | bytes 491528 | tf_op jit(solution)/shard_map/spread/ppermute | solution.py:313
  24.4 6.2 %collective-permute-start.5 = (bf16[4,2,80,128]{3,2,1,0:T(8,128)(2,1)S(1)}, bf16[4,2,80,128]{3,2,1,0:T(8,128)(2,1)S(1)}, u32[]{:S(2)}, u32[]{:S(2)}) collective-permute-start(bf16[4,2,80,128]{3,2,1,0:T(8,128)(2,1)S(1)} %get-tuple-element.25), channel_id=1, source_target_pairs={{0,12},{1,13},{2,14},{3,15},{4,8},{5,9},{6,10},{7,11},{8,4},{9,5},... | collective-permute-start | bytes 491528 | tf_op jit(solution)/shard_map/spread/ppermute | solution.py:313
  30.7 0.7 copy-start
  30.7 0.7 copy-start.1
  30.7 0.7 copy-start.2
  45.3 37.1 %collective-permute-start.12 = (f32[4,8,128]{2,1,0:T(8,128)S(1)}, f32[4,8,128]{2,1,0:T(8,128)S(1)}, u32[]{:S(2)}, u32[]{:S(2)}) collective-permute-start(f32[4,8,128]{2,1,0:T(8,128)S(1)} %get-tuple-element.14), channel_id=1, source_target_pairs={{0,1},{1,0},{2,3},{3,2},{4,5},{5,4},{6,7},{7,6},{8,9},{9,8},{10,11... | collective-permute-start | bytes 49160 | tf_op jit(solution)/shard_map/collect/ppermute | solution.py:329
  54.4 28.0 %collective-permute-start.13 = (f32[4,8,128]{2,1,0:T(8,128)S(1)}, f32[4,8,128]{2,1,0:T(8,128)S(1)}, u32[]{:S(2)}, u32[]{:S(2)}) collective-permute-start(f32[4,8,128]{2,1,0:T(8,128)S(1)} %get-tuple-element.16), channel_id=1, source_target_pairs={{0,2},{1,3},{2,0},{3,1},{4,6},{5,7},{6,4},{7,5},{8,10},{9,11},{10,... | collective-permute-start | bytes 49160 | tf_op jit(solution)/shard_map/collect/ppermute | solution.py:329
  73.7 8.8 %collective-permute-start.14 = (f32[4,8,128]{2,1,0:T(8,128)S(1)}, f32[4,8,128]{2,1,0:T(8,128)S(1)}, u32[]{:S(2)}, u32[]{:S(2)}) collective-permute-start(f32[4,8,128]{2,1,0:T(8,128)S(1)} %get-tuple-element.15), channel_id=1, source_target_pairs={{0,3},{1,2},{2,1},{3,0},{4,7},{5,6},{6,5},{7,4},{8,11},{9,10},{10,... | collective-permute-start | bytes 49160 | tf_op jit(solution)/shard_map/collect/ppermute | solution.py:329
  73.7 17.9 %all-to-all-start = ((f32[16,8,128]{2,1,0:T(8,128)}), f32[16,8,128]{2,1,0:T(8,128)S(1)}, u32[]{:S(2)}, u32[]{:S(2)}) async-start(f32[16,8,128]{2,1,0:T(8,128)} %get-tuple-element.11), calls=%async_computation | async-start | bytes 131072 | tf_op jit(solution)/shard_map/collect/all_to_all | solution.py:325
  83.1 3.9 %collective-permute-start.15 = (f32[8,128]{1,0:T(8,128)S(1)}, f32[8,128]{1,0:T(8,128)S(1)}, u32[]{:S(2)}, u32[]{:S(2)}) collective-permute-start(f32[8,128]{1,0:T(8,128)S(1)} %get-tuple-element.35), channel_id=1, source_target_pairs={{0,4},{1,5},{2,6},{3,7},{4,0},{5,1},{6,2},{7,3},{8,12},{9,13},{10,... | collective-permute-start | bytes 12296 | tf_op jit(solution)/shard_map/collect/ppermute | solution.py:330
  83.1 4.0 %collective-permute-start.16 = (f32[8,128]{1,0:T(8,128)S(1)}, f32[8,128]{1,0:T(8,128)S(1)}, u32[]{:S(2)}, u32[]{:S(2)}) collective-permute-start(f32[8,128]{1,0:T(8,128)S(1)} %get-tuple-element.34), channel_id=1, source_target_pairs={{0,8},{1,9},{2,10},{3,11},{4,12},{5,13},{6,14},{7,15},{8,0},{9,1},... | collective-permute-start | bytes 12296 | tf_op jit(solution)/shard_map/collect/ppermute | solution.py:330
  83.4 4.8 %collective-permute-start.17 = (f32[8,128]{1,0:T(8,128)S(1)}, f32[8,128]{1,0:T(8,128)S(1)}, u32[]{:S(2)}, u32[]{:S(2)}) collective-permute-start(f32[8,128]{1,0:T(8,128)S(1)} %get-tuple-element.33), channel_id=1, source_target_pairs={{0,12},{1,13},{2,14},{3,15},{4,8},{5,9},{6,10},{7,11},{8,4},{9,5},... | collective-permute-start | bytes 12296 | tf_op jit(solution)/shard_map/collect/ppermute | solution.py:330
  86.9 4.7 %copy-start.5 = (f32[8,128]{1,0:T(8,128)}, f32[8,128]{1,0:T(8,128)S(1)}, u32[]{:S(2)}) copy-start(f32[8,128]{1,0:T(8,128)S(1)} %collective-permute-done.15.one_ref) | copy-start | bytes 12292
  87.0 4.6 %copy-start.6 = (f32[8,128]{1,0:T(8,128)}, f32[8,128]{1,0:T(8,128)S(1)}, u32[]{:S(2)}) copy-start(f32[8,128]{1,0:T(8,128)S(1)} %collective-permute-done.16.two_ref) | copy-start | bytes 12292
  88.2 3.4 %copy-start.7 = (f32[8,128]{1,0:T(8,128)}, f32[8,128]{1,0:T(8,128)S(1)}, u32[]{:S(2)}) copy-start(f32[8,128]{1,0:T(8,128)S(1)} %collective-permute-done.17.three_ref) | copy-start | bytes 12292
  91.6 0.6 copy-start.3

commit v4 on v3

--- a/solution.py
+++ b/solution.py
@@ -13,7 +13,7 @@
 NRBF = 32
 PAY = 80
 LIVE = HID + 9
-ROWS = 16
+GROUPS = 4
 SOFT = 0.01
 RANGE = 6.0
 SHARP = ((NRBF - 1) / RANGE) ** 2
@@ -64,7 +64,7 @@
     tiles_ref, count_ref, base_ref, left_ref, right_ref, wr_ref, wh_ref, wo_ref,
     first_ref, second_ref,
     tangent_ref, hidden_ref, back_ref, out_ref, pick_ref, head_ref, adds_ref,
-    turned_ref, across_ref, slopes_ref, energies_ref, half1_ref, rate_ref, half2_ref, chain_ref, blocks_ref, swaps_ref,
+    turned_ref, across_ref, slopes_ref, energies_ref, half1_ref, rate_ref, half2_ref, chain_ref, source_ref, target_ref, swaps_ref,
 ):
     count = count_ref[0]
     wide = 2 * CL
@@ -72,7 +72,9 @@
     second_ref[...] = jnp.zeros_like(second_ref)
     w_radial = wr_ref[...].T
     radial = spread4(0.5 * w_radial)
-    tangent_ref[...] = spread4(w_radial * (-SHARP / SCALE)).astype(BF16)
+    tangent = spread4(w_radial * (-SHARP / SCALE))
+    high = tangent.astype(BF16).astype(F32)
+    tangent_ref[...] = jnp.concatenate([high, tangent - high], 1).astype(BF16)
     w_hidden = wh_ref[...].astype(F32)
     w_out = wo_ref[...]
     hidden_ref[...] = spread4(0.5 * w_hidden).astype(BF16)
@@ -117,39 +119,52 @@
         adds_ref[slot] = jnp.concatenate([0.5 * proj_b] * 2, 1).astype(BF16)
         turned_ref[slot] = jnp.concatenate([pos_a, live_a, jnp.zeros((CL - 4, CL), F32)], 0).T
         across_ref[slot] = jnp.concatenate([pos_b, live_b, jnp.zeros((4, CL), F32)], 0)
-        blocks_ref[slot] = (jnp.minimum(fill_left, fill_right) + ROWS - 1) // ROWS
-        return carry
-
-    lax.fori_loop(0, count, prepare, 0)
+        mine = jnp.where(slot < count, (jnp.minimum(fill_left, fill_right) + 7) // 8, 0)
+
+        def enlist(g, at):
+            source_ref[at] = slot * 16 + g
+            target_ref[at + 2 * GROUPS] = slot * 16 + g
+            return at + 1
+
+        return lax.fori_loop(0, mine, enlist, carry)
+
+    groups = lax.fori_loop(0, tiles_ref.shape[1], prepare, jnp.int32(0), unroll=2)
+    spare = slopes_ref.shape[0] - 1
+    for k in range(2 * GROUPS):
+        target_ref[k] = spare * 16
+    for k in range(3 * GROUPS):
+        source_ref[groups + k] = 0
+        target_ref[groups + 2 * GROUPS + k] = spare * 16
 
     def distances(mine, across):
         delta = [mine[:, c : c + 1] - across[c : c + 1] for c in range(3)]
         dist = jnp.sqrt(delta[0] * delta[0] + delta[1] * delta[1] + delta[2] * delta[2] + SOFT)
         return delta, dist
 
-    def enter(slot, g):
-        start = pl.multiple_of(g * ROWS, ROWS)
-        mine = turned_ref[slot, pl.ds(start, ROWS), :]
-        scaled = distances(mine, across_ref[slot])[1] * SCALE
-        for e in range(ROWS // 8):
+    def place(list_ref, at):
+        return list_ref[at] // 16, list_ref[at] % 16
+
+    def enter(n):
+        for e in range(GROUPS):
+            slot, g = place(source_ref, n * GROUPS + e)
+            mine = turned_ref[slot, pl.ds(pl.multiple_of(g * 8, 8), 8), :]
+            scaled = distances(mine, across_ref[slot])[1] * SCALE
             bases = []
             rates = []
             for q in range(4):
-                r = 8 * e + q
-                row = jnp.concatenate([scaled[r : r + 1], scaled[r + 4 : r + 5]], 1)
+                row = jnp.concatenate([scaled[q : q + 1], scaled[q + 4 : q + 5]], 1)
                 offset = row - centers
                 basis = jnp.exp2(-(offset * offset))
                 bases.append(basis.astype(BF16))
                 rates.append((basis * offset).astype(BF16))
-            block = g * (ROWS // 8) + e
-            tail = jnp.concatenate(bases + [pick_ref[block % 8], adds_ref[slot]], 0)
-            half1_ref[e] = jnp.dot(head_ref[slot, block // 8], tail, preferred_element_type=F32)
+            tail = jnp.concatenate(bases + [pick_ref[g % 8], adds_ref[slot]], 0)
+            half1_ref[e] = jnp.dot(head_ref[slot, g // 8], tail, preferred_element_type=F32)
             rate_ref[e] = jnp.dot(
-                tangent_ref[...], jnp.concatenate(rates, 0), preferred_element_type=F32
+                tangent_ref[...], jnp.concatenate(rates + rates, 0), preferred_element_type=F32
             )
 
     def middle():
-        for e in range(ROWS // 8):
+        for e in range(GROUPS):
             half1 = half1_ref[e]
             up1 = 1.0 + jnp.tanh(half1)
             silu1 = half1 * up1
@@ -157,8 +172,9 @@
             chain_ref[e] = grad1 * rate_ref[e]
             half2_ref[e] = jnp.dot(hidden_ref[...], silu1.astype(BF16), preferred_element_type=F32)
 
-    def leave(slot, g):
-        for e in range(ROWS // 8):
+    def leave(n):
+        for e in range(GROUPS):
+            slot, g = place(target_ref, n * GROUPS + e)
             half2 = half2_ref[e]
             up2 = 1.0 + jnp.tanh(half2)
             silu2 = half2 * up2
@@ -169,32 +185,17 @@
             lines = jnp.concatenate(
                 [jnp.sum(terms[q * HID : (q + 1) * HID], 0, keepdims=True) for q in range(4)], 0
             )
-            at = pl.ds(pl.multiple_of(g * ROWS + 8 * e, 8), 8)
+            at = pl.ds(pl.multiple_of(g * 8, 8), 8)
             slopes_ref[slot, at, :] = jnp.concatenate([lines[:, :CL], lines[:, CL:]], 0)
             energies_ref[slot, at, :] = jnp.concatenate([energy[:4, :CL], energy[:4, CL:]], 0)
 
-    spare = slopes_ref.shape[0] - 1
-
-    def step(carry):
-        slot, g, slot1, g1, slot2, g2, left = carry
-        leave(slot2, g2)
+    def step(n, carry):
+        leave(n)
         middle()
-        enter(slot, g)
-        last = g + 1 >= blocks_ref[slot]
-        ended = jnp.logical_and(last, slot + 1 >= count)
-        slot2, g2 = slot1, g1
-        slot1 = jnp.where(left > 2, slot, spare)
-        g1 = g
-        g = jnp.where(ended, g, jnp.where(last, 0, g + 1))
-        slot = jnp.where(jnp.logical_and(last, jnp.logical_not(ended)), slot + 1, slot)
-        return slot, g, slot1, g1, slot2, g2, left - 1
-
-    total = lax.fori_loop(0, count, lambda slot, n: n + blocks_ref[slot], 0)
-    zero = jnp.int32(0)
-    far = jnp.int32(spare)
-    lax.while_loop(
-        lambda carry: carry[6] > 0, step, (zero, zero, far, zero, far, zero, total + 2)
-    )
+        enter(n)
+        return carry
+
+    lax.fori_loop(0, (groups + GROUPS - 1) // GROUPS + 2, step, 0)
 
     sub = lax.broadcasted_iota(jnp.int32, (CL, CL), 0)
     lane = lax.broadcasted_iota(jnp.int32, (CL, CL), 1)
@@ -207,7 +208,7 @@
         mine = turned_ref[slot]
         across = across_ref[slot]
         delta, dist = distances(mine, across)
-        mask = mine[:, 3:4] * across[3:4]
+        mask = mine[:, 3:4] * across[3:4] * (slot < count).astype(F32)
         keep = jnp.logical_and(mask > 0.0, jnp.logical_or(jnp.logical_not(same), sub != lane))
         weight = jnp.where(keep, slopes_ref[slot] / dist, 0.0)
         pulls = [weight * d for d in delta]
@@ -229,14 +230,15 @@
         )
         return carry
 
-    lax.fori_loop(0, count, finish, 0)
+    lax.fori_loop(0, tiles_ref.shape[1], finish, 0, unroll=2)
 
 
 def tile_call(tiles, tile_count, base, left, right, w_radial, w_hidden, w_out):
     smem = pl.BlockSpec(memory_space=pltpu.SMEM)
     vmem = pl.BlockSpec(memory_space=pltpu.VMEM)
     slots = tiles.shape[0]
-    groups = ROWS // 8
+    groups = GROUPS
+    listed = slots * (CL // 8) + 5 * GROUPS
     hid4 = 4 * HID
     wide = 2 * CL
     return pl.pallas_call(
@@ -249,7 +251,7 @@
         in_specs=[smem] * 3 + [vmem] * 5,
         out_specs=(vmem, vmem),
         scratch_shapes=[
-            pltpu.VMEM((hid4, 4 * NRBF), BF16),
+            pltpu.VMEM((hid4, 8 * NRBF), BF16),
             pltpu.VMEM((hid4, hid4), BF16),
             pltpu.VMEM((hid4, hid4), BF16),
             pltpu.VMEM((8, hid4), BF16),
@@ -264,7 +266,8 @@
             pltpu.VMEM((groups, hid4, wide), F32),
             pltpu.VMEM((groups, hid4, wide), F32),
             pltpu.VMEM((groups, hid4, wide), F32),
-            pltpu.SMEM((slots,), jnp.int32),
+            pltpu.SMEM((listed,), jnp.int32),
+            pltpu.SMEM((listed,), jnp.int32),
             pltpu.SMEM((slots,), jnp.int32),
         ],
         compiler_params=pltpu.CompilerParams(vmem_limit_bytes=48 * 1024 * 1024),

time: 92.9 us -> 89.6 us (0.964); the launches traced: 93.7 us -> 88.7 us
  starting transfers between devices: 60.8 us -> 37 us
  Pallas kernels: 17 us -> 35.4 us
    ppermute x3, starting transfers between devices: 28.4 us -> 2.13 us  [body(): near = near + lax.ppermute(firsts[k], 'col', across(cols, k))]
    pallas_call x1, Pallas kernels: 13.9 us -> 32.3 us  [tile_call(): pl.pallas_call(tile_kernel, name='tiles', out_shape=(jax.ShapeDtypeStruct...]
    all_to_all x1, starting transfers between devices: 8.69 us -> 11.1 us  [body(): seconds = lax.all_to_all(seconds, 'row', 0, 0)]
where the time goes in v4:
time: 89.6 us; the launch traced here: 88.7 us
  starting transfers between devices  37 us (41%)
  Pallas kernels  35.4 us (40%)
  waiting for transfers between devices  11.7 us (13%)
  local copies, waits for them, and re-layouts  3.11 us (3%)
  between operations  1.51 us (2%)
    pallas_call x1, Pallas kernels, tile_call(): pl.pallas_call(tile_kernel, name='tiles', out_shape=(jax.ShapeDtypeStruct...  32.3 us
    ppermute x6, starting transfers between devices, body(): lax.ppermute(own, axis, across(16, k))  11.9 us
    all_to_all x1, starting transfers between devices, body(): seconds = lax.all_to_all(seconds, 'row', 0, 0)  11.1 us
    ppermute x6, starting transfers between devices, body(): lax.ppermute(own, axis, across(16, 4 * k))  7.95 us
    ppermute x6, waiting for transfers between devices, body(): lax.ppermute(own, axis, across(16, 4 * k))  6.06 us
    all_to_all x1, waiting for transfers between devices, body(): seconds = lax.all_to_all(seconds, 'row', 0, 0)  3.91 us
    ppermute x3, starting transfers between devices, body(): lax.ppermute(near[k], 'col', across(cols, 4 * k))  3.87 us
    unnamed x27, local copies, waits for them, and re-layouts  2.33 us
  transfers between devices with their start and end apart: 19, of which 8 were waited for; matrix products, arithmetic and copies ran while one was open for 2% of the time, Pallas kernels for 0%

profile of v4, /device:TPU:1, one launch (start us, length us, event | category | flops | bytes accessed | tf_op | source)
XLA Modules:
  0.0 88.7 jit_solution(14783428342989581157)
XLA Ops:
  0.6 1.6 %pack.1 = (bf16[1,2,80,128]{3,2,1,0:T(8,128)(2,1)}, bf16[1,2,80,128]{3,2,1,0:T(8,128)(2,1)}) custom-call(s32[2]{0:T(128)} %fill_ref.1, f32[3,256]{1,0:T(4,128)} %pos_ref.1, bf16[128,256]{1,0:T(8,128)(2,1)} %feat_ref.1, bf16[64,128]{1,0:T(8,128)(2,1)} %bitcast.25, bf16[64,128]{1,0:T(8,128)(2,1)} %bitcast.26), custom_call_target="tpu_custom_call" | custom-call | tf_op jit(solution)/shard_map/pack/pallas_call | solution.py:301
  2.3 3.8 %collective-permute-start.6 = (bf16[1,2,80,128]{3,2,1,0:T(8,128)(2,1)}, bf16[1,2,80,128]{3,2,1,0:T(8,128)(2,1)S(1)}, u32[]{:S(2)}, u32[]{:S(2)}) collective-permute-start(bf16[1,2,80,128]{3,2,1,0:T(8,128)(2,1)} %get-tuple-element.9), channel_id=1, source_target_pairs={{0,16},{16,0},{32,48},{48,32},{64,80},{80,64},{96,112},{112,96},{1... | collective-permute-start | bytes 122888 | tf_op jit(solution)/shard_map/spread/ppermute | solution.py:312
  6.1 5.1 %collective-permute-start.7 = (bf16[1,2,80,128]{3,2,1,0:T(8,128)(2,1)}, bf16[1,2,80,128]{3,2,1,0:T(8,128)(2,1)S(1)}, u32[]{:S(2)}, u32[]{:S(2)}) collective-permute-start(bf16[1,2,80,128]{3,2,1,0:T(8,128)(2,1)} %get-tuple-element.9), channel_id=1, source_target_pairs={{0,32},{16,48},{32,0},{48,16},{64,96},{80,112},{96,64},{112,80},{1... | collective-permute-start | bytes 122888 | tf_op jit(solution)/shard_map/spread/ppermute | solution.py:312
  11.2 1.2 %collective-permute-start = (bf16[1,2,80,128]{3,2,1,0:T(8,128)(2,1)}, bf16[1,2,80,128]{3,2,1,0:T(8,128)(2,1)S(1)}, u32[]{:S(2)}, u32[]{:S(2)}) collective-permute-start(bf16[1,2,80,128]{3,2,1,0:T(8,128)(2,1)} %get-tuple-element.8), channel_id=1, source_target_pairs={{0,1},{1,0},{2,3},{3,2},{4,5},{5,4},{6,7},{7,6},{8,9},{9,8},{10,11... | collective-permute-start | bytes 122888 | tf_op jit(solution)/shard_map/spread/ppermute | solution.py:312
  12.4 0.7 collective-permute-start.1
  13.2 0.8 constant_dynamic-update-slice_fusion.3
  14.1 0.1 pad_add_fusion.base_ref
  14.1 0.1 copy.12.wo_ref
  14.9 1.0 %collective-permute-start.2 = (bf16[1,2,80,128]{3,2,1,0:T(8,128)(2,1)S(1)}, bf16[1,2,80,128]{3,2,1,0:T(8,128)(2,1)S(1)}, u32[]{:S(2)}, u32[]{:S(2)}) collective-permute-start(bf16[1,2,80,128]{3,2,1,0:T(8,128)(2,1)S(1)} %copy-done.4), channel_id=1, source_target_pairs={{0,3},{1,2},{2,1},{3,0},{4,7},{5,6},{6,5},{7,4},{8,11},{9,10},{10,... | collective-permute-start | bytes 122888 | tf_op jit(solution)/shard_map/spread/ppermute | solution.py:312
  15.9 0.4 collective-permute-done.8
  16.4 1.3 %collective-permute-start.9 = (bf16[4,2,80,128]{3,2,1,0:T(8,128)(2,1)S(1)}, bf16[4,2,80,128]{3,2,1,0:T(8,128)(2,1)S(1)}, u32[]{:S(2)}, u32[]{:S(2)}) collective-permute-start(bf16[4,2,80,128]{3,2,1,0:T(8,128)(2,1)S(1)} %get-tuple-element.17), channel_id=1, source_target_pairs={{0,64},{16,80},{32,96},{48,112},{64,0},{80,16},{96,32},{112,48},{1... | collective-permute-start | bytes 491528 | tf_op jit(solution)/shard_map/spread/ppermute | solution.py:316
  17.7 2.5 %collective-permute-start.10 = (bf16[4,2,80,128]{3,2,1,0:T(8,128)(2,1)S(1)}, bf16[4,2,80,128]{3,2,1,0:T(8,128)(2,1)S(1)}, u32[]{:S(2)}, u32[]{:S(2)}) collective-permute-start(bf16[4,2,80,128]{3,2,1,0:T(8,128)(2,1)S(1)} %get-tuple-element.17), channel_id=1, source_target_pairs={{0,128},{16,144},{32,160},{48,176},{64,192},{80,208},{96,224},{112... | collective-permute-start | bytes 491528 | tf_op jit(solution)/shard_map/spread/ppermute | solution.py:316
  20.1 0.2 collective-permute-start.11
  20.4 1.4 %collective-permute-start.3 = (bf16[4,2,80,128]{3,2,1,0:T(8,128)(2,1)S(1)}, bf16[4,2,80,128]{3,2,1,0:T(8,128)(2,1)S(1)}, u32[]{:S(2)}, u32[]{:S(2)}) collective-permute-start(bf16[4,2,80,128]{3,2,1,0:T(8,128)(2,1)S(1)} %get-tuple-element.25), channel_id=1, source_target_pairs={{0,4},{1,5},{2,6},{3,7},{4,0},{5,1},{6,2},{7,3},{8,12},{9,13},{10,... | collective-permute-start | bytes 491528 | tf_op jit(solution)/shard_map/spread/ppermute | solution.py:316
  21.8 2.6 %collective-permute-start.4 = (bf16[4,2,80,128]{3,2,1,0:T(8,128)(2,1)S(1)}, bf16[4,2,80,128]{3,2,1,0:T(8,128)(2,1)S(1)}, u32[]{:S(2)}, u32[]{:S(2)}) collective-permute-start(bf16[4,2,80,128]{3,2,1,0:T(8,128)(2,1)S(1)} %get-tuple-element.25), channel_id=1, source_target_pairs={{0,8},{1,9},{2,10},{3,11},{4,12},{5,13},{6,14},{7,15},{8,0},{9,1},... | collective-permute-start | bytes 491528 | tf_op jit(solution)/shard_map/spread/ppermute | solution.py:316
  24.5 0.7 collective-permute-done.10
  25.2 1.1 %collective-permute-done.11 = bf16[4,2,80,128]{3,2,1,0:T(8,128)(2,1)S(1)} collective-permute-done((bf16[4,2,80,128]{3,2,1,0:T(8,128)(2,1)S(1)}, bf16[4,2,80,128]{3,2,1,0:T(8,128)(2,1)S(1)}, u32[]{:S(2)}, u32[]{:S(2)}) %collective-permute-start.11) | collective-permute-done | bytes 163872 | tf_op jit(solution)/shard_map/spread/ppermute | solution.py:316
  26.4 2.6 %collective-permute-done.4 = bf16[4,2,80,128]{3,2,1,0:T(8,128)(2,1)S(1)} collective-permute-done((bf16[4,2,80,128]{3,2,1,0:T(8,128)(2,1)S(1)}, bf16[4,2,80,128]{3,2,1,0:T(8,128)(2,1)S(1)}, u32[]{:S(2)}, u32[]{:S(2)}) %collective-permute-start.4) | collective-permute-done | bytes 163872 | tf_op jit(solution)/shard_map/spread/ppermute | solution.py:316
  29.0 1.6 %collective-permute-done.5 = bf16[4,2,80,128]{3,2,1,0:T(8,128)(2,1)S(1)} collective-permute-done((bf16[4,2,80,128]{3,2,1,0:T(8,128)(2,1)S(1)}, bf16[4,2,80,128]{3,2,1,0:T(8,128)(2,1)S(1)}, u32[]{:S(2)}, u32[]{:S(2)}) %collective-permute-start.5) | collective-permute-done | bytes 163872 | tf_op jit(solution)/shard_map/spread/ppermute | solution.py:316
  30.7 0.7 copy-done
  31.4 32.3 %tiles.1 = (f32[16,8,128]{2,1,0:T(8,128)S(1)}, f32[16,8,128]{2,1,0:T(8,128)}) custom-call(s32[2,8]{1,0:T(2,128)S(1)} %bitcast.24, s32[1]{0:T(128)S(6)} %copy.31.count_ref, s32[4]{0:T(128)S(1)} %pad_add_fusion.base_ref, bf16[32,80,128]{2,1,0:T(8,128)(2,1)S(1)} %bitcast.21, bf16[32,80,128]{2,1,0:T(8,128)(2,1)S(1)} %bitcast.22, f32[32,64]{1,0:T(8,128)S(1)} %bitcast.23, ...), custom_call_target="tpu_custom_call" | custom-call | tf_op jit(solution)/shard_map/tiles/tiles/pallas_call | solution.py:244
  63.7 0.1 collective-permute-start.13
  63.8 2.0 %collective-permute-start.14 = (f32[4,8,128]{2,1,0:T(8,128)S(1)}, f32[4,8,128]{2,1,0:T(8,128)S(1)}, u32[]{:S(2)}, u32[]{:S(2)}) collective-permute-start(f32[4,8,128]{2,1,0:T(8,128)S(1)} %get-tuple-element.15), channel_id=1, source_target_pairs={{0,3},{1,2},{2,1},{3,0},{4,7},{5,6},{6,5},{7,4},{8,11},{9,10},{10,... | collective-permute-start | bytes 49160 | tf_op jit(solution)/shard_map/collect/ppermute | solution.py:332
  65.8 11.1 %all-to-all-start = ((f32[16,8,128]{2,1,0:T(8,128)}), f32[16,8,128]{2,1,0:T(8,128)S(1)}, u32[]{:S(2)}, u32[]{:S(2)}) async-start(f32[16,8,128]{2,1,0:T(8,128)} %get-tuple-element.11), calls=%async_computation | async-start | bytes 131072 | tf_op jit(solution)/shard_map/collect/all_to_all | solution.py:328
  77.0 0.6 slice_bitcast_fusion
  77.6 1.0 %collective-permute-start.16 = (f32[8,128]{1,0:T(8,128)S(1)}, f32[8,128]{1,0:T(8,128)S(1)}, u32[]{:S(2)}, u32[]{:S(2)}) collective-permute-start(f32[8,128]{1,0:T(8,128)S(1)} %get-tuple-element.34), channel_id=1, source_target_pairs={{0,8},{1,9},{2,10},{3,11},{4,12},{5,13},{6,14},{7,15},{8,0},{9,1},... | collective-permute-start | bytes 12296 | tf_op jit(solution)/shard_map/collect/ppermute | solution.py:333
  78.6 2.8 %collective-permute-start.17 = (f32[8,128]{1,0:T(8,128)S(1)}, f32[8,128]{1,0:T(8,128)S(1)}, u32[]{:S(2)}, u32[]{:S(2)}) collective-permute-start(f32[8,128]{1,0:T(8,128)S(1)} %get-tuple-element.33), channel_id=1, source_target_pairs={{0,12},{1,13},{2,14},{3,15},{4,8},{5,9},{6,10},{7,11},{8,4},{9,5},... | collective-permute-start | bytes 12296 | tf_op jit(solution)/shard_map/collect/ppermute | solution.py:333
  81.5 0.4 collective-permute-done.16.two_ref
  81.8 0.9 collective-permute-done.17.three_ref
  82.7 3.9 %all-to-all-done.second_ref = f32[16,8,128]{2,1,0:T(8,128)S(1)} async-done(((f32[16,8,128]{2,1,0:T(8,128)}), f32[16,8,128]{2,1,0:T(8,128)S(1)}, u32[]{:S(2)}, u32[]{:S(2)}) %all-to-all-start) | async-done | bytes 65568 | tf_op jit(solution)/shard_map/collect/all_to_all | solution.py:328
  86.7 0.6 copy-done.3
  87.3 1.5 %add.22 = (f32[3,256]{1,0:T(4,128)}, f32[1,256]{1,0:T(1,128)}) custom-call(f32[8,128]{1,0:T(8,128)} %get-tuple-element.36.own_ref, f32[8,128]{1,0:T(8,128)} %copy-done.5, f32[8,128]{1,0:T(8,128)} %copy-done.6, f32[8,128]{1,0:T(8,128)} %copy-done.7, f32[16,8,128]{2,1,0:T(8,128)} %copy-done.3), custom_call_target="tpu_custom_call" | custom-call | tf_op jit(solution)/shard_map/add/pallas_call | solution.py:335
  (46 shorter events, 0.4 us)
Async XLA Ops:
  2.3 12.6 %collective-permute-start.6 = (bf16[1,2,80,128]{3,2,1,0:T(8,128)(2,1)}, bf16[1,2,80,128]{3,2,1,0:T(8,128)(2,1)S(1)}, u32[]{:S(2)}, u32[]{:S(2)}) collective-permute-start(bf16[1,2,80,128]{3,2,1,0:T(8,128)(2,1)} %get-tuple-element.9), channel_id=1, source_target_pairs={{0,16},{16,0},{32,48},{48,32},{64,80},{80,64},{96,112},{112,96},{1... | collective-permute-start | bytes 122888 | tf_op jit(solution)/shard_map/spread/ppermute | solution.py:312
  6.1 9.8 %collective-permute-start.7 = (bf16[1,2,80,128]{3,2,1,0:T(8,128)(2,1)}, bf16[1,2,80,128]{3,2,1,0:T(8,128)(2,1)S(1)}, u32[]{:S(2)}, u32[]{:S(2)}) collective-permute-start(bf16[1,2,80,128]{3,2,1,0:T(8,128)(2,1)} %get-tuple-element.9), channel_id=1, source_target_pairs={{0,32},{16,48},{32,0},{48,16},{64,96},{80,112},{96,64},{112,80},{1... | collective-permute-start | bytes 122888 | tf_op jit(solution)/shard_map/spread/ppermute | solution.py:312
  11.2 5.2 %collective-permute-start.8 = (bf16[1,2,80,128]{3,2,1,0:T(8,128)(2,1)}, bf16[1,2,80,128]{3,2,1,0:T(8,128)(2,1)S(1)}, u32[]{:S(2)}, u32[]{:S(2)}) collective-permute-start(bf16[1,2,80,128]{3,2,1,0:T(8,128)(2,1)} %get-tuple-element.9), channel_id=1, source_target_pairs={{0,48},{16,32},{32,16},{48,0},{64,112},{80,96},{96,80},{112,64},{1... | collective-permute-start | bytes 122888 | tf_op jit(solution)/shard_map/spread/ppermute | solution.py:312
  11.2 8.9 %collective-permute-start = (bf16[1,2,80,128]{3,2,1,0:T(8,128)(2,1)}, bf16[1,2,80,128]{3,2,1,0:T(8,128)(2,1)S(1)}, u32[]{:S(2)}, u32[]{:S(2)}) collective-permute-start(bf16[1,2,80,128]{3,2,1,0:T(8,128)(2,1)} %get-tuple-element.8), channel_id=1, source_target_pairs={{0,1},{1,0},{2,3},{3,2},{4,5},{5,4},{6,7},{7,6},{8,9},{9,8},{10,11... | collective-permute-start | bytes 122888 | tf_op jit(solution)/shard_map/spread/ppermute | solution.py:312
  12.4 7.9 %collective-permute-start.1 = (bf16[1,2,80,128]{3,2,1,0:T(8,128)(2,1)}, bf16[1,2,80,128]{3,2,1,0:T(8,128)(2,1)S(1)}, u32[]{:S(2)}, u32[]{:S(2)}) collective-permute-start(bf16[1,2,80,128]{3,2,1,0:T(8,128)(2,1)} %get-tuple-element.8), channel_id=1, source_target_pairs={{0,2},{1,3},{2,0},{3,1},{4,6},{5,7},{6,4},{7,5},{8,10},{9,11},{10,... | collective-permute-start | bytes 122888 | tf_op jit(solution)/shard_map/spread/ppermute | solution.py:312
  13.2 0.9 copy-start.8
  14.0 0.9 copy-start.4
  14.9 5.5 %collective-permute-start.2 = (bf16[1,2,80,128]{3,2,1,0:T(8,128)(2,1)S(1)}, bf16[1,2,80,128]{3,2,1,0:T(8,128)(2,1)S(1)}, u32[]{:S(2)}, u32[]{:S(2)}) collective-permute-start(bf16[1,2,80,128]{3,2,1,0:T(8,128)(2,1)S(1)} %copy-done.4), channel_id=1, source_target_pairs={{0,3},{1,2},{2,1},{3,0},{4,7},{5,6},{6,5},{7,4},{8,11},{9,10},{10,... | collective-permute-start | bytes 122888 | tf_op jit(solution)/shard_map/spread/ppermute | solution.py:312
  16.4 8.1 %collective-permute-start.9 = (bf16[4,2,80,128]{3,2,1,0:T(8,128)(2,1)S(1)}, bf16[4,2,80,128]{3,2,1,0:T(8,128)(2,1)S(1)}, u32[]{:S(2)}, u32[]{:S(2)}) collective-permute-start(bf16[4,2,80,128]{3,2,1,0:T(8,128)(2,1)S(1)} %get-tuple-element.17), channel_id=1, source_target_pairs={{0,64},{16,80},{32,96},{48,112},{64,0},{80,16},{96,32},{112,48},{1... | collective-permute-start | bytes 491528 | tf_op jit(solution)/shard_map/spread/ppermute | solution.py:316
  17.7 7.5 %collective-permute-start.10 = (bf16[4,2,80,128]{3,2,1,0:T(8,128)(2,1)S(1)}, bf16[4,2,80,128]{3,2,1,0:T(8,128)(2,1)S(1)}, u32[]{:S(2)}, u32[]{:S(2)}) collective-permute-start(bf16[4,2,80,128]{3,2,1,0:T(8,128)(2,1)S(1)} %get-tuple-element.17), channel_id=1, source_target_pairs={{0,128},{16,144},{32,160},{48,176},{64,192},{80,208},{96,224},{112... | collective-permute-start | bytes 491528 | tf_op jit(solution)/shard_map/spread/ppermute | solution.py:316
  20.1 6.2 %collective-permute-start.11 = (bf16[4,2,80,128]{3,2,1,0:T(8,128)(2,1)S(1)}, bf16[4,2,80,128]{3,2,1,0:T(8,128)(2,1)S(1)}, u32[]{:S(2)}, u32[]{:S(2)}) collective-permute-start(bf16[4,2,80,128]{3,2,1,0:T(8,128)(2,1)S(1)} %get-tuple-element.17), channel_id=1, source_target_pairs={{0,192},{16,208},{32,224},{48,240},{64,128},{80,144},{96,160},{112... | collective-permute-start | bytes 491528 | tf_op jit(solution)/shard_map/spread/ppermute | solution.py:316
  20.4 5.9 %collective-permute-start.3 = (bf16[4,2,80,128]{3,2,1,0:T(8,128)(2,1)S(1)}, bf16[4,2,80,128]{3,2,1,0:T(8,128)(2,1)S(1)}, u32[]{:S(2)}, u32[]{:S(2)}) collective-permute-start(bf16[4,2,80,128]{3,2,1,0:T(8,128)(2,1)S(1)} %get-tuple-element.25), channel_id=1, source_target_pairs={{0,4},{1,5},{2,6},{3,7},{4,0},{5,1},{6,2},{7,3},{8,12},{9,13},{10,... | collective-permute-start | bytes 491528 | tf_op jit(solution)/shard_map/spread/ppermute | solution.py:316
  21.8 7.2 %collective-permute-start.4 = (bf16[4,2,80,128]{3,2,1,0:T(8,128)(2,1)S(1)}, bf16[4,2,80,128]{3,2,1,0:T(8,128)(2,1)S(1)}, u32[]{:S(2)}, u32[]{:S(2)}) collective-permute-start(bf16[4,2,80,128]{3,2,1,0:T(8,128)(2,1)S(1)} %get-tuple-element.25), channel_id=1, source_target_pairs={{0,8},{1,9},{2,10},{3,11},{4,12},{5,13},{6,14},{7,15},{8,0},{9,1},... | collective-permute-start | bytes 491528 | tf_op jit(solution)/shard_map/spread/ppermute | solution.py:316
  24.4 6.2 %collective-permute-start.5 = (bf16[4,2,80,128]{3,2,1,0:T(8,128)(2,1)S(1)}, bf16[4,2,80,128]{3,2,1,0:T(8,128)(2,1)S(1)}, u32[]{:S(2)}, u32[]{:S(2)}) collective-permute-start(bf16[4,2,80,128]{3,2,1,0:T(8,128)(2,1)S(1)} %get-tuple-element.25), channel_id=1, source_target_pairs={{0,12},{1,13},{2,14},{3,15},{4,8},{5,9},{6,10},{7,11},{8,4},{9,5},... | collective-permute-start | bytes 491528 | tf_op jit(solution)/shard_map/spread/ppermute | solution.py:316
  30.7 0.7 copy-start
  30.7 0.7 copy-start.1
  30.7 0.7 copy-start.2
  63.7 13.3 %collective-permute-start.12 = (f32[4,8,128]{2,1,0:T(8,128)S(1)}, f32[4,8,128]{2,1,0:T(8,128)S(1)}, u32[]{:S(2)}, u32[]{:S(2)}) collective-permute-start(f32[4,8,128]{2,1,0:T(8,128)S(1)} %get-tuple-element.14), channel_id=1, source_target_pairs={{0,1},{1,0},{2,3},{3,2},{4,5},{5,4},{6,7},{7,6},{8,9},{9,8},{10,11... | collective-permute-start | bytes 49160 | tf_op jit(solution)/shard_map/collect/ppermute | solution.py:332
  63.7 13.3 %collective-permute-start.13 = (f32[4,8,128]{2,1,0:T(8,128)S(1)}, f32[4,8,128]{2,1,0:T(8,128)S(1)}, u32[]{:S(2)}, u32[]{:S(2)}) collective-permute-start(f32[4,8,128]{2,1,0:T(8,128)S(1)} %get-tuple-element.16), channel_id=1, source_target_pairs={{0,2},{1,3},{2,0},{3,1},{4,6},{5,7},{6,4},{7,5},{8,10},{9,11},{10,... | collective-permute-start | bytes 49160 | tf_op jit(solution)/shard_map/collect/ppermute | solution.py:332
  63.8 13.2 %collective-permute-start.14 = (f32[4,8,128]{2,1,0:T(8,128)S(1)}, f32[4,8,128]{2,1,0:T(8,128)S(1)}, u32[]{:S(2)}, u32[]{:S(2)}) collective-permute-start(f32[4,8,128]{2,1,0:T(8,128)S(1)} %get-tuple-element.15), channel_id=1, source_target_pairs={{0,3},{1,2},{2,1},{3,0},{4,7},{5,6},{6,5},{7,4},{8,11},{9,10},{10,... | collective-permute-start | bytes 49160 | tf_op jit(solution)/shard_map/collect/ppermute | solution.py:332
  65.8 20.8 %all-to-all-start = ((f32[16,8,128]{2,1,0:T(8,128)}), f32[16,8,128]{2,1,0:T(8,128)S(1)}, u32[]{:S(2)}, u32[]{:S(2)}) async-start(f32[16,8,128]{2,1,0:T(8,128)} %get-tuple-element.11), calls=%async_computation | async-start | bytes 131072 | tf_op jit(solution)/shard_map/collect/all_to_all | solution.py:328
  77.6 3.9 %collective-permute-start.15 = (f32[8,128]{1,0:T(8,128)S(1)}, f32[8,128]{1,0:T(8,128)S(1)}, u32[]{:S(2)}, u32[]{:S(2)}) collective-permute-start(f32[8,128]{1,0:T(8,128)S(1)} %get-tuple-element.35), channel_id=1, source_target_pairs={{0,4},{1,5},{2,6},{3,7},{4,0},{5,1},{6,2},{7,3},{8,12},{9,13},{10,... | collective-permute-start | bytes 12296 | tf_op jit(solution)/shard_map/collect/ppermute | solution.py:333
  77.6 4.3 %collective-permute-start.16 = (f32[8,128]{1,0:T(8,128)S(1)}, f32[8,128]{1,0:T(8,128)S(1)}, u32[]{:S(2)}, u32[]{:S(2)}) collective-permute-start(f32[8,128]{1,0:T(8,128)S(1)} %get-tuple-element.34), channel_id=1, source_target_pairs={{0,8},{1,9},{2,10},{3,11},{4,12},{5,13},{6,14},{7,15},{8,0},{9,1},... | collective-permute-start | bytes 12296 | tf_op jit(solution)/shard_map/collect/ppermute | solution.py:333
  78.6 4.1 %collective-permute-start.17 = (f32[8,128]{1,0:T(8,128)S(1)}, f32[8,128]{1,0:T(8,128)S(1)}, u32[]{:S(2)}, u32[]{:S(2)}) collective-permute-start(f32[8,128]{1,0:T(8,128)S(1)} %get-tuple-element.33), channel_id=1, source_target_pairs={{0,12},{1,13},{2,14},{3,15},{4,8},{5,9},{6,10},{7,11},{8,4},{9,5},... | collective-permute-start | bytes 12296 | tf_op jit(solution)/shard_map/collect/ppermute | solution.py:333
  81.4 5.2 %copy-start.5 = (f32[8,128]{1,0:T(8,128)}, f32[8,128]{1,0:T(8,128)S(1)}, u32[]{:S(2)}) copy-start(f32[8,128]{1,0:T(8,128)S(1)} %collective-permute-done.15.one_ref) | copy-start | bytes 12292
  81.8 4.8 %copy-start.6 = (f32[8,128]{1,0:T(8,128)}, f32[8,128]{1,0:T(8,128)S(1)}, u32[]{:S(2)}) copy-start(f32[8,128]{1,0:T(8,128)S(1)} %collective-permute-done.16.two_ref) | copy-start | bytes 12292
  82.7 3.9 %copy-start.7 = (f32[8,128]{1,0:T(8,128)}, f32[8,128]{1,0:T(8,128)S(1)}, u32[]{:S(2)}) copy-start(f32[8,128]{1,0:T(8,128)S(1)} %collective-permute-done.17.three_ref) | copy-start | bytes 12292
  86.6 0.6 copy-start.3

commit v5 on v4

--- a/solution.py
+++ b/solution.py
@@ -195,7 +195,14 @@
         enter(n)
         return carry
 
-    lax.fori_loop(0, (groups + GROUPS - 1) // GROUPS + 2, step, 0)
+    steps = (groups + GROUPS - 1) // GROUPS
+    enter(0)
+    middle()
+    enter(1)
+    lax.fori_loop(2, steps, step, 0)
+    leave(steps)
+    middle()
+    leave(steps + 1)
 
     sub = lax.broadcasted_iota(jnp.int32, (CL, CL), 0)
     lane = lax.broadcasted_iota(jnp.int32, (CL, CL), 1)
@@ -212,13 +219,10 @@
         keep = jnp.logical_and(mask > 0.0, jnp.logical_or(jnp.logical_not(same), sub != lane))
         weight = jnp.where(keep, slopes_ref[slot] / dist, 0.0)
         pulls = [weight * d for d in delta]
-        parts = [-jnp.sum(p, 1, keepdims=True) for p in pulls]
         kept = jnp.where(keep, energies_ref[slot], 0.0)
-        parts.append(jnp.sum(kept, 1, keepdims=True))
-        side = jnp.zeros((CL, CL), F32)
-        for c in range(4):
-            side = jnp.where(lane == c, parts[c], side)
-        down = side.T[:4]
+        down = jnp.concatenate(
+            [-jnp.sum(p.T, 0, keepdims=True) for p in pulls] + [jnp.sum(kept.T, 0, keepdims=True)], 0
+        )
         along = jnp.concatenate([jnp.sum(p, 0, keepdims=True) for p in pulls + [kept]], 0)
         swap = swaps_ref[slot] == 1
         firsts = jnp.where(swap, along, down)
@@ -230,7 +234,8 @@
         )
         return carry
 
-    lax.fori_loop(0, tiles_ref.shape[1], finish, 0, unroll=2)
+    for slot in range(tiles_ref.shape[1]):
+        finish(slot, 0)
 
 
 def tile_call(tiles, tile_count, base, left, right, w_radial, w_hidden, w_out):

time: 89.6 us -> 86 us (0.960)
  Pallas kernels: 35.4 us -> 31.1 us
  starting transfers between devices: 37 us -> 39.1 us
  waiting for transfers between devices: 11.7 us -> 10.5 us
    pallas_call x1, Pallas kernels: 32.3 us -> 28 us  [tile_call(): pl.pallas_call(tile_kernel, name='tiles', out_shape=(jax.ShapeDtypeStruct...]
    all_to_all x1, waiting for transfers between devices: 3.91 us -> 0.01 us  [body(): seconds = lax.all_to_all(seconds, 'row', 0, 0)]
    ppermute x3, waiting for transfers between devices: 1.28 us -> 3.95 us  [body(): lax.ppermute(near[k], 'col', across(cols, 4 * k))]
    ppermute x3, starting transfers between devices: 3.87 us -> 5.85 us  [body(): lax.ppermute(near[k], 'col', across(cols, 4 * k))]
  transfers between devices with their start and end apart: 19 -> 19, of which waited for: 8 -> 7; matrix products, arithmetic and copies ran while one was open for 2% -> 2% of each run, Pallas kernels for 0% -> 0%
where the time goes in v5:
time: 86 us; the launch traced here: 85.3 us
  starting transfers between devices  39.1 us (45%)
  Pallas kernels  31.1 us (36%)
  waiting for transfers between devices  10.5 us (12%)
  local copies, waits for them, and re-layouts  3.1 us (4%)
  between operations  1.51 us (2%)
    pallas_call x1, Pallas kernels, tile_call(): pl.pallas_call(tile_kernel, name='tiles', out_shape=(jax.ShapeDtypeStruct...  28 us
    ppermute x6, starting transfers between devices, body(): lax.ppermute(own, axis, across(16, k))  11.9 us
    all_to_all x1, starting transfers between devices, body(): seconds = lax.all_to_all(seconds, 'row', 0, 0)  11.1 us
    ppermute x6, starting transfers between devices, body(): lax.ppermute(own, axis, across(16, 4 * k))  7.95 us
    ppermute x6, waiting for transfers between devices, body(): lax.ppermute(own, axis, across(16, 4 * k))  6.06 us
    ppermute x3, starting transfers between devices, body(): lax.ppermute(near[k], 'col', across(cols, 4 * k))  5.85 us
    ppermute x3, waiting for transfers between devices, body(): lax.ppermute(near[k], 'col', across(cols, 4 * k))  3.95 us
    unnamed x27, local copies, waits for them, and re-layouts  2.32 us
  transfers between devices with their start and end apart: 19, of which 7 were waited for; matrix products, arithmetic and copies ran while one was open for 2% of the time, Pallas kernels for 0%

profile of v5, /device:TPU:1, one launch (start us, length us, event | category | flops | bytes accessed | tf_op | source)
XLA Modules:
  0.0 85.3 jit_solution(13040190127413628306)
XLA Ops:
  0.6 1.6 %pack.1 = (bf16[1,2,80,128]{3,2,1,0:T(8,128)(2,1)}, bf16[1,2,80,128]{3,2,1,0:T(8,128)(2,1)}) custom-call(s32[2]{0:T(128)} %fill_ref.1, f32[3,256]{1,0:T(4,128)} %pos_ref.1, bf16[128,256]{1,0:T(8,128)(2,1)} %feat_ref.1, bf16[64,128]{1,0:T(8,128)(2,1)} %bitcast.25, bf16[64,128]{1,0:T(8,128)(2,1)} %bitcast.26), custom_call_target="tpu_custom_call" | custom-call | tf_op jit(solution)/shard_map/pack/pallas_call | solution.py:306
  2.3 3.8 %collective-permute-start.6 = (bf16[1,2,80,128]{3,2,1,0:T(8,128)(2,1)}, bf16[1,2,80,128]{3,2,1,0:T(8,128)(2,1)S(1)}, u32[]{:S(2)}, u32[]{:S(2)}) collective-permute-start(bf16[1,2,80,128]{3,2,1,0:T(8,128)(2,1)} %get-tuple-element.9), channel_id=1, source_target_pairs={{0,16},{16,0},{32,48},{48,32},{64,80},{80,64},{96,112},{112,96},{1... | collective-permute-start | bytes 122888 | tf_op jit(solution)/shard_map/spread/ppermute | solution.py:317
  6.1 5.1 %collective-permute-start.7 = (bf16[1,2,80,128]{3,2,1,0:T(8,128)(2,1)}, bf16[1,2,80,128]{3,2,1,0:T(8,128)(2,1)S(1)}, u32[]{:S(2)}, u32[]{:S(2)}) collective-permute-start(bf16[1,2,80,128]{3,2,1,0:T(8,128)(2,1)} %get-tuple-element.9), channel_id=1, source_target_pairs={{0,32},{16,48},{32,0},{48,16},{64,96},{80,112},{96,64},{112,80},{1... | collective-permute-start | bytes 122888 | tf_op jit(solution)/shard_map/spread/ppermute | solution.py:317
  11.2 1.2 %collective-permute-start = (bf16[1,2,80,128]{3,2,1,0:T(8,128)(2,1)}, bf16[1,2,80,128]{3,2,1,0:T(8,128)(2,1)S(1)}, u32[]{:S(2)}, u32[]{:S(2)}) collective-permute-start(bf16[1,2,80,128]{3,2,1,0:T(8,128)(2,1)} %get-tuple-element.8), channel_id=1, source_target_pairs={{0,1},{1,0},{2,3},{3,2},{4,5},{5,4},{6,7},{7,6},{8,9},{9,8},{10,11... | collective-permute-start | bytes 122888 | tf_op jit(solution)/shard_map/spread/ppermute | solution.py:317
  12.4 0.7 collective-permute-start.1
  13.2 0.8 constant_dynamic-update-slice_fusion.3
  14.1 0.1 pad_add_fusion.base_ref
  14.1 0.1 copy.12.wo_ref
  14.9 1.0 %collective-permute-start.2 = (bf16[1,2,80,128]{3,2,1,0:T(8,128)(2,1)S(1)}, bf16[1,2,80,128]{3,2,1,0:T(8,128)(2,1)S(1)}, u32[]{:S(2)}, u32[]{:S(2)}) collective-permute-start(bf16[1,2,80,128]{3,2,1,0:T(8,128)(2,1)S(1)} %copy-done.4), channel_id=1, source_target_pairs={{0,3},{1,2},{2,1},{3,0},{4,7},{5,6},{6,5},{7,4},{8,11},{9,10},{10,... | collective-permute-start | bytes 122888 | tf_op jit(solution)/shard_map/spread/ppermute | solution.py:317
  15.9 0.4 collective-permute-done.8
  16.4 1.3 %collective-permute-start.9 = (bf16[4,2,80,128]{3,2,1,0:T(8,128)(2,1)S(1)}, bf16[4,2,80,128]{3,2,1,0:T(8,128)(2,1)S(1)}, u32[]{:S(2)}, u32[]{:S(2)}) collective-permute-start(bf16[4,2,80,128]{3,2,1,0:T(8,128)(2,1)S(1)} %get-tuple-element.17), channel_id=1, source_target_pairs={{0,64},{16,80},{32,96},{48,112},{64,0},{80,16},{96,32},{112,48},{1... | collective-permute-start | bytes 491528 | tf_op jit(solution)/shard_map/spread/ppermute | solution.py:321
  17.7 2.4 %collective-permute-start.10 = (bf16[4,2,80,128]{3,2,1,0:T(8,128)(2,1)S(1)}, bf16[4,2,80,128]{3,2,1,0:T(8,128)(2,1)S(1)}, u32[]{:S(2)}, u32[]{:S(2)}) collective-permute-start(bf16[4,2,80,128]{3,2,1,0:T(8,128)(2,1)S(1)} %get-tuple-element.17), channel_id=1, source_target_pairs={{0,128},{16,144},{32,160},{48,176},{64,192},{80,208},{96,224},{112... | collective-permute-start | bytes 491528 | tf_op jit(solution)/shard_map/spread/ppermute | solution.py:321
  20.1 0.2 collective-permute-start.11
  20.4 1.4 %collective-permute-start.3 = (bf16[4,2,80,128]{3,2,1,0:T(8,128)(2,1)S(1)}, bf16[4,2,80,128]{3,2,1,0:T(8,128)(2,1)S(1)}, u32[]{:S(2)}, u32[]{:S(2)}) collective-permute-start(bf16[4,2,80,128]{3,2,1,0:T(8,128)(2,1)S(1)} %get-tuple-element.25), channel_id=1, source_target_pairs={{0,4},{1,5},{2,6},{3,7},{4,0},{5,1},{6,2},{7,3},{8,12},{9,13},{10,... | collective-permute-start | bytes 491528 | tf_op jit(solution)/shard_map/spread/ppermute | solution.py:321
  21.8 2.6 %collective-permute-start.4 = (bf16[4,2,80,128]{3,2,1,0:T(8,128)(2,1)S(1)}, bf16[4,2,80,128]{3,2,1,0:T(8,128)(2,1)S(1)}, u32[]{:S(2)}, u32[]{:S(2)}) collective-permute-start(bf16[4,2,80,128]{3,2,1,0:T(8,128)(2,1)S(1)} %get-tuple-element.25), channel_id=1, source_target_pairs={{0,8},{1,9},{2,10},{3,11},{4,12},{5,13},{6,14},{7,15},{8,0},{9,1},... | collective-permute-start | bytes 491528 | tf_op jit(solution)/shard_map/spread/ppermute | solution.py:321
  24.5 0.7 collective-permute-done.10
  25.2 1.1 %collective-permute-done.11 = bf16[4,2,80,128]{3,2,1,0:T(8,128)(2,1)S(1)} collective-permute-done((bf16[4,2,80,128]{3,2,1,0:T(8,128)(2,1)S(1)}, bf16[4,2,80,128]{3,2,1,0:T(8,128)(2,1)S(1)}, u32[]{:S(2)}, u32[]{:S(2)}) %collective-permute-start.11) | collective-permute-done | bytes 163872 | tf_op jit(solution)/shard_map/spread/ppermute | solution.py:321
  26.4 2.6 %collective-permute-done.4 = bf16[4,2,80,128]{3,2,1,0:T(8,128)(2,1)S(1)} collective-permute-done((bf16[4,2,80,128]{3,2,1,0:T(8,128)(2,1)S(1)}, bf16[4,2,80,128]{3,2,1,0:T(8,128)(2,1)S(1)}, u32[]{:S(2)}, u32[]{:S(2)}) %collective-permute-start.4) | collective-permute-done | bytes 163872 | tf_op jit(solution)/shard_map/spread/ppermute | solution.py:321
  29.0 1.6 %collective-permute-done.5 = bf16[4,2,80,128]{3,2,1,0:T(8,128)(2,1)S(1)} collective-permute-done((bf16[4,2,80,128]{3,2,1,0:T(8,128)(2,1)S(1)}, bf16[4,2,80,128]{3,2,1,0:T(8,128)(2,1)S(1)}, u32[]{:S(2)}, u32[]{:S(2)}) %collective-permute-start.5) | collective-permute-done | bytes 163872 | tf_op jit(solution)/shard_map/spread/ppermute | solution.py:321
  30.7 0.7 copy-done
  31.4 0.0 copy-done.1
  31.4 28.0 %tiles.1 = (f32[16,8,128]{2,1,0:T(8,128)S(1)}, f32[16,8,128]{2,1,0:T(8,128)}) custom-call(s32[2,8]{1,0:T(2,128)S(1)} %bitcast.24, s32[1]{0:T(128)S(6)} %copy.31.count_ref, s32[4]{0:T(128)S(1)} %pad_add_fusion.base_ref, bf16[32,80,128]{2,1,0:T(8,128)(2,1)S(1)} %bitcast.21, bf16[32,80,128]{2,1,0:T(8,128)(2,1)S(1)} %bitcast.22, f32[32,64]{1,0:T(8,128)S(1)} %bitcast.23, ...), custom_call_target="tpu_custom_call" | custom-call | tf_op jit(solution)/shard_map/tiles/tiles/pallas_call | solution.py:249
  59.4 2.0 %collective-permute-start.13 = (f32[4,8,128]{2,1,0:T(8,128)S(1)}, f32[4,8,128]{2,1,0:T(8,128)S(1)}, u32[]{:S(2)}, u32[]{:S(2)}) collective-permute-start(f32[4,8,128]{2,1,0:T(8,128)S(1)} %get-tuple-element.16), channel_id=1, source_target_pairs={{0,2},{1,3},{2,0},{3,1},{4,6},{5,7},{6,4},{7,5},{8,10},{9,11},{10,... | collective-permute-start | bytes 49160 | tf_op jit(solution)/shard_map/collect/ppermute | solution.py:337
  61.3 0.3 collective-permute-start.14
  61.7 11.1 %all-to-all-start = ((f32[16,8,128]{2,1,0:T(8,128)}), f32[16,8,128]{2,1,0:T(8,128)S(1)}, u32[]{:S(2)}, u32[]{:S(2)}) async-start(f32[16,8,128]{2,1,0:T(8,128)} %get-tuple-element.11), calls=%async_computation | async-start | bytes 131072 | tf_op jit(solution)/shard_map/collect/all_to_all | solution.py:333
  72.8 0.6 slice_bitcast_fusion
  73.4 5.8 %collective-permute-start.16 = (f32[8,128]{1,0:T(8,128)S(1)}, f32[8,128]{1,0:T(8,128)S(1)}, u32[]{:S(2)}, u32[]{:S(2)}) collective-permute-start(f32[8,128]{1,0:T(8,128)S(1)} %get-tuple-element.34), channel_id=1, source_target_pairs={{0,8},{1,9},{2,10},{3,11},{4,12},{5,13},{6,14},{7,15},{8,0},{9,1},... | collective-permute-start | bytes 12296 | tf_op jit(solution)/shard_map/collect/ppermute | solution.py:338
  79.3 1.3 %collective-permute-done.16.two_ref = f32[8,128]{1,0:T(8,128)S(1)} collective-permute-done((f32[8,128]{1,0:T(8,128)S(1)}, f32[8,128]{1,0:T(8,128)S(1)}, u32[]{:S(2)}, u32[]{:S(2)}) %collective-permute-start.16) | collective-permute-done | bytes 4128 | tf_op jit(solution)/shard_map/collect/ppermute | solution.py:338
  80.6 2.6 %collective-permute-done.17.three_ref = f32[8,128]{1,0:T(8,128)S(1)} collective-permute-done((f32[8,128]{1,0:T(8,128)S(1)}, f32[8,128]{1,0:T(8,128)S(1)}, u32[]{:S(2)}, u32[]{:S(2)}) %collective-permute-start.17) | collective-permute-done | bytes 4128 | tf_op jit(solution)/shard_map/collect/ppermute | solution.py:338
  83.3 0.6 copy-done.7
  83.8 0.0 copy-done.3
  83.9 1.5 %add.22 = (f32[3,256]{1,0:T(4,128)}, f32[1,256]{1,0:T(1,128)}) custom-call(f32[8,128]{1,0:T(8,128)} %get-tuple-element.36.own_ref, f32[8,128]{1,0:T(8,128)} %copy-done.5, f32[8,128]{1,0:T(8,128)} %copy-done.6, f32[8,128]{1,0:T(8,128)} %copy-done.7, f32[16,8,128]{2,1,0:T(8,128)} %copy-done.3), custom_call_target="tpu_custom_call" | custom-call | tf_op jit(solution)/shard_map/add/pallas_call | solution.py:340
  (46 shorter events, 0.3 us)
Async XLA Ops:
  2.3 12.6 %collective-permute-start.6 = (bf16[1,2,80,128]{3,2,1,0:T(8,128)(2,1)}, bf16[1,2,80,128]{3,2,1,0:T(8,128)(2,1)S(1)}, u32[]{:S(2)}, u32[]{:S(2)}) collective-permute-start(bf16[1,2,80,128]{3,2,1,0:T(8,128)(2,1)} %get-tuple-element.9), channel_id=1, source_target_pairs={{0,16},{16,0},{32,48},{48,32},{64,80},{80,64},{96,112},{112,96},{1... | collective-permute-start | bytes 122888 | tf_op jit(solution)/shard_map/spread/ppermute | solution.py:317
  6.1 9.8 %collective-permute-start.7 = (bf16[1,2,80,128]{3,2,1,0:T(8,128)(2,1)}, bf16[1,2,80,128]{3,2,1,0:T(8,128)(2,1)S(1)}, u32[]{:S(2)}, u32[]{:S(2)}) collective-permute-start(bf16[1,2,80,128]{3,2,1,0:T(8,128)(2,1)} %get-tuple-element.9), channel_id=1, source_target_pairs={{0,32},{16,48},{32,0},{48,16},{64,96},{80,112},{96,64},{112,80},{1... | collective-permute-start | bytes 122888 | tf_op jit(solution)/shard_map/spread/ppermute | solution.py:317
  11.2 5.2 %collective-permute-start.8 = (bf16[1,2,80,128]{3,2,1,0:T(8,128)(2,1)}, bf16[1,2,80,128]{3,2,1,0:T(8,128)(2,1)S(1)}, u32[]{:S(2)}, u32[]{:S(2)}) collective-permute-start(bf16[1,2,80,128]{3,2,1,0:T(8,128)(2,1)} %get-tuple-element.9), channel_id=1, source_target_pairs={{0,48},{16,32},{32,16},{48,0},{64,112},{80,96},{96,80},{112,64},{1... | collective-permute-start | bytes 122888 | tf_op jit(solution)/shard_map/spread/ppermute | solution.py:317
  11.2 8.9 %collective-permute-start = (bf16[1,2,80,128]{3,2,1,0:T(8,128)(2,1)}, bf16[1,2,80,128]{3,2,1,0:T(8,128)(2,1)S(1)}, u32[]{:S(2)}, u32[]{:S(2)}) collective-permute-start(bf16[1,2,80,128]{3,2,1,0:T(8,128)(2,1)} %get-tuple-element.8), channel_id=1, source_target_pairs={{0,1},{1,0},{2,3},{3,2},{4,5},{5,4},{6,7},{7,6},{8,9},{9,8},{10,11... | collective-permute-start | bytes 122888 | tf_op jit(solution)/shard_map/spread/ppermute | solution.py:317
  12.4 7.9 %collective-permute-start.1 = (bf16[1,2,80,128]{3,2,1,0:T(8,128)(2,1)}, bf16[1,2,80,128]{3,2,1,0:T(8,128)(2,1)S(1)}, u32[]{:S(2)}, u32[]{:S(2)}) collective-permute-start(bf16[1,2,80,128]{3,2,1,0:T(8,128)(2,1)} %get-tuple-element.8), channel_id=1, source_target_pairs={{0,2},{1,3},{2,0},{3,1},{4,6},{5,7},{6,4},{7,5},{8,10},{9,11},{10,... | collective-permute-start | bytes 122888 | tf_op jit(solution)/shard_map/spread/ppermute | solution.py:317
  13.2 0.9 %copy-start.8 = (bf16[64]{0:T(256)(128)(2,1)S(1)}, bf16[64]{0:T(256)(128)(2,1)}, u32[]{:S(2)}) copy-start(bf16[64]{0:T(256)(128)(2,1)} %param.19) | copy-start | bytes 388
  14.0 0.9 %copy-start.4 = (bf16[1,2,80,128]{3,2,1,0:T(8,128)(2,1)S(1)}, bf16[1,2,80,128]{3,2,1,0:T(8,128)(2,1)}, u32[]{:S(2)}) copy-start(bf16[1,2,80,128]{3,2,1,0:T(8,128)(2,1)} %get-tuple-element.8) | copy-start | bytes 122884
  14.9 5.5 %collective-permute-start.2 = (bf16[1,2,80,128]{3,2,1,0:T(8,128)(2,1)S(1)}, bf16[1,2,80,128]{3,2,1,0:T(8,128)(2,1)S(1)}, u32[]{:S(2)}, u32[]{:S(2)}) collective-permute-start(bf16[1,2,80,128]{3,2,1,0:T(8,128)(2,1)S(1)} %copy-done.4), channel_id=1, source_target_pairs={{0,3},{1,2},{2,1},{3,0},{4,7},{5,6},{6,5},{7,4},{8,11},{9,10},{10,... | collective-permute-start | bytes 122888 | tf_op jit(solution)/shard_map/spread/ppermute | solution.py:317
  16.4 8.0 %collective-permute-start.9 = (bf16[4,2,80,128]{3,2,1,0:T(8,128)(2,1)S(1)}, bf16[4,2,80,128]{3,2,1,0:T(8,128)(2,1)S(1)}, u32[]{:S(2)}, u32[]{:S(2)}) collective-permute-start(bf16[4,2,80,128]{3,2,1,0:T(8,128)(2,1)S(1)} %get-tuple-element.17), channel_id=1, source_target_pairs={{0,64},{16,80},{32,96},{48,112},{64,0},{80,16},{96,32},{112,48},{1... | collective-permute-start | bytes 491528 | tf_op jit(solution)/shard_map/spread/ppermute | solution.py:321
  17.7 7.5 %collective-permute-start.10 = (bf16[4,2,80,128]{3,2,1,0:T(8,128)(2,1)S(1)}, bf16[4,2,80,128]{3,2,1,0:T(8,128)(2,1)S(1)}, u32[]{:S(2)}, u32[]{:S(2)}) collective-permute-start(bf16[4,2,80,128]{3,2,1,0:T(8,128)(2,1)S(1)} %get-tuple-element.17), channel_id=1, source_target_pairs={{0,128},{16,144},{32,160},{48,176},{64,192},{80,208},{96,224},{112... | collective-permute-start | bytes 491528 | tf_op jit(solution)/shard_map/spread/ppermute | solution.py:321
  20.1 6.2 %collective-permute-start.11 = (bf16[4,2,80,128]{3,2,1,0:T(8,128)(2,1)S(1)}, bf16[4,2,80,128]{3,2,1,0:T(8,128)(2,1)S(1)}, u32[]{:S(2)}, u32[]{:S(2)}) collective-permute-start(bf16[4,2,80,128]{3,2,1,0:T(8,128)(2,1)S(1)} %get-tuple-element.17), channel_id=1, source_target_pairs={{0,192},{16,208},{32,224},{48,240},{64,128},{80,144},{96,160},{112... | collective-permute-start | bytes 491528 | tf_op jit(solution)/shard_map/spread/ppermute | solution.py:321
  20.4 5.9 %collective-permute-start.3 = (bf16[4,2,80,128]{3,2,1,0:T(8,128)(2,1)S(1)}, bf16[4,2,80,128]{3,2,1,0:T(8,128)(2,1)S(1)}, u32[]{:S(2)}, u32[]{:S(2)}) collective-permute-start(bf16[4,2,80,128]{3,2,1,0:T(8,128)(2,1)S(1)} %get-tuple-element.25), channel_id=1, source_target_pairs={{0,4},{1,5},{2,6},{3,7},{4,0},{5,1},{6,2},{7,3},{8,12},{9,13},{10,... | collective-permute-start | bytes 491528 | tf_op jit(solution)/shard_map/spread/ppermute | solution.py:321
  21.8 7.2 %collective-permute-start.4 = (bf16[4,2,80,128]{3,2,1,0:T(8,128)(2,1)S(1)}, bf16[4,2,80,128]{3,2,1,0:T(8,128)(2,1)S(1)}, u32[]{:S(2)}, u32[]{:S(2)}) collective-permute-start(bf16[4,2,80,128]{3,2,1,0:T(8,128)(2,1)S(1)} %get-tuple-element.25), channel_id=1, source_target_pairs={{0,8},{1,9},{2,10},{3,11},{4,12},{5,13},{6,14},{7,15},{8,0},{9,1},... | collective-permute-start | bytes 491528 | tf_op jit(solution)/shard_map/spread/ppermute | solution.py:321
  24.4 6.2 %collective-permute-start.5 = (bf16[4,2,80,128]{3,2,1,0:T(8,128)(2,1)S(1)}, bf16[4,2,80,128]{3,2,1,0:T(8,128)(2,1)S(1)}, u32[]{:S(2)}, u32[]{:S(2)}) collective-permute-start(bf16[4,2,80,128]{3,2,1,0:T(8,128)(2,1)S(1)} %get-tuple-element.25), channel_id=1, source_target_pairs={{0,12},{1,13},{2,14},{3,15},{4,8},{5,9},{6,10},{7,11},{8,4},{9,5},... | collective-permute-start | bytes 491528 | tf_op jit(solution)/shard_map/spread/ppermute | solution.py:321
  30.7 0.7 copy-start
  30.7 0.7 copy-start.1
  30.7 0.7 copy-start.2
  59.4 13.4 %collective-permute-start.12 = (f32[4,8,128]{2,1,0:T(8,128)S(1)}, f32[4,8,128]{2,1,0:T(8,128)S(1)}, u32[]{:S(2)}, u32[]{:S(2)}) collective-permute-start(f32[4,8,128]{2,1,0:T(8,128)S(1)} %get-tuple-element.14), channel_id=1, source_target_pairs={{0,1},{1,0},{2,3},{3,2},{4,5},{5,4},{6,7},{7,6},{8,9},{9,8},{10,11... | collective-permute-start | bytes 49160 | tf_op jit(solution)/shard_map/collect/ppermute | solution.py:337
  59.4 13.4 %collective-permute-start.13 = (f32[4,8,128]{2,1,0:T(8,128)S(1)}, f32[4,8,128]{2,1,0:T(8,128)S(1)}, u32[]{:S(2)}, u32[]{:S(2)}) collective-permute-start(f32[4,8,128]{2,1,0:T(8,128)S(1)} %get-tuple-element.16), channel_id=1, source_target_pairs={{0,2},{1,3},{2,0},{3,1},{4,6},{5,7},{6,4},{7,5},{8,10},{9,11},{10,... | collective-permute-start | bytes 49160 | tf_op jit(solution)/shard_map/collect/ppermute | solution.py:337
  61.3 11.5 %collective-permute-start.14 = (f32[4,8,128]{2,1,0:T(8,128)S(1)}, f32[4,8,128]{2,1,0:T(8,128)S(1)}, u32[]{:S(2)}, u32[]{:S(2)}) collective-permute-start(f32[4,8,128]{2,1,0:T(8,128)S(1)} %get-tuple-element.15), channel_id=1, source_target_pairs={{0,3},{1,2},{2,1},{3,0},{4,7},{5,6},{6,5},{7,4},{8,11},{9,10},{10,... | collective-permute-start | bytes 49160 | tf_op jit(solution)/shard_map/collect/ppermute | solution.py:337
  61.7 21.6 %all-to-all-start = ((f32[16,8,128]{2,1,0:T(8,128)}), f32[16,8,128]{2,1,0:T(8,128)S(1)}, u32[]{:S(2)}, u32[]{:S(2)}) async-start(f32[16,8,128]{2,1,0:T(8,128)} %get-tuple-element.11), calls=%async_computation | async-start | bytes 131072 | tf_op jit(solution)/shard_map/collect/all_to_all | solution.py:333
  73.4 5.9 %collective-permute-start.15 = (f32[8,128]{1,0:T(8,128)S(1)}, f32[8,128]{1,0:T(8,128)S(1)}, u32[]{:S(2)}, u32[]{:S(2)}) collective-permute-start(f32[8,128]{1,0:T(8,128)S(1)} %get-tuple-element.35), channel_id=1, source_target_pairs={{0,4},{1,5},{2,6},{3,7},{4,0},{5,1},{6,2},{7,3},{8,12},{9,13},{10,... | collective-permute-start | bytes 12296 | tf_op jit(solution)/shard_map/collect/ppermute | solution.py:338
  73.4 7.2 %collective-permute-start.16 = (f32[8,128]{1,0:T(8,128)S(1)}, f32[8,128]{1,0:T(8,128)S(1)}, u32[]{:S(2)}, u32[]{:S(2)}) collective-permute-start(f32[8,128]{1,0:T(8,128)S(1)} %get-tuple-element.34), channel_id=1, source_target_pairs={{0,8},{1,9},{2,10},{3,11},{4,12},{5,13},{6,14},{7,15},{8,0},{9,1},... | collective-permute-start | bytes 12296 | tf_op jit(solution)/shard_map/collect/ppermute | solution.py:338
  79.3 4.0 %collective-permute-start.17 = (f32[8,128]{1,0:T(8,128)S(1)}, f32[8,128]{1,0:T(8,128)S(1)}, u32[]{:S(2)}, u32[]{:S(2)}) collective-permute-start(f32[8,128]{1,0:T(8,128)S(1)} %get-tuple-element.33), channel_id=1, source_target_pairs={{0,12},{1,13},{2,14},{3,15},{4,8},{5,9},{6,10},{7,11},{8,4},{9,5},... | collective-permute-start | bytes 12296 | tf_op jit(solution)/shard_map/collect/ppermute | solution.py:338
  79.3 4.0 %copy-start.5 = (f32[8,128]{1,0:T(8,128)}, f32[8,128]{1,0:T(8,128)S(1)}, u32[]{:S(2)}) copy-start(f32[8,128]{1,0:T(8,128)S(1)} %collective-permute-done.15.one_ref) | copy-start | bytes 12292
  80.6 2.6 %copy-start.6 = (f32[8,128]{1,0:T(8,128)}, f32[8,128]{1,0:T(8,128)S(1)}, u32[]{:S(2)}) copy-start(f32[8,128]{1,0:T(8,128)S(1)} %collective-permute-done.16.two_ref) | copy-start | bytes 12292
  83.2 0.6 copy-start.7
  83.2 0.6 copy-start.3

commit v6 on v5

--- a/solution.py
+++ b/solution.py
@@ -97,7 +97,7 @@
     ).astype(F32)
     lane4 = lax.broadcasted_iota(jnp.int32, (HID, CL), 1) % 4
 
-    def prepare(slot, carry):
+    def prepare(slot):
         first = tiles_ref[0, slot]
         away = jnp.bitwise_xor(first // CPD, base_ref[1])
         left = left_ref[away * CPD + first % CPD].astype(F32)
@@ -119,16 +119,15 @@
         adds_ref[slot] = jnp.concatenate([0.5 * proj_b] * 2, 1).astype(BF16)
         turned_ref[slot] = jnp.concatenate([pos_a, live_a, jnp.zeros((CL - 4, CL), F32)], 0).T
         across_ref[slot] = jnp.concatenate([pos_b, live_b, jnp.zeros((4, CL), F32)], 0)
-        mine = jnp.where(slot < count, (jnp.minimum(fill_left, fill_right) + 7) // 8, 0)
-
-        def enlist(g, at):
-            source_ref[at] = slot * 16 + g
-            target_ref[at + 2 * GROUPS] = slot * 16 + g
-            return at + 1
-
-        return lax.fori_loop(0, mine, enlist, carry)
-
-    groups = lax.fori_loop(0, tiles_ref.shape[1], prepare, jnp.int32(0), unroll=2)
+        return jnp.where(slot < count, (jnp.minimum(fill_left, fill_right) + 7) // 8, 0)
+
+    sizes = [prepare(slot) for slot in range(tiles_ref.shape[1])]
+    groups = jnp.int32(0)
+    for slot, size in enumerate(sizes):
+        for g in range(CL // 8):
+            source_ref[groups + g] = slot * 16 + g
+            target_ref[groups + 2 * GROUPS + g] = slot * 16 + g
+        groups = groups + size
     spare = slopes_ref.shape[0] - 1
     for k in range(2 * GROUPS):
         target_ref[k] = spare * 16
@@ -243,7 +242,7 @@
     vmem = pl.BlockSpec(memory_space=pltpu.VMEM)
     slots = tiles.shape[0]
     groups = GROUPS
-    listed = slots * (CL // 8) + 5 * GROUPS
+    listed = (slots + 1) * (CL // 8) + 5 * GROUPS
     hid4 = 4 * HID
     wide = 2 * CL
     return pl.pallas_call(

time: 86 us -> 85.1 us (0.990)
  Pallas kernels: 31.1 us -> 25.9 us
  starting transfers between devices: 39.1 us -> 42.6 us
    pallas_call x1, Pallas kernels: 28 us -> 22.8 us  [tile_call(): pl.pallas_call(tile_kernel, name='tiles', out_shape=(jax.ShapeDtypeStruct...]
    ppermute x3, starting transfers between devices: 2.3 us -> 6.54 us  [body(): near = near + lax.ppermute(firsts[k], 'col', across(cols, k))]
    all_to_all x1, waiting for transfers between devices: 0.01 us -> 2.86 us  [body(): seconds = lax.all_to_all(seconds, 'row', 0, 0)]
    ppermute x3, waiting for transfers between devices: 3.95 us -> 1.94 us  [body(): lax.ppermute(near[k], 'col', across(cols, 4 * k))]
    ppermute x3, starting transfers between devices: 5.85 us -> 3.87 us  [body(): lax.ppermute(near[k], 'col', across(cols, 4 * k))]
    all_to_all x1, starting transfers between devices: 11.1 us -> 12.4 us  [body(): seconds = lax.all_to_all(seconds, 'row', 0, 0)]
  transfers between devices with their start and end apart: 19 -> 19, of which waited for: 7 -> 8; matrix products, arithmetic and copies ran while one was open for 2% -> 2% of each run, Pallas kernels for 0% -> 0%
where the time goes in v6:
time: 85.1 us; the launch traced here: 84.6 us
  starting transfers between devices  42.6 us (50%)
  Pallas kernels  25.9 us (30%)
  waiting for transfers between devices  11.3 us (13%)
  local copies, waits for them, and re-layouts  3.11 us (4%)
  between operations  1.5 us (2%)
    pallas_call x1, Pallas kernels, tile_call(): pl.pallas_call(tile_kernel, name='tiles', out_shape=(jax.ShapeDtypeStruct...  22.8 us
    all_to_all x1, starting transfers between devices, body(): seconds = lax.all_to_all(seconds, 'row', 0, 0)  12.4 us
    ppermute x6, starting transfers between devices, body(): lax.ppermute(own, axis, across(16, k))  11.9 us
    ppermute x6, starting transfers between devices, body(): lax.ppermute(own, axis, across(16, 4 * k))  7.95 us
    ppermute x3, starting transfers between devices, body(): near = near + lax.ppermute(firsts[k], 'col', across(cols, k))  6.54 us
    ppermute x6, waiting for transfers between devices, body(): lax.ppermute(own, axis, across(16, 4 * k))  6.06 us
    ppermute x3, starting transfers between devices, body(): lax.ppermute(near[k], 'col', across(cols, 4 * k))  3.87 us
    all_to_all x1, waiting for transfers between devices, body(): seconds = lax.all_to_all(seconds, 'row', 0, 0)  2.86 us
  transfers between devices with their start and end apart: 19, of which 8 were waited for; matrix products, arithmetic and copies ran while one was open for 2% of the time, Pallas kernels for 0%

profile of v6, /device:TPU:1, one launch (start us, length us, event | category | flops | bytes accessed | tf_op | source)
XLA Modules:
  0.0 84.6 jit_solution(13355117541209600431)
XLA Ops:
  0.6 1.6 %pack.1 = (bf16[1,2,80,128]{3,2,1,0:T(8,128)(2,1)}, bf16[1,2,80,128]{3,2,1,0:T(8,128)(2,1)}) custom-call(s32[2]{0:T(128)} %fill_ref.1, f32[3,256]{1,0:T(4,128)} %pos_ref.1, bf16[128,256]{1,0:T(8,128)(2,1)} %feat_ref.1, bf16[64,128]{1,0:T(8,128)(2,1)} %bitcast.25, bf16[64,128]{1,0:T(8,128)(2,1)} %bitcast.26), custom_call_target="tpu_custom_call" | custom-call | tf_op jit(solution)/shard_map/pack/pallas_call | solution.py:305
  2.3 3.8 %collective-permute-start.6 = (bf16[1,2,80,128]{3,2,1,0:T(8,128)(2,1)}, bf16[1,2,80,128]{3,2,1,0:T(8,128)(2,1)S(1)}, u32[]{:S(2)}, u32[]{:S(2)}) collective-permute-start(bf16[1,2,80,128]{3,2,1,0:T(8,128)(2,1)} %get-tuple-element.9), channel_id=1, source_target_pairs={{0,16},{16,0},{32,48},{48,32},{64,80},{80,64},{96,112},{112,96},{1... | collective-permute-start | bytes 122888 | tf_op jit(solution)/shard_map/spread/ppermute | solution.py:316
  6.1 5.1 %collective-permute-start.7 = (bf16[1,2,80,128]{3,2,1,0:T(8,128)(2,1)}, bf16[1,2,80,128]{3,2,1,0:T(8,128)(2,1)S(1)}, u32[]{:S(2)}, u32[]{:S(2)}) collective-permute-start(bf16[1,2,80,128]{3,2,1,0:T(8,128)(2,1)} %get-tuple-element.9), channel_id=1, source_target_pairs={{0,32},{16,48},{32,0},{48,16},{64,96},{80,112},{96,64},{112,80},{1... | collective-permute-start | bytes 122888 | tf_op jit(solution)/shard_map/spread/ppermute | solution.py:316
  11.2 1.2 %collective-permute-start = (bf16[1,2,80,128]{3,2,1,0:T(8,128)(2,1)}, bf16[1,2,80,128]{3,2,1,0:T(8,128)(2,1)S(1)}, u32[]{:S(2)}, u32[]{:S(2)}) collective-permute-start(bf16[1,2,80,128]{3,2,1,0:T(8,128)(2,1)} %get-tuple-element.8), channel_id=1, source_target_pairs={{0,1},{1,0},{2,3},{3,2},{4,5},{5,4},{6,7},{7,6},{8,9},{9,8},{10,11... | collective-permute-start | bytes 122888 | tf_op jit(solution)/shard_map/spread/ppermute | solution.py:316
  12.4 0.7 collective-permute-start.1
  13.2 0.8 constant_dynamic-update-slice_fusion.3
  14.1 0.1 pad_add_fusion.base_ref
  14.1 0.1 copy.12.wo_ref
  14.9 1.0 %collective-permute-start.2 = (bf16[1,2,80,128]{3,2,1,0:T(8,128)(2,1)S(1)}, bf16[1,2,80,128]{3,2,1,0:T(8,128)(2,1)S(1)}, u32[]{:S(2)}, u32[]{:S(2)}) collective-permute-start(bf16[1,2,80,128]{3,2,1,0:T(8,128)(2,1)S(1)} %copy-done.4), channel_id=1, source_target_pairs={{0,3},{1,2},{2,1},{3,0},{4,7},{5,6},{6,5},{7,4},{8,11},{9,10},{10,... | collective-permute-start | bytes 122888 | tf_op jit(solution)/shard_map/spread/ppermute | solution.py:316
  15.9 0.4 collective-permute-done.8
  16.4 1.3 %collective-permute-start.9 = (bf16[4,2,80,128]{3,2,1,0:T(8,128)(2,1)S(1)}, bf16[4,2,80,128]{3,2,1,0:T(8,128)(2,1)S(1)}, u32[]{:S(2)}, u32[]{:S(2)}) collective-permute-start(bf16[4,2,80,128]{3,2,1,0:T(8,128)(2,1)S(1)} %get-tuple-element.17), channel_id=1, source_target_pairs={{0,64},{16,80},{32,96},{48,112},{64,0},{80,16},{96,32},{112,48},{1... | collective-permute-start | bytes 491528 | tf_op jit(solution)/shard_map/spread/ppermute | solution.py:320
  17.7 2.4 %collective-permute-start.10 = (bf16[4,2,80,128]{3,2,1,0:T(8,128)(2,1)S(1)}, bf16[4,2,80,128]{3,2,1,0:T(8,128)(2,1)S(1)}, u32[]{:S(2)}, u32[]{:S(2)}) collective-permute-start(bf16[4,2,80,128]{3,2,1,0:T(8,128)(2,1)S(1)} %get-tuple-element.17), channel_id=1, source_target_pairs={{0,128},{16,144},{32,160},{48,176},{64,192},{80,208},{96,224},{112... | collective-permute-start | bytes 491528 | tf_op jit(solution)/shard_map/spread/ppermute | solution.py:320
  20.1 0.2 collective-permute-start.11
  20.4 1.4 %collective-permute-start.3 = (bf16[4,2,80,128]{3,2,1,0:T(8,128)(2,1)S(1)}, bf16[4,2,80,128]{3,2,1,0:T(8,128)(2,1)S(1)}, u32[]{:S(2)}, u32[]{:S(2)}) collective-permute-start(bf16[4,2,80,128]{3,2,1,0:T(8,128)(2,1)S(1)} %get-tuple-element.25), channel_id=1, source_target_pairs={{0,4},{1,5},{2,6},{3,7},{4,0},{5,1},{6,2},{7,3},{8,12},{9,13},{10,... | collective-permute-start | bytes 491528 | tf_op jit(solution)/shard_map/spread/ppermute | solution.py:320
  21.8 2.6 %collective-permute-start.4 = (bf16[4,2,80,128]{3,2,1,0:T(8,128)(2,1)S(1)}, bf16[4,2,80,128]{3,2,1,0:T(8,128)(2,1)S(1)}, u32[]{:S(2)}, u32[]{:S(2)}) collective-permute-start(bf16[4,2,80,128]{3,2,1,0:T(8,128)(2,1)S(1)} %get-tuple-element.25), channel_id=1, source_target_pairs={{0,8},{1,9},{2,10},{3,11},{4,12},{5,13},{6,14},{7,15},{8,0},{9,1},... | collective-permute-start | bytes 491528 | tf_op jit(solution)/shard_map/spread/ppermute | solution.py:320
  24.5 0.7 collective-permute-done.10
  25.2 1.1 %collective-permute-done.11 = bf16[4,2,80,128]{3,2,1,0:T(8,128)(2,1)S(1)} collective-permute-done((bf16[4,2,80,128]{3,2,1,0:T(8,128)(2,1)S(1)}, bf16[4,2,80,128]{3,2,1,0:T(8,128)(2,1)S(1)}, u32[]{:S(2)}, u32[]{:S(2)}) %collective-permute-start.11) | collective-permute-done | bytes 163872 | tf_op jit(solution)/shard_map/spread/ppermute | solution.py:320
  26.4 2.6 %collective-permute-done.4 = bf16[4,2,80,128]{3,2,1,0:T(8,128)(2,1)S(1)} collective-permute-done((bf16[4,2,80,128]{3,2,1,0:T(8,128)(2,1)S(1)}, bf16[4,2,80,128]{3,2,1,0:T(8,128)(2,1)S(1)}, u32[]{:S(2)}, u32[]{:S(2)}) %collective-permute-start.4) | collective-permute-done | bytes 163872 | tf_op jit(solution)/shard_map/spread/ppermute | solution.py:320
  29.0 1.6 %collective-permute-done.5 = bf16[4,2,80,128]{3,2,1,0:T(8,128)(2,1)S(1)} collective-permute-done((bf16[4,2,80,128]{3,2,1,0:T(8,128)(2,1)S(1)}, bf16[4,2,80,128]{3,2,1,0:T(8,128)(2,1)S(1)}, u32[]{:S(2)}, u32[]{:S(2)}) %collective-permute-start.5) | collective-permute-done | bytes 163872 | tf_op jit(solution)/shard_map/spread/ppermute | solution.py:320
  30.7 0.7 copy-done
  31.4 22.8 %tiles.1 = (f32[16,8,128]{2,1,0:T(8,128)S(1)}, f32[16,8,128]{2,1,0:T(8,128)}) custom-call(s32[2,8]{1,0:T(2,128)S(1)} %bitcast.24, s32[1]{0:T(128)S(6)} %copy.31.count_ref, s32[4]{0:T(128)S(1)} %pad_add_fusion.base_ref, bf16[32,80,128]{2,1,0:T(8,128)(2,1)S(1)} %bitcast.21, bf16[32,80,128]{2,1,0:T(8,128)(2,1)S(1)} %bitcast.22, f32[32,64]{1,0:T(8,128)S(1)} %bitcast.23, ...), custom_call_target="tpu_custom_call" | custom-call | tf_op jit(solution)/shard_map/tiles/tiles/pallas_call | solution.py:248
  54.2 6.2 %collective-permute-start.13 = (f32[4,8,128]{2,1,0:T(8,128)S(1)}, f32[4,8,128]{2,1,0:T(8,128)S(1)}, u32[]{:S(2)}, u32[]{:S(2)}) collective-permute-start(f32[4,8,128]{2,1,0:T(8,128)S(1)} %get-tuple-element.16), channel_id=1, source_target_pairs={{0,2},{1,3},{2,0},{3,1},{4,6},{5,7},{6,4},{7,5},{8,10},{9,11},{10,... | collective-permute-start | bytes 49160 | tf_op jit(solution)/shard_map/collect/ppermute | solution.py:336
  60.4 0.3 collective-permute-start.14
  60.8 12.4 %all-to-all-start = ((f32[16,8,128]{2,1,0:T(8,128)}), f32[16,8,128]{2,1,0:T(8,128)S(1)}, u32[]{:S(2)}, u32[]{:S(2)}) async-start(f32[16,8,128]{2,1,0:T(8,128)} %get-tuple-element.11), calls=%async_computation | async-start | bytes 131072 | tf_op jit(solution)/shard_map/collect/all_to_all | solution.py:332
  73.2 0.6 slice_bitcast_fusion
  73.8 1.9 %collective-permute-start.16 = (f32[8,128]{1,0:T(8,128)S(1)}, f32[8,128]{1,0:T(8,128)S(1)}, u32[]{:S(2)}, u32[]{:S(2)}) collective-permute-start(f32[8,128]{1,0:T(8,128)S(1)} %get-tuple-element.34), channel_id=1, source_target_pairs={{0,8},{1,9},{2,10},{3,11},{4,12},{5,13},{6,14},{7,15},{8,0},{9,1},... | collective-permute-start | bytes 12296 | tf_op jit(solution)/shard_map/collect/ppermute | solution.py:337
  75.7 2.0 %collective-permute-start.17 = (f32[8,128]{1,0:T(8,128)S(1)}, f32[8,128]{1,0:T(8,128)S(1)}, u32[]{:S(2)}, u32[]{:S(2)}) collective-permute-start(f32[8,128]{1,0:T(8,128)S(1)} %get-tuple-element.33), channel_id=1, source_target_pairs={{0,12},{1,13},{2,14},{3,15},{4,8},{5,9},{6,10},{7,11},{8,4},{9,5},... | collective-permute-start | bytes 12296 | tf_op jit(solution)/shard_map/collect/ppermute | solution.py:337
  77.7 0.4 collective-permute-done.16.two_ref
  78.1 1.5 %collective-permute-done.17.three_ref = f32[8,128]{1,0:T(8,128)S(1)} collective-permute-done((f32[8,128]{1,0:T(8,128)S(1)}, f32[8,128]{1,0:T(8,128)S(1)}, u32[]{:S(2)}, u32[]{:S(2)}) %collective-permute-start.17) | collective-permute-done | bytes 4128 | tf_op jit(solution)/shard_map/collect/ppermute | solution.py:337
  79.6 2.9 %all-to-all-done.second_ref = f32[16,8,128]{2,1,0:T(8,128)S(1)} async-done(((f32[16,8,128]{2,1,0:T(8,128)}), f32[16,8,128]{2,1,0:T(8,128)S(1)}, u32[]{:S(2)}, u32[]{:S(2)}) %all-to-all-start) | async-done | bytes 65568 | tf_op jit(solution)/shard_map/collect/all_to_all | solution.py:332
  82.5 0.6 copy-done.3
  83.1 1.5 %add.22 = (f32[3,256]{1,0:T(4,128)}, f32[1,256]{1,0:T(1,128)}) custom-call(f32[8,128]{1,0:T(8,128)} %get-tuple-element.36.own_ref, f32[8,128]{1,0:T(8,128)} %copy-done.5, f32[8,128]{1,0:T(8,128)} %copy-done.6, f32[8,128]{1,0:T(8,128)} %copy-done.7, f32[16,8,128]{2,1,0:T(8,128)} %copy-done.3), custom_call_target="tpu_custom_call" | custom-call | tf_op jit(solution)/shard_map/add/pallas_call | solution.py:339
  (46 shorter events, 0.4 us)
Async XLA Ops:
  2.3 12.6 %collective-permute-start.6 = (bf16[1,2,80,128]{3,2,1,0:T(8,128)(2,1)}, bf16[1,2,80,128]{3,2,1,0:T(8,128)(2,1)S(1)}, u32[]{:S(2)}, u32[]{:S(2)}) collective-permute-start(bf16[1,2,80,128]{3,2,1,0:T(8,128)(2,1)} %get-tuple-element.9), channel_id=1, source_target_pairs={{0,16},{16,0},{32,48},{48,32},{64,80},{80,64},{96,112},{112,96},{1... | collective-permute-start | bytes 122888 | tf_op jit(solution)/shard_map/spread/ppermute | solution.py:316
  6.1 9.8 %collective-permute-start.7 = (bf16[1,2,80,128]{3,2,1,0:T(8,128)(2,1)}, bf16[1,2,80,128]{3,2,1,0:T(8,128)(2,1)S(1)}, u32[]{:S(2)}, u32[]{:S(2)}) collective-permute-start(bf16[1,2,80,128]{3,2,1,0:T(8,128)(2,1)} %get-tuple-element.9), channel_id=1, source_target_pairs={{0,32},{16,48},{32,0},{48,16},{64,96},{80,112},{96,64},{112,80},{1... | collective-permute-start | bytes 122888 | tf_op jit(solution)/shard_map/spread/ppermute | solution.py:316
  11.2 5.2 %collective-permute-start.8 = (bf16[1,2,80,128]{3,2,1,0:T(8,128)(2,1)}, bf16[1,2,80,128]{3,2,1,0:T(8,128)(2,1)S(1)}, u32[]{:S(2)}, u32[]{:S(2)}) collective-permute-start(bf16[1,2,80,128]{3,2,1,0:T(8,128)(2,1)} %get-tuple-element.9), channel_id=1, source_target_pairs={{0,48},{16,32},{32,16},{48,0},{64,112},{80,96},{96,80},{112,64},{1... | collective-permute-start | bytes 122888 | tf_op jit(solution)/shard_map/spread/ppermute | solution.py:316
  11.2 8.9 %collective-permute-start = (bf16[1,2,80,128]{3,2,1,0:T(8,128)(2,1)}, bf16[1,2,80,128]{3,2,1,0:T(8,128)(2,1)S(1)}, u32[]{:S(2)}, u32[]{:S(2)}) collective-permute-start(bf16[1,2,80,128]{3,2,1,0:T(8,128)(2,1)} %get-tuple-element.8), channel_id=1, source_target_pairs={{0,1},{1,0},{2,3},{3,2},{4,5},{5,4},{6,7},{7,6},{8,9},{9,8},{10,11... | collective-permute-start | bytes 122888 | tf_op jit(solution)/shard_map/spread/ppermute | solution.py:316
  12.4 7.9 %collective-permute-start.1 = (bf16[1,2,80,128]{3,2,1,0:T(8,128)(2,1)}, bf16[1,2,80,128]{3,2,1,0:T(8,128)(2,1)S(1)}, u32[]{:S(2)}, u32[]{:S(2)}) collective-permute-start(bf16[1,2,80,128]{3,2,1,0:T(8,128)(2,1)} %get-tuple-element.8), channel_id=1, source_target_pairs={{0,2},{1,3},{2,0},{3,1},{4,6},{5,7},{6,4},{7,5},{8,10},{9,11},{10,... | collective-permute-start | bytes 122888 | tf_op jit(solution)/shard_map/spread/ppermute | solution.py:316
  13.2 0.9 %copy-start.8 = (bf16[64]{0:T(256)(128)(2,1)S(1)}, bf16[64]{0:T(256)(128)(2,1)}, u32[]{:S(2)}) copy-start(bf16[64]{0:T(256)(128)(2,1)} %param.19) | copy-start | bytes 388
  14.0 0.9 %copy-start.4 = (bf16[1,2,80,128]{3,2,1,0:T(8,128)(2,1)S(1)}, bf16[1,2,80,128]{3,2,1,0:T(8,128)(2,1)}, u32[]{:S(2)}) copy-start(bf16[1,2,80,128]{3,2,1,0:T(8,128)(2,1)} %get-tuple-element.8) | copy-start | bytes 122884
  14.9 5.5 %collective-permute-start.2 = (bf16[1,2,80,128]{3,2,1,0:T(8,128)(2,1)S(1)}, bf16[1,2,80,128]{3,2,1,0:T(8,128)(2,1)S(1)}, u32[]{:S(2)}, u32[]{:S(2)}) collective-permute-start(bf16[1,2,80,128]{3,2,1,0:T(8,128)(2,1)S(1)} %copy-done.4), channel_id=1, source_target_pairs={{0,3},{1,2},{2,1},{3,0},{4,7},{5,6},{6,5},{7,4},{8,11},{9,10},{10,... | collective-permute-start | bytes 122888 | tf_op jit(solution)/shard_map/spread/ppermute | solution.py:316
  16.4 8.0 %collective-permute-start.9 = (bf16[4,2,80,128]{3,2,1,0:T(8,128)(2,1)S(1)}, bf16[4,2,80,128]{3,2,1,0:T(8,128)(2,1)S(1)}, u32[]{:S(2)}, u32[]{:S(2)}) collective-permute-start(bf16[4,2,80,128]{3,2,1,0:T(8,128)(2,1)S(1)} %get-tuple-element.17), channel_id=1, source_target_pairs={{0,64},{16,80},{32,96},{48,112},{64,0},{80,16},{96,32},{112,48},{1... | collective-permute-start | bytes 491528 | tf_op jit(solution)/shard_map/spread/ppermute | solution.py:320
  17.7 7.5 %collective-permute-start.10 = (bf16[4,2,80,128]{3,2,1,0:T(8,128)(2,1)S(1)}, bf16[4,2,80,128]{3,2,1,0:T(8,128)(2,1)S(1)}, u32[]{:S(2)}, u32[]{:S(2)}) collective-permute-start(bf16[4,2,80,128]{3,2,1,0:T(8,128)(2,1)S(1)} %get-tuple-element.17), channel_id=1, source_target_pairs={{0,128},{16,144},{32,160},{48,176},{64,192},{80,208},{96,224},{112... | collective-permute-start | bytes 491528 | tf_op jit(solution)/shard_map/spread/ppermute | solution.py:320
  20.1 6.2 %collective-permute-start.11 = (bf16[4,2,80,128]{3,2,1,0:T(8,128)(2,1)S(1)}, bf16[4,2,80,128]{3,2,1,0:T(8,128)(2,1)S(1)}, u32[]{:S(2)}, u32[]{:S(2)}) collective-permute-start(bf16[4,2,80,128]{3,2,1,0:T(8,128)(2,1)S(1)} %get-tuple-element.17), channel_id=1, source_target_pairs={{0,192},{16,208},{32,224},{48,240},{64,128},{80,144},{96,160},{112... | collective-permute-start | bytes 491528 | tf_op jit(solution)/shard_map/spread/ppermute | solution.py:320
  20.4 5.9 %collective-permute-start.3 = (bf16[4,2,80,128]{3,2,1,0:T(8,128)(2,1)S(1)}, bf16[4,2,80,128]{3,2,1,0:T(8,128)(2,1)S(1)}, u32[]{:S(2)}, u32[]{:S(2)}) collective-permute-start(bf16[4,2,80,128]{3,2,1,0:T(8,128)(2,1)S(1)} %get-tuple-element.25), channel_id=1, source_target_pairs={{0,4},{1,5},{2,6},{3,7},{4,0},{5,1},{6,2},{7,3},{8,12},{9,13},{10,... | collective-permute-start | bytes 491528 | tf_op jit(solution)/shard_map/spread/ppermute | solution.py:320
  21.8 7.2 %collective-permute-start.4 = (bf16[4,2,80,128]{3,2,1,0:T(8,128)(2,1)S(1)}, bf16[4,2,80,128]{3,2,1,0:T(8,128)(2,1)S(1)}, u32[]{:S(2)}, u32[]{:S(2)}) collective-permute-start(bf16[4,2,80,128]{3,2,1,0:T(8,128)(2,1)S(1)} %get-tuple-element.25), channel_id=1, source_target_pairs={{0,8},{1,9},{2,10},{3,11},{4,12},{5,13},{6,14},{7,15},{8,0},{9,1},... | collective-permute-start | bytes 491528 | tf_op jit(solution)/shard_map/spread/ppermute | solution.py:320
  24.4 6.2 %collective-permute-start.5 = (bf16[4,2,80,128]{3,2,1,0:T(8,128)(2,1)S(1)}, bf16[4,2,80,128]{3,2,1,0:T(8,128)(2,1)S(1)}, u32[]{:S(2)}, u32[]{:S(2)}) collective-permute-start(bf16[4,2,80,128]{3,2,1,0:T(8,128)(2,1)S(1)} %get-tuple-element.25), channel_id=1, source_target_pairs={{0,12},{1,13},{2,14},{3,15},{4,8},{5,9},{6,10},{7,11},{8,4},{9,5},... | collective-permute-start | bytes 491528 | tf_op jit(solution)/shard_map/spread/ppermute | solution.py:320
  30.7 0.7 copy-start
  30.7 0.7 copy-start.1
  30.7 0.7 copy-start.2
  54.2 18.9 %collective-permute-start.12 = (f32[4,8,128]{2,1,0:T(8,128)S(1)}, f32[4,8,128]{2,1,0:T(8,128)S(1)}, u32[]{:S(2)}, u32[]{:S(2)}) collective-permute-start(f32[4,8,128]{2,1,0:T(8,128)S(1)} %get-tuple-element.14), channel_id=1, source_target_pairs={{0,1},{1,0},{2,3},{3,2},{4,5},{5,4},{6,7},{7,6},{8,9},{9,8},{10,11... | collective-permute-start | bytes 49160 | tf_op jit(solution)/shard_map/collect/ppermute | solution.py:336
  54.2 18.9 %collective-permute-start.13 = (f32[4,8,128]{2,1,0:T(8,128)S(1)}, f32[4,8,128]{2,1,0:T(8,128)S(1)}, u32[]{:S(2)}, u32[]{:S(2)}) collective-permute-start(f32[4,8,128]{2,1,0:T(8,128)S(1)} %get-tuple-element.16), channel_id=1, source_target_pairs={{0,2},{1,3},{2,0},{3,1},{4,6},{5,7},{6,4},{7,5},{8,10},{9,11},{10,... | collective-permute-start | bytes 49160 | tf_op jit(solution)/shard_map/collect/ppermute | solution.py:336
  60.4 12.7 %collective-permute-start.14 = (f32[4,8,128]{2,1,0:T(8,128)S(1)}, f32[4,8,128]{2,1,0:T(8,128)S(1)}, u32[]{:S(2)}, u32[]{:S(2)}) collective-permute-start(f32[4,8,128]{2,1,0:T(8,128)S(1)} %get-tuple-element.15), channel_id=1, source_target_pairs={{0,3},{1,2},{2,1},{3,0},{4,7},{5,6},{6,5},{7,4},{8,11},{9,10},{10,... | collective-permute-start | bytes 49160 | tf_op jit(solution)/shard_map/collect/ppermute | solution.py:336
  60.8 21.7 %all-to-all-start = ((f32[16,8,128]{2,1,0:T(8,128)}), f32[16,8,128]{2,1,0:T(8,128)S(1)}, u32[]{:S(2)}, u32[]{:S(2)}) async-start(f32[16,8,128]{2,1,0:T(8,128)} %get-tuple-element.11), calls=%async_computation | async-start | bytes 131072 | tf_op jit(solution)/shard_map/collect/all_to_all | solution.py:332
  73.8 3.9 %collective-permute-start.15 = (f32[8,128]{1,0:T(8,128)S(1)}, f32[8,128]{1,0:T(8,128)S(1)}, u32[]{:S(2)}, u32[]{:S(2)}) collective-permute-start(f32[8,128]{1,0:T(8,128)S(1)} %get-tuple-element.35), channel_id=1, source_target_pairs={{0,4},{1,5},{2,6},{3,7},{4,0},{5,1},{6,2},{7,3},{8,12},{9,13},{10,... | collective-permute-start | bytes 12296 | tf_op jit(solution)/shard_map/collect/ppermute | solution.py:337
  73.8 4.3 %collective-permute-start.16 = (f32[8,128]{1,0:T(8,128)S(1)}, f32[8,128]{1,0:T(8,128)S(1)}, u32[]{:S(2)}, u32[]{:S(2)}) collective-permute-start(f32[8,128]{1,0:T(8,128)S(1)} %get-tuple-element.34), channel_id=1, source_target_pairs={{0,8},{1,9},{2,10},{3,11},{4,12},{5,13},{6,14},{7,15},{8,0},{9,1},... | collective-permute-start | bytes 12296 | tf_op jit(solution)/shard_map/collect/ppermute | solution.py:337
  75.7 4.0 %collective-permute-start.17 = (f32[8,128]{1,0:T(8,128)S(1)}, f32[8,128]{1,0:T(8,128)S(1)}, u32[]{:S(2)}, u32[]{:S(2)}) collective-permute-start(f32[8,128]{1,0:T(8,128)S(1)} %get-tuple-element.33), channel_id=1, source_target_pairs={{0,12},{1,13},{2,14},{3,15},{4,8},{5,9},{6,10},{7,11},{8,4},{9,5},... | collective-permute-start | bytes 12296 | tf_op jit(solution)/shard_map/collect/ppermute | solution.py:337
  77.7 4.8 %copy-start.5 = (f32[8,128]{1,0:T(8,128)}, f32[8,128]{1,0:T(8,128)S(1)}, u32[]{:S(2)}) copy-start(f32[8,128]{1,0:T(8,128)S(1)} %collective-permute-done.15.one_ref) | copy-start | bytes 12292
  78.1 4.4 %copy-start.6 = (f32[8,128]{1,0:T(8,128)}, f32[8,128]{1,0:T(8,128)S(1)}, u32[]{:S(2)}) copy-start(f32[8,128]{1,0:T(8,128)S(1)} %collective-permute-done.16.two_ref) | copy-start | bytes 12292
  79.6 2.9 %copy-start.7 = (f32[8,128]{1,0:T(8,128)}, f32[8,128]{1,0:T(8,128)S(1)}, u32[]{:S(2)}) copy-start(f32[8,128]{1,0:T(8,128)S(1)} %collective-permute-done.17.three_ref) | copy-start | bytes 12292
  82.5 0.6 copy-start.3

commit v7 on v6

--- a/solution.py
+++ b/solution.py
@@ -11,8 +11,8 @@
 CPD = 2
 HID = 64
 NRBF = 32
-PAY = 80
-LIVE = HID + 9
+PAY = 72
+LIVE = HID + 6
 GROUPS = 4
 SOFT = 0.01
 RANGE = 6.0
@@ -30,7 +30,6 @@
     high = pos.astype(BF16).astype(F32)
     rest = pos - high
     mid = rest.astype(BF16).astype(F32)
-    low = (rest - mid).astype(BF16).astype(F32)
     lane = lax.broadcasted_iota(jnp.int32, (1, CL), 1)
     for weight_ref, out_ref in ((wl_ref, left_ref), (wr_ref, right_ref)):
         proj = jnp.dot(weight_ref[...], feat, preferred_element_type=F32)
@@ -38,7 +37,7 @@
             cut = slice(k * CL, (k + 1) * CL)
             live = (lane < fill_ref[k]).astype(F32)
             extra = jnp.concatenate(
-                [high[:, cut], mid[:, cut], low[:, cut], live, jnp.zeros((6, CL), F32)], 0
+                [high[:, cut], mid[:, cut], live, jnp.zeros((1, CL), F32)], 0
             )
             both = jnp.concatenate([proj[:, cut], extra], 0).astype(BF16)
             for peer in range(out_ref.shape[0]):
@@ -47,8 +46,8 @@
 
 def unpack(block):
     extra = block[HID:]
-    pos = extra[0:3] + extra[3:6] + extra[6:9]
-    return block[:HID], pos, extra[9:10]
+    pos = extra[0:3] + extra[3:6]
+    return block[:HID], pos, extra[6:7]
 
 
 def spread4(value):

time: 85.1 us -> 84.4 us (level)
  Pallas kernels: 25.9 us -> 25 us
    ppermute x3, starting transfers between devices: 6.54 us -> 7.53 us  [body(): near = near + lax.ppermute(firsts[k], 'col', across(cols, k))]
    pallas_call x1, Pallas kernels: 22.8 us -> 21.9 us  [tile_call(): pl.pallas_call(tile_kernel, name='tiles', out_shape=(jax.ShapeDtypeStruct...]
  transfers between devices with their start and end apart: 19 -> 19, of which waited for: 8 -> 7; matrix products, arithmetic and copies ran while one was open for 2% -> 2% of each run, Pallas kernels for 0% -> 0%
where the time goes in v7:
time: 84.4 us; the launch traced here: 83.5 us
  starting transfers between devices  43.3 us (51%)
  Pallas kernels  25 us (30%)
  waiting for transfers between devices  10.5 us (12%)
  local copies, waits for them, and re-layouts  3.08 us (4%)
  between operations  1.5 us (2%)
    pallas_call x1, Pallas kernels, tile_call(): pl.pallas_call(tile_kernel, name='tiles', out_shape=(jax.ShapeDtypeStruct...  21.9 us
    all_to_all x1, starting transfers between devices, body(): seconds = lax.all_to_all(seconds, 'row', 0, 0)  12.1 us
    ppermute x6, starting transfers between devices, body(): lax.ppermute(own, axis, across(16, k))  11.9 us
    ppermute x6, starting transfers between devices, body(): lax.ppermute(own, axis, across(16, 4 * k))  7.95 us
    ppermute x3, starting transfers between devices, body(): near = near + lax.ppermute(firsts[k], 'col', across(cols, k))  7.53 us
    ppermute x6, waiting for transfers between devices, body(): lax.ppermute(own, axis, across(16, 4 * k))  5.54 us
    ppermute x3, starting transfers between devices, body(): lax.ppermute(near[k], 'col', across(cols, 4 * k))  3.86 us
    all_to_all x1, waiting for transfers between devices, body(): seconds = lax.all_to_all(seconds, 'row', 0, 0)  2.65 us
  transfers between devices with their start and end apart: 19, of which 7 were waited for; matrix products, arithmetic and copies ran while one was open for 2% of the time, Pallas kernels for 0%

profile of v7, /device:TPU:1, one launch (start us, length us, event | category | flops | bytes accessed | tf_op | source)
XLA Modules:
  0.0 83.5 jit_solution(13530833096329520158)
XLA Ops:
  0.6 1.6 %pack.1 = (bf16[1,2,72,128]{3,2,1,0:T(8,128)(2,1)}, bf16[1,2,72,128]{3,2,1,0:T(8,128)(2,1)}) custom-call(s32[2]{0:T(128)} %fill_ref.1, f32[3,256]{1,0:T(4,128)} %pos_ref.1, bf16[128,256]{1,0:T(8,128)(2,1)} %feat_ref.1, bf16[64,128]{1,0:T(8,128)(2,1)} %bitcast.25, bf16[64,128]{1,0:T(8,128)(2,1)} %bitcast.26), custom_call_target="tpu_custom_call" | custom-call | tf_op jit(solution)/shard_map/pack/pallas_call | solution.py:304
  2.2 3.8 %collective-permute-start.6 = (bf16[1,2,72,128]{3,2,1,0:T(8,128)(2,1)}, bf16[1,2,72,128]{3,2,1,0:T(8,128)(2,1)S(1)}, u32[]{:S(2)}, u32[]{:S(2)}) collective-permute-start(bf16[1,2,72,128]{3,2,1,0:T(8,128)(2,1)} %get-tuple-element.9), channel_id=1, source_target_pairs={{0,16},{16,0},{32,48},{48,32},{64,80},{80,64},{96,112},{112,96},{1... | collective-permute-start | bytes 110600 | tf_op jit(solution)/shard_map/spread/ppermute | solution.py:315
  6.1 5.1 %collective-permute-start.7 = (bf16[1,2,72,128]{3,2,1,0:T(8,128)(2,1)}, bf16[1,2,72,128]{3,2,1,0:T(8,128)(2,1)S(1)}, u32[]{:S(2)}, u32[]{:S(2)}) collective-permute-start(bf16[1,2,72,128]{3,2,1,0:T(8,128)(2,1)} %get-tuple-element.9), channel_id=1, source_target_pairs={{0,32},{16,48},{32,0},{48,16},{64,96},{80,112},{96,64},{112,80},{1... | collective-permute-start | bytes 110600 | tf_op jit(solution)/shard_map/spread/ppermute | solution.py:315
  11.2 1.2 %collective-permute-start = (bf16[1,2,72,128]{3,2,1,0:T(8,128)(2,1)}, bf16[1,2,72,128]{3,2,1,0:T(8,128)(2,1)S(1)}, u32[]{:S(2)}, u32[]{:S(2)}) collective-permute-start(bf16[1,2,72,128]{3,2,1,0:T(8,128)(2,1)} %get-tuple-element.8), channel_id=1, source_target_pairs={{0,1},{1,0},{2,3},{3,2},{4,5},{5,4},{6,7},{7,6},{8,9},{9,8},{10,11... | collective-permute-start | bytes 110600 | tf_op jit(solution)/shard_map/spread/ppermute | solution.py:315
  12.4 0.7 collective-permute-start.1
  13.2 0.8 constant_dynamic-update-slice_fusion.3
  14.0 0.1 pad_add_fusion.base_ref
  14.1 0.1 copy.12.wo_ref
  14.9 1.0 %collective-permute-start.2 = (bf16[1,2,72,128]{3,2,1,0:T(8,128)(2,1)S(1)}, bf16[1,2,72,128]{3,2,1,0:T(8,128)(2,1)S(1)}, u32[]{:S(2)}, u32[]{:S(2)}) collective-permute-start(bf16[1,2,72,128]{3,2,1,0:T(8,128)(2,1)S(1)} %copy-done.4), channel_id=1, source_target_pairs={{0,3},{1,2},{2,1},{3,0},{4,7},{5,6},{6,5},{7,4},{8,11},{9,10},{10,... | collective-permute-start | bytes 110600 | tf_op jit(solution)/shard_map/spread/ppermute | solution.py:315
  15.9 0.4 collective-permute-done.8
  16.3 1.3 %collective-permute-start.9 = (bf16[4,2,72,128]{3,2,1,0:T(8,128)(2,1)S(1)}, bf16[4,2,72,128]{3,2,1,0:T(8,128)(2,1)S(1)}, u32[]{:S(2)}, u32[]{:S(2)}) collective-permute-start(bf16[4,2,72,128]{3,2,1,0:T(8,128)(2,1)S(1)} %get-tuple-element.17), channel_id=1, source_target_pairs={{0,64},{16,80},{32,96},{48,112},{64,0},{80,16},{96,32},{112,48},{1... | collective-permute-start | bytes 442376 | tf_op jit(solution)/shard_map/spread/ppermute | solution.py:319
  17.6 2.4 %collective-permute-start.10 = (bf16[4,2,72,128]{3,2,1,0:T(8,128)(2,1)S(1)}, bf16[4,2,72,128]{3,2,1,0:T(8,128)(2,1)S(1)}, u32[]{:S(2)}, u32[]{:S(2)}) collective-permute-start(bf16[4,2,72,128]{3,2,1,0:T(8,128)(2,1)S(1)} %get-tuple-element.17), channel_id=1, source_target_pairs={{0,128},{16,144},{32,160},{48,176},{64,192},{80,208},{96,224},{112... | collective-permute-start | bytes 442376 | tf_op jit(solution)/shard_map/spread/ppermute | solution.py:319
  20.1 0.2 collective-permute-start.11
  20.4 1.4 %collective-permute-start.3 = (bf16[4,2,72,128]{3,2,1,0:T(8,128)(2,1)S(1)}, bf16[4,2,72,128]{3,2,1,0:T(8,128)(2,1)S(1)}, u32[]{:S(2)}, u32[]{:S(2)}) collective-permute-start(bf16[4,2,72,128]{3,2,1,0:T(8,128)(2,1)S(1)} %get-tuple-element.25), channel_id=1, source_target_pairs={{0,4},{1,5},{2,6},{3,7},{4,0},{5,1},{6,2},{7,3},{8,12},{9,13},{10,... | collective-permute-start | bytes 442376 | tf_op jit(solution)/shard_map/spread/ppermute | solution.py:319
  21.8 2.6 %collective-permute-start.4 = (bf16[4,2,72,128]{3,2,1,0:T(8,128)(2,1)S(1)}, bf16[4,2,72,128]{3,2,1,0:T(8,128)(2,1)S(1)}, u32[]{:S(2)}, u32[]{:S(2)}) collective-permute-start(bf16[4,2,72,128]{3,2,1,0:T(8,128)(2,1)S(1)} %get-tuple-element.25), channel_id=1, source_target_pairs={{0,8},{1,9},{2,10},{3,11},{4,12},{5,13},{6,14},{7,15},{8,0},{9,1},... | collective-permute-start | bytes 442376 | tf_op jit(solution)/shard_map/spread/ppermute | solution.py:319
  24.5 1.3 %collective-permute-done.11 = bf16[4,2,72,128]{3,2,1,0:T(8,128)(2,1)S(1)} collective-permute-done((bf16[4,2,72,128]{3,2,1,0:T(8,128)(2,1)S(1)}, bf16[4,2,72,128]{3,2,1,0:T(8,128)(2,1)S(1)}, u32[]{:S(2)}, u32[]{:S(2)}) %collective-permute-start.11) | collective-permute-done | bytes 147488 | tf_op jit(solution)/shard_map/spread/ppermute | solution.py:319
  25.8 2.7 %collective-permute-done.4 = bf16[4,2,72,128]{3,2,1,0:T(8,128)(2,1)S(1)} collective-permute-done((bf16[4,2,72,128]{3,2,1,0:T(8,128)(2,1)S(1)}, bf16[4,2,72,128]{3,2,1,0:T(8,128)(2,1)S(1)}, u32[]{:S(2)}, u32[]{:S(2)}) %collective-permute-start.4) | collective-permute-done | bytes 147488 | tf_op jit(solution)/shard_map/spread/ppermute | solution.py:319
  28.6 1.5 %collective-permute-done.5 = bf16[4,2,72,128]{3,2,1,0:T(8,128)(2,1)S(1)} collective-permute-done((bf16[4,2,72,128]{3,2,1,0:T(8,128)(2,1)S(1)}, bf16[4,2,72,128]{3,2,1,0:T(8,128)(2,1)S(1)}, u32[]{:S(2)}, u32[]{:S(2)}) %collective-permute-start.5) | collective-permute-done | bytes 147488 | tf_op jit(solution)/shard_map/spread/ppermute | solution.py:319
  30.1 0.7 copy-done
  30.8 21.9 %tiles.1 = (f32[16,8,128]{2,1,0:T(8,128)S(1)}, f32[16,8,128]{2,1,0:T(8,128)}) custom-call(s32[2,8]{1,0:T(2,128)S(1)} %bitcast.24, s32[1]{0:T(128)S(6)} %copy.31.count_ref, s32[4]{0:T(128)S(1)} %pad_add_fusion.base_ref, bf16[32,72,128]{2,1,0:T(8,128)(2,1)S(1)} %bitcast.21, bf16[32,72,128]{2,1,0:T(8,128)(2,1)S(1)} %bitcast.22, f32[32,64]{1,0:T(8,128)S(1)} %bitcast.23, ...), custom_call_target="tpu_custom_call" | custom-call | tf_op jit(solution)/shard_map/tiles/tiles/pallas_call | solution.py:247
  52.7 7.5 %collective-permute-start.13 = (f32[4,8,128]{2,1,0:T(8,128)S(1)}, f32[4,8,128]{2,1,0:T(8,128)S(1)}, u32[]{:S(2)}, u32[]{:S(2)}) collective-permute-start(f32[4,8,128]{2,1,0:T(8,128)S(1)} %get-tuple-element.16), channel_id=1, source_target_pairs={{0,2},{1,3},{2,0},{3,1},{4,6},{5,7},{6,4},{7,5},{8,10},{9,11},{10,... | collective-permute-start | bytes 49160 | tf_op jit(solution)/shard_map/collect/ppermute | solution.py:335
  60.2 0.1 collective-permute-start.14
  60.3 12.1 %all-to-all-start = ((f32[16,8,128]{2,1,0:T(8,128)}), f32[16,8,128]{2,1,0:T(8,128)S(1)}, u32[]{:S(2)}, u32[]{:S(2)}) async-start(f32[16,8,128]{2,1,0:T(8,128)} %get-tuple-element.11), calls=%async_computation | async-start | bytes 131072 | tf_op jit(solution)/shard_map/collect/all_to_all | solution.py:331
  72.4 0.6 slice_bitcast_fusion
  73.0 0.8 collective-permute-start.15
  73.8 1.0 %collective-permute-start.16 = (f32[8,128]{1,0:T(8,128)S(1)}, f32[8,128]{1,0:T(8,128)S(1)}, u32[]{:S(2)}, u32[]{:S(2)}) collective-permute-start(f32[8,128]{1,0:T(8,128)S(1)} %get-tuple-element.34), channel_id=1, source_target_pairs={{0,8},{1,9},{2,10},{3,11},{4,12},{5,13},{6,14},{7,15},{8,0},{9,1},... | collective-permute-start | bytes 12296 | tf_op jit(solution)/shard_map/collect/ppermute | solution.py:336
  74.8 2.1 %collective-permute-start.17 = (f32[8,128]{1,0:T(8,128)S(1)}, f32[8,128]{1,0:T(8,128)S(1)}, u32[]{:S(2)}, u32[]{:S(2)}) collective-permute-start(f32[8,128]{1,0:T(8,128)S(1)} %get-tuple-element.33), channel_id=1, source_target_pairs={{0,12},{1,13},{2,14},{3,15},{4,8},{5,9},{6,10},{7,11},{8,4},{9,5},... | collective-permute-start | bytes 12296 | tf_op jit(solution)/shard_map/collect/ppermute | solution.py:336
  76.9 0.9 %collective-permute-done.16.two_ref = f32[8,128]{1,0:T(8,128)S(1)} collective-permute-done((f32[8,128]{1,0:T(8,128)S(1)}, f32[8,128]{1,0:T(8,128)S(1)}, u32[]{:S(2)}, u32[]{:S(2)}) %collective-permute-start.16) | collective-permute-done | bytes 4128 | tf_op jit(solution)/shard_map/collect/ppermute | solution.py:336
  77.8 1.0 %collective-permute-done.17.three_ref = f32[8,128]{1,0:T(8,128)S(1)} collective-permute-done((f32[8,128]{1,0:T(8,128)S(1)}, f32[8,128]{1,0:T(8,128)S(1)}, u32[]{:S(2)}, u32[]{:S(2)}) %collective-permute-start.17) | collective-permute-done | bytes 4128 | tf_op jit(solution)/shard_map/collect/ppermute | solution.py:336
  78.8 2.6 %all-to-all-done.second_ref = f32[16,8,128]{2,1,0:T(8,128)S(1)} async-done(((f32[16,8,128]{2,1,0:T(8,128)}), f32[16,8,128]{2,1,0:T(8,128)S(1)}, u32[]{:S(2)}, u32[]{:S(2)}) %all-to-all-start) | async-done | bytes 65568 | tf_op jit(solution)/shard_map/collect/all_to_all | solution.py:331
  81.4 0.6 copy-done.3
  82.0 1.5 %add.22 = (f32[3,256]{1,0:T(4,128)}, f32[1,256]{1,0:T(1,128)}) custom-call(f32[8,128]{1,0:T(8,128)} %get-tuple-element.36.own_ref, f32[8,128]{1,0:T(8,128)} %copy-done.5, f32[8,128]{1,0:T(8,128)} %copy-done.6, f32[8,128]{1,0:T(8,128)} %copy-done.7, f32[16,8,128]{2,1,0:T(8,128)} %copy-done.3), custom_call_target="tpu_custom_call" | custom-call | tf_op jit(solution)/shard_map/add/pallas_call | solution.py:338
  (46 shorter events, 0.4 us)
Async XLA Ops:
  2.2 12.6 %collective-permute-start.6 = (bf16[1,2,72,128]{3,2,1,0:T(8,128)(2,1)}, bf16[1,2,72,128]{3,2,1,0:T(8,128)(2,1)S(1)}, u32[]{:S(2)}, u32[]{:S(2)}) collective-permute-start(bf16[1,2,72,128]{3,2,1,0:T(8,128)(2,1)} %get-tuple-element.9), channel_id=1, source_target_pairs={{0,16},{16,0},{32,48},{48,32},{64,80},{80,64},{96,112},{112,96},{1... | collective-permute-start | bytes 110600 | tf_op jit(solution)/shard_map/spread/ppermute | solution.py:315
  6.1 9.8 %collective-permute-start.7 = (bf16[1,2,72,128]{3,2,1,0:T(8,128)(2,1)}, bf16[1,2,72,128]{3,2,1,0:T(8,128)(2,1)S(1)}, u32[]{:S(2)}, u32[]{:S(2)}) collective-permute-start(bf16[1,2,72,128]{3,2,1,0:T(8,128)(2,1)} %get-tuple-element.9), channel_id=1, source_target_pairs={{0,32},{16,48},{32,0},{48,16},{64,96},{80,112},{96,64},{112,80},{1... | collective-permute-start | bytes 110600 | tf_op jit(solution)/shard_map/spread/ppermute | solution.py:315
  11.2 5.1 %collective-permute-start.8 = (bf16[1,2,72,128]{3,2,1,0:T(8,128)(2,1)}, bf16[1,2,72,128]{3,2,1,0:T(8,128)(2,1)S(1)}, u32[]{:S(2)}, u32[]{:S(2)}) collective-permute-start(bf16[1,2,72,128]{3,2,1,0:T(8,128)(2,1)} %get-tuple-element.9), channel_id=1, source_target_pairs={{0,48},{16,32},{32,16},{48,0},{64,112},{80,96},{96,80},{112,64},{1... | collective-permute-start | bytes 110600 | tf_op jit(solution)/shard_map/spread/ppermute | solution.py:315
  11.2 8.9 %collective-permute-start = (bf16[1,2,72,128]{3,2,1,0:T(8,128)(2,1)}, bf16[1,2,72,128]{3,2,1,0:T(8,128)(2,1)S(1)}, u32[]{:S(2)}, u32[]{:S(2)}) collective-permute-start(bf16[1,2,72,128]{3,2,1,0:T(8,128)(2,1)} %get-tuple-element.8), channel_id=1, source_target_pairs={{0,1},{1,0},{2,3},{3,2},{4,5},{5,4},{6,7},{7,6},{8,9},{9,8},{10,11... | collective-permute-start | bytes 110600 | tf_op jit(solution)/shard_map/spread/ppermute | solution.py:315
  12.4 7.9 %collective-permute-start.1 = (bf16[1,2,72,128]{3,2,1,0:T(8,128)(2,1)}, bf16[1,2,72,128]{3,2,1,0:T(8,128)(2,1)S(1)}, u32[]{:S(2)}, u32[]{:S(2)}) collective-permute-start(bf16[1,2,72,128]{3,2,1,0:T(8,128)(2,1)} %get-tuple-element.8), channel_id=1, source_target_pairs={{0,2},{1,3},{2,0},{3,1},{4,6},{5,7},{6,4},{7,5},{8,10},{9,11},{10,... | collective-permute-start | bytes 110600 | tf_op jit(solution)/shard_map/spread/ppermute | solution.py:315
  13.2 0.8 %copy-start.8 = (bf16[64]{0:T(256)(128)(2,1)S(1)}, bf16[64]{0:T(256)(128)(2,1)}, u32[]{:S(2)}) copy-start(bf16[64]{0:T(256)(128)(2,1)} %param.19) | copy-start | bytes 388
  14.0 0.9 %copy-start.4 = (bf16[1,2,72,128]{3,2,1,0:T(8,128)(2,1)S(1)}, bf16[1,2,72,128]{3,2,1,0:T(8,128)(2,1)}, u32[]{:S(2)}) copy-start(bf16[1,2,72,128]{3,2,1,0:T(8,128)(2,1)} %get-tuple-element.8) | copy-start | bytes 110596
  14.9 5.5 %collective-permute-start.2 = (bf16[1,2,72,128]{3,2,1,0:T(8,128)(2,1)S(1)}, bf16[1,2,72,128]{3,2,1,0:T(8,128)(2,1)S(1)}, u32[]{:S(2)}, u32[]{:S(2)}) collective-permute-start(bf16[1,2,72,128]{3,2,1,0:T(8,128)(2,1)S(1)} %copy-done.4), channel_id=1, source_target_pairs={{0,3},{1,2},{2,1},{3,0},{4,7},{5,6},{6,5},{7,4},{8,11},{9,10},{10,... | collective-permute-start | bytes 110600 | tf_op jit(solution)/shard_map/spread/ppermute | solution.py:315
  16.3 8.0 %collective-permute-start.9 = (bf16[4,2,72,128]{3,2,1,0:T(8,128)(2,1)S(1)}, bf16[4,2,72,128]{3,2,1,0:T(8,128)(2,1)S(1)}, u32[]{:S(2)}, u32[]{:S(2)}) collective-permute-start(bf16[4,2,72,128]{3,2,1,0:T(8,128)(2,1)S(1)} %get-tuple-element.17), channel_id=1, source_target_pairs={{0,64},{16,80},{32,96},{48,112},{64,0},{80,16},{96,32},{112,48},{1... | collective-permute-start | bytes 442376 | tf_op jit(solution)/shard_map/spread/ppermute | solution.py:319
  17.6 6.8 %collective-permute-start.10 = (bf16[4,2,72,128]{3,2,1,0:T(8,128)(2,1)S(1)}, bf16[4,2,72,128]{3,2,1,0:T(8,128)(2,1)S(1)}, u32[]{:S(2)}, u32[]{:S(2)}) collective-permute-start(bf16[4,2,72,128]{3,2,1,0:T(8,128)(2,1)S(1)} %get-tuple-element.17), channel_id=1, source_target_pairs={{0,128},{16,144},{32,160},{48,176},{64,192},{80,208},{96,224},{112... | collective-permute-start | bytes 442376 | tf_op jit(solution)/shard_map/spread/ppermute | solution.py:319
  20.1 5.7 %collective-permute-start.11 = (bf16[4,2,72,128]{3,2,1,0:T(8,128)(2,1)S(1)}, bf16[4,2,72,128]{3,2,1,0:T(8,128)(2,1)S(1)}, u32[]{:S(2)}, u32[]{:S(2)}) collective-permute-start(bf16[4,2,72,128]{3,2,1,0:T(8,128)(2,1)S(1)} %get-tuple-element.17), channel_id=1, source_target_pairs={{0,192},{16,208},{32,224},{48,240},{64,128},{80,144},{96,160},{112... | collective-permute-start | bytes 442376 | tf_op jit(solution)/shard_map/spread/ppermute | solution.py:319
  20.4 5.4 %collective-permute-start.3 = (bf16[4,2,72,128]{3,2,1,0:T(8,128)(2,1)S(1)}, bf16[4,2,72,128]{3,2,1,0:T(8,128)(2,1)S(1)}, u32[]{:S(2)}, u32[]{:S(2)}) collective-permute-start(bf16[4,2,72,128]{3,2,1,0:T(8,128)(2,1)S(1)} %get-tuple-element.25), channel_id=1, source_target_pairs={{0,4},{1,5},{2,6},{3,7},{4,0},{5,1},{6,2},{7,3},{8,12},{9,13},{10,... | collective-permute-start | bytes 442376 | tf_op jit(solution)/shard_map/spread/ppermute | solution.py:319
  21.8 6.8 %collective-permute-start.4 = (bf16[4,2,72,128]{3,2,1,0:T(8,128)(2,1)S(1)}, bf16[4,2,72,128]{3,2,1,0:T(8,128)(2,1)S(1)}, u32[]{:S(2)}, u32[]{:S(2)}) collective-permute-start(bf16[4,2,72,128]{3,2,1,0:T(8,128)(2,1)S(1)} %get-tuple-element.25), channel_id=1, source_target_pairs={{0,8},{1,9},{2,10},{3,11},{4,12},{5,13},{6,14},{7,15},{8,0},{9,1},... | collective-permute-start | bytes 442376 | tf_op jit(solution)/shard_map/spread/ppermute | solution.py:319
  24.4 5.7 %collective-permute-start.5 = (bf16[4,2,72,128]{3,2,1,0:T(8,128)(2,1)S(1)}, bf16[4,2,72,128]{3,2,1,0:T(8,128)(2,1)S(1)}, u32[]{:S(2)}, u32[]{:S(2)}) collective-permute-start(bf16[4,2,72,128]{3,2,1,0:T(8,128)(2,1)S(1)} %get-tuple-element.25), channel_id=1, source_target_pairs={{0,12},{1,13},{2,14},{3,15},{4,8},{5,9},{6,10},{7,11},{8,4},{9,5},... | collective-permute-start | bytes 442376 | tf_op jit(solution)/shard_map/spread/ppermute | solution.py:319
  30.1 0.7 copy-start
  30.1 0.7 copy-start.1
  30.1 0.7 copy-start.2
  52.7 19.6 %collective-permute-start.12 = (f32[4,8,128]{2,1,0:T(8,128)S(1)}, f32[4,8,128]{2,1,0:T(8,128)S(1)}, u32[]{:S(2)}, u32[]{:S(2)}) collective-permute-start(f32[4,8,128]{2,1,0:T(8,128)S(1)} %get-tuple-element.14), channel_id=1, source_target_pairs={{0,1},{1,0},{2,3},{3,2},{4,5},{5,4},{6,7},{7,6},{8,9},{9,8},{10,11... | collective-permute-start | bytes 49160 | tf_op jit(solution)/shard_map/collect/ppermute | solution.py:335
  52.7 19.6 %collective-permute-start.13 = (f32[4,8,128]{2,1,0:T(8,128)S(1)}, f32[4,8,128]{2,1,0:T(8,128)S(1)}, u32[]{:S(2)}, u32[]{:S(2)}) collective-permute-start(f32[4,8,128]{2,1,0:T(8,128)S(1)} %get-tuple-element.16), channel_id=1, source_target_pairs={{0,2},{1,3},{2,0},{3,1},{4,6},{5,7},{6,4},{7,5},{8,10},{9,11},{10,... | collective-permute-start | bytes 49160 | tf_op jit(solution)/shard_map/collect/ppermute | solution.py:335
  60.2 12.2 %collective-permute-start.14 = (f32[4,8,128]{2,1,0:T(8,128)S(1)}, f32[4,8,128]{2,1,0:T(8,128)S(1)}, u32[]{:S(2)}, u32[]{:S(2)}) collective-permute-start(f32[4,8,128]{2,1,0:T(8,128)S(1)} %get-tuple-element.15), channel_id=1, source_target_pairs={{0,3},{1,2},{2,1},{3,0},{4,7},{5,6},{6,5},{7,4},{8,11},{9,10},{10,... | collective-permute-start | bytes 49160 | tf_op jit(solution)/shard_map/collect/ppermute | solution.py:335
  60.3 21.1 %all-to-all-start = ((f32[16,8,128]{2,1,0:T(8,128)}), f32[16,8,128]{2,1,0:T(8,128)S(1)}, u32[]{:S(2)}, u32[]{:S(2)}) async-start(f32[16,8,128]{2,1,0:T(8,128)} %get-tuple-element.11), calls=%async_computation | async-start | bytes 131072 | tf_op jit(solution)/shard_map/collect/all_to_all | solution.py:331
  73.0 3.9 %collective-permute-start.15 = (f32[8,128]{1,0:T(8,128)S(1)}, f32[8,128]{1,0:T(8,128)S(1)}, u32[]{:S(2)}, u32[]{:S(2)}) collective-permute-start(f32[8,128]{1,0:T(8,128)S(1)} %get-tuple-element.35), channel_id=1, source_target_pairs={{0,4},{1,5},{2,6},{3,7},{4,0},{5,1},{6,2},{7,3},{8,12},{9,13},{10,... | collective-permute-start | bytes 12296 | tf_op jit(solution)/shard_map/collect/ppermute | solution.py:336
  73.8 4.0 %collective-permute-start.16 = (f32[8,128]{1,0:T(8,128)S(1)}, f32[8,128]{1,0:T(8,128)S(1)}, u32[]{:S(2)}, u32[]{:S(2)}) collective-permute-start(f32[8,128]{1,0:T(8,128)S(1)} %get-tuple-element.34), channel_id=1, source_target_pairs={{0,8},{1,9},{2,10},{3,11},{4,12},{5,13},{6,14},{7,15},{8,0},{9,1},... | collective-permute-start | bytes 12296 | tf_op jit(solution)/shard_map/collect/ppermute | solution.py:336
  74.8 4.0 %collective-permute-start.17 = (f32[8,128]{1,0:T(8,128)S(1)}, f32[8,128]{1,0:T(8,128)S(1)}, u32[]{:S(2)}, u32[]{:S(2)}) collective-permute-start(f32[8,128]{1,0:T(8,128)S(1)} %get-tuple-element.33), channel_id=1, source_target_pairs={{0,12},{1,13},{2,14},{3,15},{4,8},{5,9},{6,10},{7,11},{8,4},{9,5},... | collective-permute-start | bytes 12296 | tf_op jit(solution)/shard_map/collect/ppermute | solution.py:336
  76.9 4.5 %copy-start.5 = (f32[8,128]{1,0:T(8,128)}, f32[8,128]{1,0:T(8,128)S(1)}, u32[]{:S(2)}) copy-start(f32[8,128]{1,0:T(8,128)S(1)} %collective-permute-done.15.one_ref) | copy-start | bytes 12292
  77.8 3.6 %copy-start.6 = (f32[8,128]{1,0:T(8,128)}, f32[8,128]{1,0:T(8,128)S(1)}, u32[]{:S(2)}) copy-start(f32[8,128]{1,0:T(8,128)S(1)} %collective-permute-done.16.two_ref) | copy-start | bytes 12292
  78.8 2.7 %copy-start.7 = (f32[8,128]{1,0:T(8,128)}, f32[8,128]{1,0:T(8,128)S(1)}, u32[]{:S(2)}) copy-start(f32[8,128]{1,0:T(8,128)S(1)} %collective-permute-done.17.three_ref) | copy-start | bytes 12292
  81.4 0.6 copy-start.3
